TPU v7x, 32 devices: a whole 2x2x4 slice. The times are simulated.
32 devices in a mesh: dp: 16 (over z, y, core), mp: 2 (over x).
Axes of the slice: x: 2, y: 2, z: 4, core: 2. Of those that a mesh axis runs over, the one named last changes fastest.
Arguments:
- layer_in: bfloat16 [16, 256, 2048], P('dp'), may hold values from -36 to 36
- seg_ids: int32 [16, 256], P('dp'), may hold values from 0 to 3, never falling along the last dimension, each value on 1 to 192 neighbouring positions
- w_q: bfloat16 [2048, 2048], P('dp', 'mp'), may hold values from -0.125 to 0.125
- w_k: bfloat16 [2048, 1024], P('dp', 'mp'), may hold values from -0.125 to 0.125
- w_v: bfloat16 [2048, 1024], P('dp', 'mp'), may hold values from -0.125 to 0.125
- w_o: bfloat16 [2048, 2048], P('dp', 'mp'), may hold values from -1 to 1
- w_gate: bfloat16 [2048, 6144], P('dp', 'mp'), may hold values from -0.125 to 0.125
- w_up: bfloat16 [2048, 6144], P('dp', 'mp'), may hold values from -0.125 to 0.125
- w_down: bfloat16 [2048, 6144], P('dp', 'mp'), may hold values from -0.078125 to 0.078125
- attn_gain: float32 [2048], replicated, may hold values from 0.25 to 1.75
- mlp_gain: float32 [2048], replicated, may hold values from 0.25 to 1.75
- q_gain: float32 [128], replicated, may hold values from 0.5 to 1.5
- k_gain: float32 [128], replicated, may hold values from 0.5 to 1.5
- cotangent: bfloat16 [16, 256, 2048], P('dp'), may hold values from -6 to 6
Outputs:
- layer_out: bfloat16 [16, 256, 2048], P('dp')
- in_grad: bfloat16 [16, 256, 2048], P('dp')
- grad_q: float32 [2048, 2048], P('dp', 'mp')
- grad_k: float32 [2048, 1024], P('dp', 'mp')
- grad_v: float32 [2048, 1024], P('dp', 'mp')
- grad_o: float32 [2048, 2048], P('dp', 'mp')
- grad_gate: float32 [2048, 6144], P('dp', 'mp')
- grad_up: float32 [2048, 6144], P('dp', 'mp')
- grad_down: float32 [2048, 6144], P('dp', 'mp')
- grad_attn_gain: float32 [2048], P('dp')
- grad_mlp_gain: float32 [2048], P('dp')
- grad_q_gain: float32 [128], P('dp')
- grad_k_gain: float32 [128], P('dp')
Inputs may be any that keep to these rules, and one draw needn't show every extreme that they name: `seg_ids`: along each row the document number never falls; each number 0 to 3 covers 1 to 192 positions of the row, and some covers exactly 192.
All inputs are finite; a program needn't handle non-finite values.
Results may differ from a plain program's by a relative error of at most 0.014.
Values may be sent and summed in bfloat16 or wider, within the bound.
A program may use at most 256 MiB of HBM per device.

v0:
```python
import math

import jax
import jax.numpy as jnp
from jax import lax
from jax.sharding import PartitionSpec as P

EPSILON = 1e-06
ROPE_BASE = 1000000.0
MASKED = -1e30


def matmul(left_op, right_op):
    return jnp.dot(left_op, right_op, preferred_element_type=jnp.float32)


def batched(pattern, left_op, right_op):
    return jnp.einsum(pattern, left_op, right_op, preferred_element_type=jnp.float32)


def rms_norm(values, gain_vec):
    inv_rms = lax.rsqrt(jnp.mean(values * values, axis=-1, keepdims=True) + EPSILON)
    return (values * inv_rms * gain_vec, inv_rms)


def norm_back(grad_norm, values, inv_rms, gain_vec):
    scaled = grad_norm * gain_vec
    cubed = inv_rms * inv_rms * inv_rms
    grad_values = inv_rms * scaled - values * cubed * jnp.mean(
        scaled * values, axis=-1, keepdims=True
    )
    return (grad_values, grad_norm * values * inv_rms)


def rope_tables(seg_row, head_dim):
    seq_len = seg_row.shape[0]
    row_index = jnp.arange(seq_len, dtype=jnp.int32)
    previous = jnp.concatenate([jnp.full((1,), -1, jnp.int32), seg_row[:-1]])
    starts = lax.cummax(jnp.where(seg_row != previous, row_index, jnp.int32(0)), axis=0)
    position = (row_index - starts).astype(jnp.float32)
    frequency = ROPE_BASE ** (-jnp.arange(0, head_dim, 2).astype(jnp.float32) / head_dim)
    angles = position[:, None] * frequency[None, :]
    return (jnp.cos(angles), jnp.sin(angles))


def rope_apply(values, cosine_table, sine_table):
    half_dim = values.shape[-1] // 2
    first_half = values[..., :half_dim]
    second_half = values[..., half_dim:]
    cos_wide = cosine_table[:, None, :]
    sin_wide = sine_table[:, None, :]
    return jnp.concatenate(
        [
            first_half * cos_wide - second_half * sin_wide,
            second_half * cos_wide + first_half * sin_wide,
        ],
        axis=-1,
    )


def rope_back(grads, cosine_table, sine_table):
    half_dim = grads.shape[-1] // 2
    first_half = grads[..., :half_dim]
    second_half = grads[..., half_dim:]
    cos_wide = cosine_table[:, None, :]
    sin_wide = sine_table[:, None, :]
    return jnp.concatenate(
        [
            first_half * cos_wide + second_half * sin_wide,
            second_half * cos_wide - first_half * sin_wide,
        ],
        axis=-1,
    )


def score_block(queries_half, keys_half, seg_row, group_size):
    seq_len, num_heads, head_dim = queries_half.shape
    kv_heads = keys_half.shape[1]
    grouped = queries_half.reshape(seq_len, kv_heads, group_size, head_dim)
    scores = batched("qkgd,skd->kgqs", grouped, keys_half) * (1.0 / math.sqrt(head_dim))
    row_index = jnp.arange(seq_len, dtype=jnp.int32)
    allowed = (seg_row[:, None] == seg_row[None, :]) & (row_index[None, :] <= row_index[:, None])
    return (jnp.where(allowed[None, None], scores, MASKED), grouped)


def attend(queries_half, keys_half, values_half, seg_row, group_size):
    seq_len = queries_half.shape[0]
    scores, grouped = score_block(queries_half, keys_half, seg_row, group_size)
    row_max = jnp.max(scores, axis=-1, keepdims=True)
    log_total = row_max + jnp.log(jnp.sum(jnp.exp(scores - row_max), axis=-1, keepdims=True))
    probs_half = jnp.exp(scores - log_total).astype(jnp.bfloat16)
    context = batched("kgqs,skd->qkgd", probs_half, values_half)
    return (context.reshape(seq_len, -1).astype(jnp.bfloat16), log_total)


def attend_back(
    queries_half,
    keys_half,
    values_half,
    seg_row,
    group_size,
    log_total,
    context_half,
    grad_context_half,
):
    seq_len, num_heads, head_dim = queries_half.shape
    kv_heads = keys_half.shape[1]
    scores, grouped = score_block(queries_half, keys_half, seg_row, group_size)
    probs_full = jnp.exp(scores - log_total)
    probs_half = probs_full.astype(jnp.bfloat16)
    grad_grouped = grad_context_half.reshape(seq_len, kv_heads, group_size, head_dim)
    context_grouped = context_half.reshape(seq_len, kv_heads, group_size, head_dim)
    grad_probs = batched("qkgd,skd->kgqs", grad_grouped, values_half)
    delta_sum = jnp.einsum(
        "qkgd,qkgd->kgq", grad_grouped.astype(jnp.float32), context_grouped.astype(jnp.float32)
    )[..., None]
    grad_scores = (probs_full * (grad_probs - delta_sum) * (1.0 / math.sqrt(head_dim))).astype(
        jnp.bfloat16
    )
    grad_queries = batched("kgqs,skd->qkgd", grad_scores, keys_half).reshape(
        seq_len, num_heads, head_dim
    )
    grad_keys = batched("kgqs,qkgd->skd", grad_scores, grouped)
    grad_values = batched("kgqs,qkgd->skd", probs_half, grad_grouped)
    return (grad_queries, grad_keys, grad_values)


def body(
    layer_in,
    seg_ids,
    w_q,
    w_k,
    w_v,
    w_o,
    w_gate,
    w_up,
    w_down,
    attn_gain,
    mlp_gain,
    q_gain,
    k_gain,
    cotangent,
):
    head_dim = q_gain.shape[0]
    group_size = w_q.shape[1] // w_k.shape[1]
    model_width = w_q.shape[0] * lax.axis_size("dp")
    totals = [
        jnp.zeros((model_width, shard.shape[1]), jnp.float32)
        for shard in (w_q, w_k, w_v, w_o, w_gate, w_up, w_down)
    ]
    totals = totals + [
        jnp.zeros((model_width,), jnp.float32),
        jnp.zeros((model_width,), jnp.float32),
        jnp.zeros((head_dim,), jnp.float32),
        jnp.zeros((head_dim,), jnp.float32),
    ]
    full_q = lax.all_gather(w_q, "dp", axis=0, tiled=True)
    full_k = lax.all_gather(w_k, "dp", axis=0, tiled=True)
    full_v = lax.all_gather(w_v, "dp", axis=0, tiled=True)
    full_o = lax.all_gather(w_o, "dp", axis=0, tiled=True)
    full_gate = lax.all_gather(w_gate, "dp", axis=0, tiled=True)
    full_up = lax.all_gather(w_up, "dp", axis=0, tiled=True)
    full_down = lax.all_gather(w_down, "dp", axis=0, tiled=True)
    row_in = layer_in[0]
    seg_row = seg_ids[0]
    row_cot = cotangent[0]
    seq_len = row_in.shape[0]
    residual = row_in.astype(jnp.float32)
    normed_full, scale_one = rms_norm(residual, attn_gain)
    normed_one = normed_full.astype(jnp.bfloat16)
    query_raw = matmul(normed_one, full_q).reshape(seq_len, -1, head_dim)
    key_raw = matmul(normed_one, full_k).reshape(seq_len, -1, head_dim)
    values_half = matmul(normed_one, full_v).astype(jnp.bfloat16).reshape(seq_len, -1, head_dim)
    cosine_table, sine_table = rope_tables(seg_row, head_dim)
    query_norm, scale_q = rms_norm(query_raw, q_gain)
    key_norm, scale_k = rms_norm(key_raw, k_gain)
    queries_half = rope_apply(query_norm, cosine_table, sine_table).astype(jnp.bfloat16)
    keys_half = rope_apply(key_norm, cosine_table, sine_table).astype(jnp.bfloat16)
    context_half, log_total = attend(queries_half, keys_half, values_half, seg_row, group_size)
    attn_out = lax.psum(matmul(context_half, full_o.T), "mp")
    mid = residual + attn_out
    normed_mid, scale_two = rms_norm(mid, mlp_gain)
    normed_two = normed_mid.astype(jnp.bfloat16)
    gate_pre = matmul(normed_two, full_gate)
    up_pre = matmul(normed_two, full_up)
    sigmoid_gate = jax.nn.sigmoid(gate_pre)
    silu_val = gate_pre * sigmoid_gate
    act_half = (silu_val * up_pre).astype(jnp.bfloat16)
    mlp_out = lax.psum(matmul(act_half, full_down.T), "mp")
    out_rows = [(mid + mlp_out).astype(jnp.bfloat16)]
    full_gate = lax.all_gather(w_gate, "dp", axis=0, tiled=True)
    full_up = lax.all_gather(w_up, "dp", axis=0, tiled=True)
    full_down = lax.all_gather(w_down, "dp", axis=0, tiled=True)
    grad_act = matmul(row_cot, full_down)
    grad_down = matmul(row_cot.T, act_half)
    grad_gate_pre = (
        grad_act * up_pre * sigmoid_gate * (1.0 + gate_pre * (1.0 - sigmoid_gate))
    ).astype(jnp.bfloat16)
    grad_up_pre = (grad_act * silu_val).astype(jnp.bfloat16)
    grad_gate = matmul(normed_two.T, grad_gate_pre)
    grad_up = matmul(normed_two.T, grad_up_pre)
    grad_normed_two = lax.psum(
        matmul(grad_gate_pre, full_gate.T) + matmul(grad_up_pre, full_up.T), "mp"
    )
    grad_mid_norm, gain_two_terms = norm_back(grad_normed_two, mid, scale_two, mlp_gain)
    grad_mid = row_cot.astype(jnp.float32) + grad_mid_norm
    grad_mid_half = grad_mid.astype(jnp.bfloat16)
    full_q = lax.all_gather(w_q, "dp", axis=0, tiled=True)
    full_k = lax.all_gather(w_k, "dp", axis=0, tiled=True)
    full_v = lax.all_gather(w_v, "dp", axis=0, tiled=True)
    full_o = lax.all_gather(w_o, "dp", axis=0, tiled=True)
    grad_o = matmul(grad_mid_half.T, context_half)
    grad_context_half = matmul(grad_mid_half, full_o).astype(jnp.bfloat16)
    grad_queries, grad_keys, grad_values = attend_back(
        queries_half,
        keys_half,
        values_half,
        seg_row,
        group_size,
        log_total,
        context_half,
        grad_context_half,
    )
    grad_query_raw, q_gain_terms = norm_back(
        rope_back(grad_queries, cosine_table, sine_table), query_raw, scale_q, q_gain
    )
    grad_key_raw, k_gain_terms = norm_back(
        rope_back(grad_keys, cosine_table, sine_table), key_raw, scale_k, k_gain
    )
    query_grad_half = grad_query_raw.reshape(seq_len, -1).astype(jnp.bfloat16)
    key_grad_half = grad_key_raw.reshape(seq_len, -1).astype(jnp.bfloat16)
    value_grad_half = grad_values.reshape(seq_len, -1).astype(jnp.bfloat16)
    normed_part = (
        matmul(query_grad_half, full_q.T)
        + matmul(key_grad_half, full_k.T)
        + matmul(value_grad_half, full_v.T)
    )
    grad_normed_one, q_gain_sum, k_gain_sum = lax.psum(
        (normed_part, jnp.sum(q_gain_terms, axis=(0, 1)), jnp.sum(k_gain_terms, axis=(0, 1))), "mp"
    )
    grad_res_norm, gain_one_terms = norm_back(grad_normed_one, residual, scale_one, attn_gain)
    grad_rows = [(grad_mid + grad_res_norm).astype(jnp.bfloat16)]
    new_terms = [
        matmul(normed_one.T, query_grad_half),
        matmul(normed_one.T, key_grad_half),
        matmul(normed_one.T, value_grad_half),
        grad_o,
        grad_gate,
        grad_up,
        grad_down,
        jnp.sum(gain_one_terms, axis=0),
        jnp.sum(gain_two_terms, axis=0),
        q_gain_sum,
        k_gain_sum,
    ]
    totals = [new for new in new_terms]
    reduced = (
        lax.psum_scatter(totals[0], "dp", scatter_dimension=0, tiled=True),
        lax.psum_scatter(totals[1], "dp", scatter_dimension=0, tiled=True),
        lax.psum_scatter(totals[2], "dp", scatter_dimension=0, tiled=True),
        lax.psum_scatter(totals[3], "dp", scatter_dimension=0, tiled=True),
        lax.psum_scatter(totals[4], "dp", scatter_dimension=0, tiled=True),
        lax.psum_scatter(totals[5], "dp", scatter_dimension=0, tiled=True),
        lax.psum_scatter(totals[6], "dp", scatter_dimension=0, tiled=True),
        lax.psum_scatter(totals[7], "dp", scatter_dimension=0, tiled=True),
        lax.psum_scatter(totals[8], "dp", scatter_dimension=0, tiled=True),
        lax.psum_scatter(totals[9], "dp", scatter_dimension=0, tiled=True),
        lax.psum_scatter(totals[10], "dp", scatter_dimension=0, tiled=True),
    )
    return (jnp.stack(out_rows), jnp.stack(grad_rows)) + tuple(reduced)


def solution(mesh):
    return jax.shard_map(
        body,
        mesh=mesh,
        in_specs=(
            P("dp", None, None),
            P("dp", None),
            P("dp", "mp"),
            P("dp", "mp"),
            P("dp", "mp"),
            P("dp", "mp"),
            P("dp", "mp"),
            P("dp", "mp"),
            P("dp", "mp"),
            P(),
            P(),
            P(),
            P(),
            P("dp", None, None),
        ),
        out_specs=(
            P("dp", None, None),
            P("dp", None, None),
            P("dp", "mp"),
            P("dp", "mp"),
            P("dp", "mp"),
            P("dp", "mp"),
            P("dp", "mp"),
            P("dp", "mp"),
            P("dp", "mp"),
            P("dp"),
            P("dp"),
            P("dp"),
            P("dp"),
        ),
        check_vma=False,
    )
```

profile of v0, /device:TPU:0, one launch (start us, length us, event | category | flops | bytes accessed | tf_op | source)
XLA Modules:
  0.0 1928.0 jit_solution(1926368836086712174)
XLA Ops:
  15.4 38.9 %all-gather.10.cloned.1.call-done = bf16[2048,512]{1,0:T(8,128)(2,1)} async-done(((bf16[128,512]{1,0:T(8,128)(2,1)}), bf16[2048,512]{1,0:T(8,128)(2,1)}) %all-gather.10.cloned.1.call-update) | async-done | bytes 2097168 | tf_op jit(solution)/shard_map/all_gather | solution.py:158
  54.3 4.0 copy.57
  58.4 38.3 %all-gather.8.cloned.1.call-done = bf16[2048,512]{1,0:T(8,128)(2,1)} async-done(((bf16[128,512]{1,0:T(8,128)(2,1)}), bf16[2048,512]{1,0:T(8,128)(2,1)}) %all-gather.8.cloned.1.call-update) | async-done | bytes 2097168 | tf_op jit(solution)/shard_map/all_gather | solution.py:159
  96.7 2.3 convolution_convert_fusion.2
  99.1 2.4 multiply_reduce_fusion.9
  103.1 45.3 %all-gather.12.cloned.1.call-done = bf16[2048,1024]{1,0:T(8,128)(2,1)} async-done(((bf16[128,1024]{1,0:T(8,128)(2,1)}), bf16[2048,1024]{1,0:T(8,128)(2,1)}) %all-gather.12.cloned.1.call-update) | async-done | bytes 4194320 | tf_op jit(solution)/shard_map/all_gather | solution.py:157
  148.4 6.5 copy.58
  154.9 3.7 multiply_reduce_fusion.6
  168.9 30.6 %all-gather.14.cloned.1.call-done = bf16[2048,1024]{1,0:T(8,128)(2,1)} async-done(((bf16[128,1024]{1,0:T(8,128)(2,1)}), bf16[2048,1024]{1,0:T(8,128)(2,1)}) %all-gather.14.cloned.1.call-update) | async-done | bytes 4194320 | tf_op jit(solution)/shard_map/all_gather | solution.py:160
  199.5 5.0 fusion.62
  207.1 59.0 %all-reduce.11.cloned.1.call-done = f32[256,2048]{1,0:T(8,128)} async-done(((f32[256,2048]{1,0:T(8,128)}), f32[256,2048]{1,0:T(8,128)}) %all-reduce.11.cloned.1.call-update) | async-done | bytes 2097168 | tf_op jit(solution)/shard_map/psum | solution.py:180
  271.0 98.2 %all-gather.16.cloned.1.call-done = bf16[2048,3072]{1,0:T(8,128)(2,1)} async-done(((bf16[128,3072]{1,0:T(8,128)(2,1)}), bf16[2048,3072]{1,0:T(8,128)(2,1)}) %all-gather.16.cloned.1.call-update) | async-done | bytes 12582928 | tf_op jit(solution)/shard_map/all_gather | solution.py:161
  369.2 9.9 fusion.63
  379.2 91.6 %all-gather.18.cloned.1.call-done = bf16[2048,3072]{1,0:T(8,128)(2,1)} async-done(((bf16[128,3072]{1,0:T(8,128)(2,1)}), bf16[2048,3072]{1,0:T(8,128)(2,1)}) %all-gather.18.cloned.1.call-update) | async-done | bytes 12582928 | tf_op jit(solution)/shard_map/all_gather | solution.py:162
  470.7 9.9 fusion.64
  480.7 91.6 %all-gather.20.cloned.1.call-done = bf16[2048,3072]{1,0:T(8,128)(2,1)} async-done(((bf16[128,3072]{1,0:T(8,128)(2,1)}), bf16[2048,3072]{1,0:T(8,128)(2,1)}) %all-gather.20.cloned.1.call-update) | async-done | bytes 12582928 | tf_op jit(solution)/shard_map/all_gather | solution.py:163
  572.2 12.2 multiply_convert_fusion
  584.4 7.6 fusion.66
  592.1 9.3 convolution_add_fusion.2
  601.5 10.5 fusion.65
  612.0 50.7 %all-reduce.13.cloned.1.call-done = f32[256,2048]{1,0:T(8,128)} async-done(((f32[256,2048]{1,0:T(8,128)}), f32[256,2048]{1,0:T(8,128)}) %all-reduce.13.cloned.1.call-update) | async-done | bytes 2097168 | tf_op jit(solution)/shard_map/psum | solution.py:202
  662.7 2.9 multiply_reduce_fusion
  670.7 2.2 reshape.341
  672.9 2.2 copy.69
  675.1 2.4 bitcast_convert_fusion
  677.4 2.9 fusion.23
  680.3 2.3 copy.81
  684.1 2.3 fusion.21
  697.1 13.8 convolution_bitcast_fusion
  711.6 3.8 fusion.36
  715.5 2.8 fusion.38
  718.7 6.3 fusion.42
  725.1 5.7 fusion.34
  730.8 13.6 fusion.68
  744.5 14.4 fusion.69
  760.8 44.7 %all-reduce.15.cloned.1.call-done = (f32[256,2048]{1,0:T(8,128)}, f32[256,2048]{1,0:T(8,128)}) async-done(((f32[256,2048]{1,0:T(8,128)}, f32[256,2048]{1,0:T(8,128)}), (f32[256,2048]{1,0:T(8,128)}, f32[256,2048]{1,0:T(8,128)})) %all-reduce.15.cloned.1.call-update) | async-done | bytes 4194320 | tf_op jit(solution)/shard_map/psum | solution.py:189
  805.5 2.1 fusion.16
  807.6 61.9 %all-reduce.4 = (f32[2048]{0:T(1024)S(1)}, f32[2048]{0:T(1024)S(1)}, f32[128]{0:T(128)S(1)}, f32[128]{0:T(128)S(1)}) all-reduce(f32[2048]{0:T(1024)S(1)} %get-tuple-element.54, f32[2048]{0:T(1024)S(1)} %copy-done.28, f32[128]{0:T(128)S(1)} %get-tuple-element.56, f32[128]{0:T(128)S(1)} %copy-done.38), channel_id=9, replica_groups=mesh['dp'=16,'mp'=2] {'dp'}, use_global_device_ids=true, to_apply=%region_24.25.clone | all-reduce | flops 4352 | bytes 34816
  870.3 5.4 all-reduce.5
  877.0 4.9 fusion.24
  881.9 172.1 %reduce-scatter.20.cloned.1.call-done = f32[128,3072]{0,1:T(8,128)} async-done(((f32[2048,3072]{0,1:T(8,128)}), f32[128,3072]{0,1:T(8,128)}) %reduce-scatter.20.cloned.1.call-update) | async-done | bytes 1572880 | tf_op jit(solution)/shard_map/reduce_scatter | solution.py:264
  1054.0 3.0 copy.71
  1057.0 73.3 %reduce-scatter.12.cloned.1.call-done = f32[128,512]{1,0:T(8,128)} async-done(((f32[2048,512]{1,0:T(8,128)}), f32[128,512]{1,0:T(8,128)}) %reduce-scatter.12.cloned.1.call-update) | async-done | bytes 262160 | tf_op jit(solution)/shard_map/reduce_scatter | solution.py:260
  1130.4 75.8 %reduce-scatter.10.cloned.1.call-done = f32[128,512]{1,0:T(8,128)} async-done(((f32[2048,512]{1,0:T(8,128)}), f32[128,512]{1,0:T(8,128)}) %reduce-scatter.10.cloned.1.call-update) | async-done | bytes 262160 | tf_op jit(solution)/shard_map/reduce_scatter | solution.py:259
  1206.1 108.8 %reduce-scatter.14.cloned.1.call-done = f32[128,1024]{1,0:T(8,128)} async-done(((f32[2048,1024]{1,0:T(8,128)}), f32[128,1024]{1,0:T(8,128)}) %reduce-scatter.14.cloned.1.call-update) | async-done | bytes 524304 | tf_op jit(solution)/shard_map/reduce_scatter | solution.py:261
  1314.9 109.4 %reduce-scatter.8.cloned.1.call-done = f32[128,1024]{1,0:T(8,128)} async-done(((f32[2048,1024]{1,0:T(8,128)}), f32[128,1024]{1,0:T(8,128)}) %reduce-scatter.8.cloned.1.call-update) | async-done | bytes 524304 | tf_op jit(solution)/shard_map/reduce_scatter | solution.py:258
  1424.3 248.7 %reduce-scatter.16.cloned.1.call-done = f32[128,3072]{1,0:T(8,128)} async-done(((f32[2048,3072]{1,0:T(8,128)}), f32[128,3072]{1,0:T(8,128)}) %reduce-scatter.16.cloned.1.call-update) | async-done | bytes 1572880 | tf_op jit(solution)/shard_map/reduce_scatter | solution.py:262
  1673.0 248.0 %reduce-scatter.18.cloned.1.call-done = f32[128,3072]{1,0:T(8,128)} async-done(((f32[2048,3072]{1,0:T(8,128)}), f32[128,3072]{1,0:T(8,128)}) %reduce-scatter.18.cloned.1.call-update) | async-done | bytes 1572880 | tf_op jit(solution)/shard_map/reduce_scatter | solution.py:263
  (166 shorter events, 48.4 us)
Async XLA Ops:
  7.2 47.1 %all-gather.10.cloned.1.call-start = ((), (), s32[]{:S(2)}) async-start(), calls=%async_computation.8 | async-start | bytes 2228224 | tf_op jit(solution)/shard_map/all_gather | solution.py:158
  7.9 88.8 %all-gather.8.cloned.1.call-start = ((), (), s32[]{:S(2)}) async-start(), calls=%async_computation.7 | async-start | bytes 2228224 | tf_op jit(solution)/shard_map/all_gather | solution.py:159
  8.7 139.7 %all-gather.12.cloned.1.call-start = ((), (), s32[]{:S(2)}) async-start(), calls=%async_computation.9 | async-start | bytes 4456448 | tf_op jit(solution)/shard_map/all_gather | solution.py:157
  9.4 190.1 %all-gather.14.cloned.1.call-start = ((), (), s32[]{:S(2)}) async-start(), calls=%async_computation.10 | async-start | bytes 4456448 | tf_op jit(solution)/shard_map/all_gather | solution.py:160
  10.0 256.1 %all-reduce.11.cloned.1.call-start = ((), (), s32[]{:S(2)}) async-start(), calls=%async_computation.11 | async-start | bytes 4194304 | tf_op jit(solution)/shard_map/psum | solution.py:180
  13.6 141.3 %copy-start.22 = (f32[256]{0:T(256)}, f32[256]{0:T(256)S(1)}, u32[]{:S(2)}) copy-start(f32[256]{0:T(256)S(1)} %get-tuple-element.88) | copy-start | bytes 3076
  54.3 42.4 %copy-start = (bf16[1,256,2048]{2,1,0:T(8,128)(2,1)S(1)}, bf16[1,256,2048]{2,1,0:T(8,128)(2,1)}, u32[]{:S(2)}) copy-start(bf16[1,256,2048]{2,1,0:T(8,128)(2,1)} %param.14) | copy-start | bytes 3145732
  54.3 42.4 %copy-start.20 = (f32[2048]{0:T(1024)S(1)}, f32[2048]{0:T(1024)}, u32[]{:S(2)}) copy-start(f32[2048]{0:T(1024)} %param.23) | copy-start | bytes 24580
  99.1 3.1 copy-start.32
  101.5 53.3 %copy-start.7 = (f32[256,4,128]{0,2,1:T(8,128)}, f32[256,4,128]{0,2,1:T(8,128)S(1)}, u32[]{:S(2)}) copy-start(f32[256,4,128]{0,2,1:T(8,128)S(1)} %get-tuple-element.92) | copy-start | bytes 1572868
  102.2 52.7 %copy-start.25 = (f32[256,4]{0,1:T(4,128)}, f32[256,4]{0,1:T(4,128)S(1)}, u32[]{:S(2)}) copy-start(f32[256,4]{0,1:T(4,128)S(1)} %get-tuple-element.84) | copy-start | bytes 12292
  154.9 4.4 copy-start.34
  158.6 3.8 copy-start.3
  166.4 2.5 copy-start.1
  204.5 164.8 %all-gather.16.cloned.1.call-start = ((), (), s32[]{:S(2)}) async-start(), calls=%async_computation.12 | async-start | bytes 13369344 | tf_op jit(solution)/shard_map/all_gather | solution.py:161
  205.1 265.7 %all-gather.18.cloned.1.call-start = ((), (), s32[]{:S(2)}) async-start(), calls=%async_computation.13 | async-start | bytes 13369344 | tf_op jit(solution)/shard_map/all_gather | solution.py:162
  205.8 366.4 %all-gather.20.cloned.1.call-start = ((), (), s32[]{:S(2)}) async-start(), calls=%async_computation.14 | async-start | bytes 13369344 | tf_op jit(solution)/shard_map/all_gather | solution.py:163
  206.6 456.1 %all-reduce.13.cloned.1.call-start = ((), (), s32[]{:S(2)}) async-start(), calls=%async_computation.15 | async-start | bytes 4194304 | tf_op jit(solution)/shard_map/psum | solution.py:202
  584.4 7.6 copy-start.17
  584.4 7.6 copy-start.16
  601.4 204.0 %all-reduce.15.cloned.1.call-start = ((), (), s32[]{:S(2)}) async-start(), calls=%async_computation.23 | async-start | bytes 8388608 | tf_op jit(solution)/shard_map/psum | solution.py:189
  662.7 2.9 copy-start.6
  662.7 2.9 copy-start.11
  662.7 2.9 copy-start.24
  662.7 2.9 copy-start.31
  662.7 2.9 copy-start.37
  665.6 2.9 copy-start.39
  666.2 1.3 copy-start.2
  684.0 2.4 copy-start.9
  684.1 2.4 copy-start.10
  687.4 1.0 copy-start.26
  687.4 1.0 copy-start.33
  687.7 1.6 copy-start.4
  687.7 1.6 copy-start.35
  689.3 2.4 copy-start.12
  690.2 2.7 copy-start.15
  691.7 1.6 copy-start.5
  693.3 1.7 copy-start.14
  697.1 356.9 %reduce-scatter.20.cloned.1.call-start = ((), (), s32[]{:S(2)}) async-start(), calls=%async_computation.22 | async-start | bytes 26738688 | tf_op jit(solution)/shard_map/reduce_scatter | solution.py:264
  711.0 419.4 %reduce-scatter.12.cloned.1.call-start = ((), (), s32[]{:S(2)}) async-start(), calls=%async_computation.18 | async-start | bytes 4456448 | tf_op jit(solution)/shard_map/reduce_scatter | solution.py:260
  715.5 490.7 %reduce-scatter.10.cloned.1.call-start = ((), (), s32[]{:S(2)}) async-start(), calls=%async_computation.17 | async-start | bytes 4456448 | tf_op jit(solution)/shard_map/reduce_scatter | solution.py:259
  718.4 596.5 %reduce-scatter.14.cloned.1.call-start = ((), (), s32[]{:S(2)}) async-start(), calls=%async_computation.19 | async-start | bytes 8912896 | tf_op jit(solution)/shard_map/reduce_scatter | solution.py:261
  725.0 699.3 %reduce-scatter.8.cloned.1.call-start = ((), (), s32[]{:S(2)}) async-start(), calls=%async_computation.16 | async-start | bytes 8912896 | tf_op jit(solution)/shard_map/reduce_scatter | solution.py:258
  730.8 942.3 %reduce-scatter.16.cloned.1.call-start = ((), (), s32[]{:S(2)}) async-start(), calls=%async_computation.20 | async-start | bytes 26738688 | tf_op jit(solution)/shard_map/reduce_scatter | solution.py:262
  744.4 1176.6 %reduce-scatter.18.cloned.1.call-start = ((), (), s32[]{:S(2)}) async-start(), calls=%async_computation.21 | async-start | bytes 26738688 | tf_op jit(solution)/shard_map/reduce_scatter | solution.py:263
  758.9 48.7 %copy-start.28 = (f32[2048]{0:T(1024)S(1)}, f32[2048]{0:T(1024)}, u32[]{:S(2)}) copy-start(f32[2048]{0:T(1024)} %get-tuple-element.52) | copy-start | bytes 24580
  758.9 48.7 %copy-start.38 = (f32[128]{0:T(128)S(1)}, f32[128]{0:T(128)}, u32[]{:S(2)}) copy-start(f32[128]{0:T(128)} %get-tuple-element.58) | copy-start | bytes 1540
  759.0 118.0 %copy-start.36 = (f32[256]{0:T(256)S(1)}, f32[256]{0:T(256)}, u32[]{:S(2)}) copy-start(f32[256]{0:T(256)} %get-tuple-element.87) | copy-start | bytes 3076
  (10 other events, 8.0 us)
Sparse Core Ops, SparseCore 0:
  10.2 44.0 all-gather.9
  56.5 40.1 all-gather.7
  98.8 49.4 all-gather.11
  150.4 49.0 all-gather.13
  204.6 61.3 all-reduce.10
  268.4 100.7 all-gather.15
  371.8 98.9 all-gather.17
  473.3 98.9 all-gather.19
  601.5 61.0 all-reduce.12
  697.2 108.2 all-reduce.14
  810.1 243.8 reduce-scatter.19
  1058.8 71.5 reduce-scatter.11
  1134.8 71.3 reduce-scatter.9
  1211.2 103.6 reduce-scatter.13
  1319.9 104.3 reduce-scatter.7
  1429.4 243.5 reduce-scatter.15
  1678.1 242.8 reduce-scatter.17
where the time goes:
time: 1940 us; the launch traced here: 1930 us
  waiting for transfers between devices  1630 us (84%)
  matrix products  149 us (8%)
  blocking collectives  67.4 us (3%)
  local copies, waits for them, and re-layouts  34.9 us (2%)
  other arithmetic  29.2 us (2%)
    reduce_scatter x1, waiting for transfers between devices, body(): lax.psum_scatter(totals[4], 'dp', scatter_dimension=0, tiled=True)  249 us
    reduce_scatter x1, waiting for transfers between devices, body(): lax.psum_scatter(totals[5], 'dp', scatter_dimension=0, tiled=True)  248 us
    reduce_scatter x1, waiting for transfers between devices, body(): lax.psum_scatter(totals[6], 'dp', scatter_dimension=0, tiled=True)  172 us
    dot_general x21, matrix products, matmul(): return jnp.dot(left_op, right_op, preferred_element_type=jnp.float32)  140 us
    reduce_scatter x1, waiting for transfers between devices, body(): lax.psum_scatter(totals[0], 'dp', scatter_dimension=0, tiled=True)  109 us
    reduce_scatter x1, waiting for transfers between devices, body(): lax.psum_scatter(totals[3], 'dp', scatter_dimension=0, tiled=True)  109 us
    all_gather x1, waiting for transfers between devices, body(): full_gate = lax.all_gather(w_gate, 'dp', axis=0, tiled=True)  98.2 us
    all_gather x1, waiting for transfers between devices, body(): full_down = lax.all_gather(w_down, 'dp', axis=0, tiled=True)  91.6 us
  transfers between devices with their start and end apart: 17, of which 17 were waited for; matrix products, arithmetic and copies ran while one was open for 7% of the time, Pallas kernels for 0%

commit v1 on v0

--- a/solution.py
+++ b/solution.py
@@ -1,8 +1,11 @@
+import functools
 import math
 
 import jax
 import jax.numpy as jnp
 from jax import lax
+from jax.experimental import pallas as pl
+from jax.experimental.pallas import tpu as pltpu
 from jax.sharding import PartitionSpec as P
 
 EPSILON = 1e-06
@@ -125,7 +128,559 @@
     return (grad_queries, grad_keys, grad_values)
 
 
+MESH = pl.DeviceIdType.MESH
+ANY = pl.BlockSpec(memory_space=pl.ANY)
+VMEM = pl.BlockSpec(memory_space=pltpu.VMEM)
+DEPTH = 4
+CORES = 2
+HALVES = 2
+
+
+class Place:
+    def __init__(self, dp_size):
+        self.wide = dp_size // (DEPTH * CORES)
+        here = lax.axis_index("dp")
+        self.x = lax.axis_index("mp")
+        self.z = lax.div(here, jnp.int32(self.wide * CORES))
+        self.y = lax.rem(lax.div(here, jnp.int32(CORES)), jnp.int32(self.wide))
+        self.c = lax.rem(here, jnp.int32(CORES))
+
+    def device(self, z=None, y=None, c=None, x=None):
+        z = self.z if z is None else z
+        y = self.y if y is None else y
+        c = self.c if c is None else c
+        x = self.x if x is None else x
+        return ((z * self.wide + y) * CORES + c, x)
+
+    def z_off(self, step):
+        return lax.rem(self.z + DEPTH + step, jnp.int32(DEPTH))
+
+    def y_off(self, step):
+        return lax.rem(self.y + self.wide + step, jnp.int32(self.wide))
+
+
+def snake(z, side):
+    odd = lax.rem(side, jnp.int32(2))
+    return side * DEPTH + z + odd * (DEPTH - 1 - 2 * z)
+
+
+def unsnake(index, size):
+    index = lax.rem(index + 2 * size, jnp.int32(size))
+    side = lax.div(index, jnp.int32(DEPTH))
+    rest = lax.rem(index, jnp.int32(DEPTH))
+    return rest + lax.rem(side, jnp.int32(2)) * (DEPTH - 1 - 2 * rest), side
+
+
+class Mail:
+    def __init__(self, send_sems, recv_sems):
+        self.send_sems, self.recv_sems = send_sems, recv_sems
+        self.count = 0
+        self.open = []
+
+    def send(self, source, target, device):
+        copy = pltpu.make_async_remote_copy(
+            source,
+            target,
+            self.send_sems.at[self.count],
+            self.recv_sems.at[self.count],
+            device_id=device,
+            device_id_type=MESH,
+        )
+        self.count += 1
+        copy.start()
+        self.open.append(copy)
+        return copy
+
+    def finish(self):
+        for copy in self.open:
+            copy.wait_send()
+
+
+def meet(devices):
+    barrier = pltpu.get_barrier_semaphore()
+    for device in devices:
+        pl.semaphore_signal(barrier, inc=1, device_id=device, device_id_type=MESH)
+    pl.semaphore_wait(barrier, len(devices))
+
+
+def receive(copies):
+    for copy in copies:
+        copy.wait_recv()
+
+
+def own_copies(pairs, sems):
+    copies = [
+        pltpu.make_async_copy(source, target, sems.at[i]) for i, (source, target) in enumerate(pairs)
+    ]
+    for copy in copies:
+        copy.start()
+    return copies
+
+
+def gather_kernel(
+    dp_size, w_q, w_k, w_v, w_o, w_g, w_u, w_d, cot,
+    o_q, o_k, o_v, o_o, o_g, o_u, o_d, o_c, own_sems, send_sems, recv_sems,
+):
+    at = Place(dp_size)
+    z, y, c, x = at.z, at.y, at.c, at.x
+    ring = DEPTH * at.wide
+    loop = DEPTH * HALVES
+    spot, seat = snake(z, y), snake(z, x)
+    ring_z, ring_y = unsnake(spot + 1, ring)
+    back_z, back_y = unsnake(spot - 1, ring)
+    ahead, behind = at.device(z=ring_z, y=ring_y), at.device(z=back_z, y=back_y)
+    loop_z, loop_x = unsnake(seat + 1, loop)
+    tail_z, tail_x = unsnake(seat - 1, loop)
+    after, before = at.device(z=loop_z, x=loop_x), at.device(z=tail_z, x=tail_x)
+    sibling = at.device(c=1 - c)
+    z_peers = [at.device(z=at.z_off(k)) for k in range(1, DEPTH)]
+    y_peers = [at.device(y=at.y_off(j)) for j in range(1, at.wide)]
+    meet([ahead, behind, after, before, sibling] + z_peers + y_peers)
+
+    mail = Mail(send_sems, recv_sems)
+    part = w_g.shape[1] // DEPTH
+    tokens = cot.shape[0] // HALVES
+    strip = tokens // 2
+    ffn = ((w_g, o_g), (w_u, o_u), (w_d, o_d))
+    attn = ((w_q, o_q), (w_k, o_k), (w_v, o_v), (w_o, o_o))
+
+    def columns(index):
+        return pl.ds(pl.multiple_of(index * part, part), part)
+
+    mine = own_copies(
+        [(weight, out.at[z, y, c]) for weight, out in attn]
+        + [(weight.at[:, columns(z)], out.at[z, y, c]) for weight, out in ffn]
+        + [(cot.at[pl.ds(pl.multiple_of(x * tokens, tokens), tokens)], o_c.at[z, x])],
+        own_sems,
+    )
+
+    to_sibling = []
+    rounds = [
+        mail.send(weight, out.at[z, y, c], ahead if i < 2 else behind)
+        for i, (weight, out) in enumerate(attn)
+    ]
+    turns = [
+        mail.send(
+            cot.at[pl.ds(pl.multiple_of(x * tokens + i * strip, strip), strip)],
+            o_c.at[z, x, pl.ds(i * strip, strip)],
+            after if i == 0 else before,
+        )
+        for i in range(2)
+    ]
+    spread = {}
+    for k in range(1, DEPTH):
+        target = at.z_off(k)
+        spread[k] = [
+            mail.send(weight.at[:, columns(target)], out.at[z, y, c], z_peers[k - 1])
+            for weight, out in ffn
+        ]
+    crossing = {}
+    for j in range(1, at.wide):
+        crossing[0, j] = [
+            mail.send(weight.at[:, columns(z)], out.at[z, y, c], y_peers[j - 1])
+            for weight, out in ffn
+        ]
+    to_sibling += [mail.send(weight, out.at[z, y, c], sibling) for weight, out in attn]
+    to_sibling += [
+        mail.send(weight.at[:, columns(z)], out.at[z, y, c], sibling) for weight, out in ffn
+    ]
+
+    for step in range(max(ring, loop) - 1):
+        if step < ring - 1:
+            receive(rounds)
+            one_z, one_y = unsnake(spot - 1 - step, ring)
+            two_z, two_y = unsnake(spot + 1 + step, ring)
+            places = [(one_z, one_y)] * 2 + [(two_z, two_y)] * 2
+            blocks = [out.at[pz, py, c] for (_, out), (pz, py) in zip(attn, places)]
+            if step < ring - 2:
+                rounds = [
+                    mail.send(block, block, ahead if i < 2 else behind)
+                    for i, block in enumerate(blocks)
+                ]
+            to_sibling += [mail.send(block, block, sibling) for block in blocks]
+        if step < loop - 1:
+            receive(turns)
+            one_z, one_x = unsnake(seat - 1 - step, loop)
+            two_z, two_x = unsnake(seat + 1 + step, loop)
+            if step < loop - 2:
+                first = o_c.at[one_z, one_x, pl.ds(0, strip)]
+                second = o_c.at[two_z, two_x, pl.ds(strip, strip)]
+                turns = [mail.send(first, first, after), mail.send(second, second, before)]
+        k = step - 1
+        if 1 <= k < DEPTH:
+            receive(spread[k])
+            source = at.z_off(-k)
+            blocks = [out.at[source, y, c] for _, out in ffn]
+            for j in range(1, at.wide):
+                crossing[k, j] = [mail.send(block, block, y_peers[j - 1]) for block in blocks]
+            to_sibling += [mail.send(block, block, sibling) for block in blocks]
+        k = step - 3
+        if 0 <= k < DEPTH:
+            source = at.z_off(-k)
+            for j in range(1, at.wide):
+                receive(crossing[k, j])
+                blocks = [out.at[source, at.y_off(-j), c] for _, out in ffn]
+                to_sibling += [mail.send(block, block, sibling) for block in blocks]
+    receive(to_sibling)
+    mail.finish()
+    for copy in mine:
+        copy.wait()
+
+
+def gather_copies(dp_size):
+    wide = dp_size // (DEPTH * CORES)
+    ring, loop = DEPTH * wide, DEPTH * HALVES
+    return 4 * (ring - 1) + 2 * (loop - 1) + 9 + 3 * DEPTH * (wide - 1) + 4 * ring + 3 * ring
+
+
+def gather(dp_size, w_q, w_k, w_v, w_o, w_g, w_u, w_d, cot):
+    wide = dp_size // (DEPTH * CORES)
+    rows = w_q.shape[0]
+    grid = (DEPTH, wide, CORES, rows)
+    part = w_g.shape[1] // DEPTH
+    half = jnp.bfloat16
+    shapes = [jax.ShapeDtypeStruct(grid + (w.shape[1],), half) for w in (w_q, w_k, w_v, w_o)]
+    shapes += [jax.ShapeDtypeStruct(grid + (part,), half)] * 3
+    shapes += [jax.ShapeDtypeStruct((DEPTH, HALVES, cot.shape[0] // HALVES, cot.shape[1]), half)]
+    copies = gather_copies(dp_size)
+    return pl.pallas_call(
+        functools.partial(gather_kernel, dp_size),
+        out_shape=shapes,
+        in_specs=[ANY] * 8,
+        out_specs=[ANY] * 8,
+        scratch_shapes=[
+            pltpu.SemaphoreType.DMA((8,)),
+            pltpu.SemaphoreType.DMA((copies,)),
+            pltpu.SemaphoreType.DMA((copies,)),
+        ],
+        compiler_params=pltpu.CompilerParams(collective_id=0, has_side_effects=True),
+    )(w_q, w_k, w_v, w_o, w_g, w_u, w_d, cot)
+
+
+def middle_kernel(
+    dp_size, partial, row_in, gain, mid, o_n, outgoing, incoming, normed, own_sems, send_sems, recv_sems
+):
+    at = Place(dp_size)
+    z, x = at.z, at.x
+    loop = DEPTH * HALVES
+    seat = snake(z, x)
+    loop_z, loop_x = unsnake(seat + 1, loop)
+    tail_z, tail_x = unsnake(seat - 1, loop)
+    after, before = at.device(z=loop_z, x=loop_x), at.device(z=tail_z, x=tail_x)
+    other = at.device(x=1 - x)
+    tokens = mid.shape[0]
+    strip = tokens // 2
+    kept = pl.ds(pl.multiple_of(x * tokens, tokens), tokens)
+    given = pl.ds(pl.multiple_of((1 - x) * tokens, tokens), tokens)
+    outgoing[...] = partial[given, :].astype(jnp.bfloat16)
+    meet([after, before, other])
+    mail = Mail(send_sems, recv_sems)
+    swap = mail.send(outgoing, incoming, other)
+    swap.wait_recv()
+    values = row_in[kept, :].astype(jnp.float32) + (
+        partial[kept, :] + incoming[...].astype(jnp.float32)
+    )
+    mid[...] = values
+    inv_rms = lax.rsqrt(jnp.mean(values * values, axis=-1, keepdims=True) + EPSILON)
+    normed[...] = (values * inv_rms * gain[...]).astype(jnp.bfloat16)
+    mine = own_copies([(normed, o_n.at[z, x])], own_sems)
+    turns = [
+        mail.send(
+            normed.at[pl.ds(i * strip, strip)],
+            o_n.at[z, x, pl.ds(i * strip, strip)],
+            after if i == 0 else before,
+        )
+        for i in range(2)
+    ]
+    for step in range(loop - 1):
+        receive(turns)
+        one_z, one_x = unsnake(seat - 1 - step, loop)
+        two_z, two_x = unsnake(seat + 1 + step, loop)
+        if step < loop - 2:
+            first = o_n.at[one_z, one_x, pl.ds(0, strip)]
+            second = o_n.at[two_z, two_x, pl.ds(strip, strip)]
+            turns = [mail.send(first, first, after), mail.send(second, second, before)]
+    mail.finish()
+    for copy in mine:
+        copy.wait()
+
+
+def middle(dp_size, partial, row_in, gain):
+    tokens, width = partial.shape[0] // HALVES, partial.shape[1]
+    copies = 1 + 2 * (DEPTH * HALVES - 1)
+    return pl.pallas_call(
+        functools.partial(middle_kernel, dp_size),
+        out_shape=[
+            jax.ShapeDtypeStruct((tokens, width), jnp.float32),
+            jax.ShapeDtypeStruct((DEPTH, HALVES, tokens, width), jnp.bfloat16),
+        ],
+        in_specs=[VMEM] * 3,
+        out_specs=[VMEM, ANY],
+        scratch_shapes=[
+            pltpu.VMEM((tokens, width), jnp.bfloat16),
+            pltpu.VMEM((tokens, width), jnp.bfloat16),
+            pltpu.VMEM((tokens, width), jnp.bfloat16),
+            pltpu.SemaphoreType.DMA((1,)),
+            pltpu.SemaphoreType.DMA((copies,)),
+            pltpu.SemaphoreType.DMA((copies,)),
+        ],
+        compiler_params=pltpu.CompilerParams(
+            collective_id=1, has_side_effects=True, vmem_limit_bytes=40 * 2**20
+        ),
+    )(partial, row_in, gain[None, :])
+
+
+def add_into(target, *others):
+    total = target[...].astype(jnp.float32)
+    for other in others:
+        total = total + other[...].astype(jnp.float32)
+    target[...] = total.astype(target.dtype)
+
+
+def ffn_reduce_kernel(
+    dp_size, p_n, p_o, g_g, g_u, g_d, mid, cot, gain,
+    o_m, o_h, o_l, o_t, w_g, w_u, w_d,
+    r_n, r_o, c_g, c_u, c_d, y_g, y_u, y_d, z_g, z_u, z_d, send_sems, recv_sems,
+):
+    at = Place(dp_size)
+    z, y, c, x = at.z, at.y, at.c, at.x
+    loop = DEPTH * HALVES
+    seat = snake(z, x)
+    loop_z, loop_x = unsnake(seat + 1, loop)
+    tail_z, tail_x = unsnake(seat - 1, loop)
+    after, before = at.device(z=loop_z, x=loop_x), at.device(z=tail_z, x=tail_x)
+    other = at.device(x=1 - x)
+    sibling = at.device(c=1 - c)
+    z_peers = [at.device(z=at.z_off(k)) for k in range(1, DEPTH)]
+    y_peers = [at.device(y=at.y_off(j)) for j in range(1, at.wide)]
+    meet([after, before, other, sibling] + z_peers + y_peers)
+    mail = Mail(send_sems, recv_sems)
+    tokens = mid.shape[0]
+    strip = tokens // 2
+    part = w_g.shape[1] // DEPTH
+    strips = (pl.ds(0, strip), pl.ds(strip, strip))
+    grads = ((g_g, c_g, y_g, z_g, w_g), (g_u, c_u, y_u, z_u, w_u), (g_d, c_d, y_d, z_d, w_d))
+
+    def block(array, i, step):
+        shift = -1 - step if i == 0 else 1 + step
+        bz, bx = unsnake(seat + shift, loop)
+        return array.at[bz, bx, strips[i]]
+
+    def ring_start(array, landing):
+        return [
+            mail.send(block(array, i, 0), landing.at[0, i], after if i == 0 else before)
+            for i in range(2)
+        ]
+
+    def ring_step(turns, array, landing, step):
+        receive(turns)
+        turns = []
+        for i in range(2):
+            add_into(landing.at[step, i], block(array, i, step + 1))
+            turns.append(
+                mail.send(landing.at[step, i], landing.at[step + 1, i], after if i == 0 else before)
+            )
+        return turns
+
+    turns_n = ring_start(p_n, r_n)
+    order = [(k, at.z_off(k)) for k in (2, 1, 3, 0)]
+    to_core = {
+        k: [mail.send(grad.at[to, :, 1 - c], land.at[to], sibling) for grad, land, *_ in grads]
+        for k, to in order
+    }
+    turns_o = ring_start(p_o, r_o)
+    to_y, to_z = {}, {}
+
+    def core_stage(k, to):
+        receive(to_core[k])
+        for grad, land, *_ in grads:
+            for row in range(at.wide):
+                add_into(land.at[to, row], grad.at[to, row, c])
+        to_y[k] = [
+            mail.send(land.at[to, at.y_off(j)], arrive.at[j - 1, to], y_peers[j - 1])
+            for j in range(1, at.wide)
+            for _, land, arrive, *_ in grads
+        ]
+
+    def y_stage(k, to):
+        receive(to_y[k])
+        for _, land, arrive, *_ in grads:
+            add_into(land.at[to, y], *[arrive.at[j - 1, to] for j in range(1, at.wide)])
+        if k > 0:
+            to_z[k] = [
+                mail.send(land.at[to, y], last.at[k - 1], z_peers[k - 1])
+                for _, land, _, last, _ in grads
+            ]
+
+    def final_norm():
+        receive(turns_n)
+        gain_sum = jnp.zeros(o_t.shape, jnp.float32)
+        kept = pl.multiple_of(x * tokens, tokens)
+        for i in range(2):
+            grad_norm = r_n[loop - 2, i].astype(jnp.float32) + p_n[z, x, strips[i]].astype(jnp.float32)
+            values = mid[strips[i], :]
+            inv_rms = lax.rsqrt(jnp.mean(values * values, axis=-1, keepdims=True) + EPSILON)
+            grad_values, terms = norm_back(grad_norm, values, inv_rms, gain[...])
+            gain_sum = gain_sum + jnp.sum(terms, axis=0, keepdims=True)
+            rows = pl.ds(pl.multiple_of(kept + i * strip, strip), strip)
+            total = cot[rows, :].astype(jnp.float32) + grad_values
+            o_m[strips[i], :] = total
+            o_h[rows, :] = total.astype(jnp.bfloat16)
+        o_t[...] = gain_sum
+        rows = pl.ds(kept, tokens)
+        return mail.send(o_h.at[rows], o_h.at[rows], other)
+
+    for step in range(loop - 2):
+        turns_n = ring_step(turns_n, p_n, r_n, step)
+        if step < DEPTH:
+            core_stage(*order[step])
+        if 2 <= step:
+            y_stage(*order[step - 2])
+        turns_o = ring_step(turns_o, p_o, r_o, step)
+    swap_h = final_norm()
+    receive(turns_o)
+    kept = pl.multiple_of(x * tokens, tokens)
+    for i in range(2):
+        rows = pl.ds(pl.multiple_of(kept + i * strip, strip), strip)
+        total = r_o[loop - 2, i].astype(jnp.float32) + p_o[z, x, strips[i]].astype(jnp.float32)
+        o_l[rows, :] = (mid[strips[i], :] + total).astype(jnp.bfloat16)
+    rows = pl.ds(kept, tokens)
+    swap_l = mail.send(o_l.at[rows], o_l.at[rows], other)
+    for _, land, _, last, out in grads:
+        for k in range(DEPTH):
+            source = at.z_off(-k)
+            columns = pl.ds(pl.multiple_of(source * part, part), part)
+            if k == 0:
+                out[:, columns] = land[z, y].astype(jnp.float32)
+    for k in range(1, DEPTH):
+        receive(to_z[k])
+        source = at.z_off(-k)
+        columns = pl.ds(pl.multiple_of(source * part, part), part)
+        for _, _, _, last, out in grads:
+            out[:, columns] = last[k - 1].astype(jnp.float32)
+    receive([swap_h, swap_l])
+    mail.finish()
+
+
+def ffn_reduce(dp_size, p_n, p_o, g_g, g_u, g_d, mid, cot, gain):
+    wide = dp_size // (DEPTH * CORES)
+    tokens, width = mid.shape
+    loop = DEPTH * HALVES
+    rows, part = g_g.shape[-2:]
+    copies = 4 * (loop - 1) + 3 * DEPTH + 3 * DEPTH * (wide - 1) + 9 + 2
+    half = jnp.bfloat16
+    return pl.pallas_call(
+        functools.partial(ffn_reduce_kernel, dp_size),
+        out_shape=[
+            jax.ShapeDtypeStruct((tokens, width), jnp.float32),
+            jax.ShapeDtypeStruct((HALVES * tokens, width), half),
+            jax.ShapeDtypeStruct((HALVES * tokens, width), half),
+            jax.ShapeDtypeStruct((1, width), jnp.float32),
+        ]
+        + [jax.ShapeDtypeStruct((rows, part * DEPTH), jnp.float32)] * 3,
+        in_specs=[VMEM] * 8,
+        out_specs=[VMEM] * 7,
+        scratch_shapes=[pltpu.VMEM((loop - 1, 2, tokens // 2, width), half)] * 2
+        + [pltpu.VMEM((DEPTH, wide, rows, part), half)] * 3
+        + [pltpu.VMEM((wide - 1, DEPTH, rows, part), half)] * 3
+        + [pltpu.VMEM((DEPTH - 1, rows, part), half)] * 3
+        + [pltpu.SemaphoreType.DMA((copies,)), pltpu.SemaphoreType.DMA((copies,))],
+        compiler_params=pltpu.CompilerParams(
+            collective_id=2, has_side_effects=True, vmem_limit_bytes=58 * 2**20
+        ),
+    )(p_n, p_o, g_g, g_u, g_d, mid, cot, gain[None, :])
+
+
+def attn_reduce_kernel(
+    dp_size, g_q, g_k, g_v, g_o, partial, row_in, grad_mid, gain,
+    o_i, w_q, w_k, w_v, w_o,
+    outgoing, incoming, c_q, c_k, c_v, c_o, r_q, r_k, r_v, r_o, send_sems, recv_sems,
+):
+    at = Place(dp_size)
+    z, y, c, x = at.z, at.y, at.c, at.x
+    ring = DEPTH * at.wide
+    spot = snake(z, y)
+    ring_z, ring_y = unsnake(spot + 1, ring)
+    back_z, back_y = unsnake(spot - 1, ring)
+    ahead, behind = at.device(z=ring_z, y=ring_y), at.device(z=back_z, y=back_y)
+    other = at.device(x=1 - x)
+    sibling = at.device(c=1 - c)
+    tokens = grad_mid.shape[0]
+    kept = pl.ds(pl.multiple_of(x * tokens, tokens), tokens)
+    given = pl.ds(pl.multiple_of((1 - x) * tokens, tokens), tokens)
+    outgoing[...] = partial[given, :].astype(jnp.bfloat16)
+    meet([ahead, behind, other, sibling])
+    mail = Mail(send_sems, recv_sems)
+    sets = ((g_q, c_q, r_q, w_q), (g_k, c_k, r_k, w_k), (g_v, c_v, r_v, w_v), (g_o, c_o, r_o, w_o))
+
+    def spot_of(i, step):
+        return unsnake(spot + (-1 - step if i < 2 else 1 + step), ring)
+
+    to_core = []
+    for step in range(ring):
+        row = []
+        for i, (grad, land, _, _) in enumerate(sets):
+            bz, by = spot_of(i, step)
+            row.append(mail.send(grad.at[bz, by, 1 - c], land.at[bz, by], sibling))
+        to_core.append(row)
+    swap = mail.send(outgoing, incoming, other)
+    turns = []
+    for step in range(ring):
+        receive(to_core[step])
+        if step > 0:
+            receive(turns)
+        turns = []
+        for i, (grad, land, arrive, out) in enumerate(sets):
+            bz, by = spot_of(i, step)
+            terms = [grad[bz, by, c].astype(jnp.float32), land[bz, by].astype(jnp.float32)]
+            if step > 0:
+                terms.append(arrive[step - 1].astype(jnp.float32))
+            total = sum(terms[1:], terms[0])
+            if step < ring - 1:
+                land[bz, by] = total.astype(jnp.bfloat16)
+                turns.append(
+                    mail.send(land.at[bz, by], arrive.at[step], ahead if i < 2 else behind)
+                )
+            else:
+                out[...] = total
+        if step == 1:
+            swap.wait_recv()
+            grad_norm = partial[kept, :] + incoming[...].astype(jnp.float32)
+            values = row_in[kept, :].astype(jnp.float32)
+            inv_rms = lax.rsqrt(jnp.mean(values * values, axis=-1, keepdims=True) + EPSILON)
+            grad_values, _ = norm_back(grad_norm, values, inv_rms, gain[...])
+            o_i[kept, :] = (grad_mid[...] + grad_values).astype(jnp.bfloat16)
+            swap_back = mail.send(o_i.at[kept], o_i.at[kept], other)
+    swap_back.wait_recv()
+    mail.finish()
+
+
+def attn_reduce(dp_size, grads, partial, row_in, grad_mid, gain):
+    wide = dp_size // (DEPTH * CORES)
+    ring = DEPTH * wide
+    tokens, width = grad_mid.shape
+    half = jnp.bfloat16
+    rows = grads[0].shape[-2]
+    cols = [grad.shape[-1] for grad in grads]
+    copies = 4 * ring + 4 * (ring - 1) + 2
+    return pl.pallas_call(
+        functools.partial(attn_reduce_kernel, dp_size),
+        out_shape=[jax.ShapeDtypeStruct((HALVES * tokens, width), half)]
+        + [jax.ShapeDtypeStruct((rows, col), jnp.float32) for col in cols],
+        in_specs=[VMEM] * 8,
+        out_specs=[VMEM] * 5,
+        scratch_shapes=[pltpu.VMEM((tokens, width), half)] * 2
+        + [pltpu.VMEM((DEPTH, wide, rows, col), half) for col in cols]
+        + [pltpu.VMEM((ring - 1, rows, col), half) for col in cols]
+        + [pltpu.SemaphoreType.DMA((copies,)), pltpu.SemaphoreType.DMA((copies,))],
+        compiler_params=pltpu.CompilerParams(
+            collective_id=3, has_side_effects=True, vmem_limit_bytes=58 * 2**20
+        ),
+    )(*grads, partial, row_in, grad_mid, gain[None, :])
+
+
 def body(
+    dp_size,
     layer_in,
     seg_ids,
     w_q,
@@ -143,28 +698,19 @@
 ):
     head_dim = q_gain.shape[0]
     group_size = w_q.shape[1] // w_k.shape[1]
-    model_width = w_q.shape[0] * lax.axis_size("dp")
-    totals = [
-        jnp.zeros((model_width, shard.shape[1]), jnp.float32)
-        for shard in (w_q, w_k, w_v, w_o, w_gate, w_up, w_down)
-    ]
-    totals = totals + [
-        jnp.zeros((model_width,), jnp.float32),
-        jnp.zeros((model_width,), jnp.float32),
-        jnp.zeros((head_dim,), jnp.float32),
-        jnp.zeros((head_dim,), jnp.float32),
-    ]
-    full_q = lax.all_gather(w_q, "dp", axis=0, tiled=True)
-    full_k = lax.all_gather(w_k, "dp", axis=0, tiled=True)
-    full_v = lax.all_gather(w_v, "dp", axis=0, tiled=True)
-    full_o = lax.all_gather(w_o, "dp", axis=0, tiled=True)
-    full_gate = lax.all_gather(w_gate, "dp", axis=0, tiled=True)
-    full_up = lax.all_gather(w_up, "dp", axis=0, tiled=True)
-    full_down = lax.all_gather(w_down, "dp", axis=0, tiled=True)
+    rows = w_q.shape[0]
+    width = rows * dp_size
+    wide = dp_size // (DEPTH * CORES)
     row_in = layer_in[0]
     seg_row = seg_ids[0]
     row_cot = cotangent[0]
     seq_len = row_in.shape[0]
+    gathered = gather(dp_size, w_q, w_k, w_v, w_o, w_gate, w_up, w_down, row_cot)
+    full_q, full_k, full_v, full_o, part_gate, part_up, part_down = [
+        array.reshape(width, -1) for array in gathered[:7]
+    ]
+    cots = gathered[7].reshape(-1, width)
+
     residual = row_in.astype(jnp.float32)
     normed_full, scale_one = rms_norm(residual, attn_gain)
     normed_one = normed_full.astype(jnp.bfloat16)
@@ -177,38 +723,36 @@
     queries_half = rope_apply(query_norm, cosine_table, sine_table).astype(jnp.bfloat16)
     keys_half = rope_apply(key_norm, cosine_table, sine_table).astype(jnp.bfloat16)
     context_half, log_total = attend(queries_half, keys_half, values_half, seg_row, group_size)
-    attn_out = lax.psum(matmul(context_half, full_o.T), "mp")
-    mid = residual + attn_out
-    normed_mid, scale_two = rms_norm(mid, mlp_gain)
-    normed_two = normed_mid.astype(jnp.bfloat16)
-    gate_pre = matmul(normed_two, full_gate)
-    up_pre = matmul(normed_two, full_up)
+
+    mid, normed = middle(dp_size, matmul(context_half, full_o.T), row_in, mlp_gain)
+    normed_two = normed.reshape(-1, width)
+    gate_pre = matmul(normed_two, part_gate)
+    up_pre = matmul(normed_two, part_up)
     sigmoid_gate = jax.nn.sigmoid(gate_pre)
     silu_val = gate_pre * sigmoid_gate
     act_half = (silu_val * up_pre).astype(jnp.bfloat16)
-    mlp_out = lax.psum(matmul(act_half, full_down.T), "mp")
-    out_rows = [(mid + mlp_out).astype(jnp.bfloat16)]
-    full_gate = lax.all_gather(w_gate, "dp", axis=0, tiled=True)
-    full_up = lax.all_gather(w_up, "dp", axis=0, tiled=True)
-    full_down = lax.all_gather(w_down, "dp", axis=0, tiled=True)
-    grad_act = matmul(row_cot, full_down)
-    grad_down = matmul(row_cot.T, act_half)
+    out_part = matmul(act_half, part_down.T).astype(jnp.bfloat16)
+    grad_act = matmul(cots, part_down)
     grad_gate_pre = (
         grad_act * up_pre * sigmoid_gate * (1.0 + gate_pre * (1.0 - sigmoid_gate))
     ).astype(jnp.bfloat16)
     grad_up_pre = (grad_act * silu_val).astype(jnp.bfloat16)
-    grad_gate = matmul(normed_two.T, grad_gate_pre)
-    grad_up = matmul(normed_two.T, grad_up_pre)
-    grad_normed_two = lax.psum(
-        matmul(grad_gate_pre, full_gate.T) + matmul(grad_up_pre, full_up.T), "mp"
-    )
-    grad_mid_norm, gain_two_terms = norm_back(grad_normed_two, mid, scale_two, mlp_gain)
-    grad_mid = row_cot.astype(jnp.float32) + grad_mid_norm
-    grad_mid_half = grad_mid.astype(jnp.bfloat16)
-    full_q = lax.all_gather(w_q, "dp", axis=0, tiled=True)
-    full_k = lax.all_gather(w_k, "dp", axis=0, tiled=True)
-    full_v = lax.all_gather(w_v, "dp", axis=0, tiled=True)
-    full_o = lax.all_gather(w_o, "dp", axis=0, tiled=True)
+    norm_part = (
+        matmul(grad_gate_pre, part_gate.T) + matmul(grad_up_pre, part_up.T)
+    ).astype(jnp.bfloat16)
+    grads = [
+        matmul(left.T, right).astype(jnp.bfloat16).reshape(DEPTH, wide, CORES, rows, -1)
+        for left, right in (
+            (normed_two, grad_gate_pre),
+            (normed_two, grad_up_pre),
+            (cots, act_half),
+        )
+    ]
+    shape = (DEPTH, HALVES, seq_len // HALVES, width)
+    grad_mid, grad_mid_half, out_row, gain_two, grad_gate, grad_up, grad_down = ffn_reduce(
+        dp_size, norm_part.reshape(shape), out_part.reshape(shape), *grads, mid, row_cot, mlp_gain
+    )
+
     grad_o = matmul(grad_mid_half.T, context_half)
     grad_context_half = matmul(grad_mid_half, full_o).astype(jnp.bfloat16)
     grad_queries, grad_keys, grad_values = attend_back(
@@ -235,44 +779,47 @@
         + matmul(key_grad_half, full_k.T)
         + matmul(value_grad_half, full_v.T)
     )
-    grad_normed_one, q_gain_sum, k_gain_sum = lax.psum(
-        (normed_part, jnp.sum(q_gain_terms, axis=(0, 1)), jnp.sum(k_gain_terms, axis=(0, 1))), "mp"
-    )
-    grad_res_norm, gain_one_terms = norm_back(grad_normed_one, residual, scale_one, attn_gain)
-    grad_rows = [(grad_mid + grad_res_norm).astype(jnp.bfloat16)]
-    new_terms = [
-        matmul(normed_one.T, query_grad_half),
-        matmul(normed_one.T, key_grad_half),
-        matmul(normed_one.T, value_grad_half),
+    grads = [
+        matmul(left.T, right).astype(jnp.bfloat16).reshape(DEPTH, wide, CORES, rows, -1)
+        for left, right in (
+            (normed_one, query_grad_half),
+            (normed_one, key_grad_half),
+            (normed_one, value_grad_half),
+        )
+    ] + [grad_o.astype(jnp.bfloat16).reshape(DEPTH, wide, CORES, rows, -1)]
+    in_grad, grad_q, grad_k, grad_v, grad_o = attn_reduce(
+        dp_size, grads, normed_part, row_in, grad_mid, attn_gain
+    )
+
+    gain_one = jnp.sum(normed_part * residual * scale_one, axis=0)
+    gains = [gain_one, gain_two[0], jnp.sum(q_gain_terms, axis=(0, 1)), jnp.sum(k_gain_terms, axis=(0, 1))]
+    sizes = [gain.shape[0] for gain in gains]
+    summed = lax.psum(jnp.concatenate(gains), ("dp", "mp"))
+    gain_outs = []
+    start = 0
+    for size in sizes:
+        share = size // dp_size
+        gain_outs.append(
+            lax.dynamic_slice(summed, (start + lax.axis_index("dp") * share,), (share,))
+        )
+        start += size
+    return (
+        out_row[None],
+        in_grad[None],
+        grad_q,
+        grad_k,
+        grad_v,
         grad_o,
         grad_gate,
         grad_up,
         grad_down,
-        jnp.sum(gain_one_terms, axis=0),
-        jnp.sum(gain_two_terms, axis=0),
-        q_gain_sum,
-        k_gain_sum,
-    ]
-    totals = [new for new in new_terms]
-    reduced = (
-        lax.psum_scatter(totals[0], "dp", scatter_dimension=0, tiled=True),
-        lax.psum_scatter(totals[1], "dp", scatter_dimension=0, tiled=True),
-        lax.psum_scatter(totals[2], "dp", scatter_dimension=0, tiled=True),
-        lax.psum_scatter(totals[3], "dp", scatter_dimension=0, tiled=True),
-        lax.psum_scatter(totals[4], "dp", scatter_dimension=0, tiled=True),
-        lax.psum_scatter(totals[5], "dp", scatter_dimension=0, tiled=True),
-        lax.psum_scatter(totals[6], "dp", scatter_dimension=0, tiled=True),
-        lax.psum_scatter(totals[7], "dp", scatter_dimension=0, tiled=True),
-        lax.psum_scatter(totals[8], "dp", scatter_dimension=0, tiled=True),
-        lax.psum_scatter(totals[9], "dp", scatter_dimension=0, tiled=True),
-        lax.psum_scatter(totals[10], "dp", scatter_dimension=0, tiled=True),
-    )
-    return (jnp.stack(out_rows), jnp.stack(grad_rows)) + tuple(reduced)
+        *gain_outs,
+    )
 
 
 def solution(mesh):
     return jax.shard_map(
-        body,
+        functools.partial(body, mesh.shape["dp"]),
         mesh=mesh,
         in_specs=(
             P("dp", None, None),

time: 1940 us -> 646 us (0.33)
  waiting for transfers between devices: 1630 us -> 0 us
  Pallas kernels: 0 us -> 469 us
  matrix products: 149 us -> 78.8 us
  blocking collectives: 67.4 us -> 42.8 us
  other arithmetic: 29.2 us -> 9.03 us
    reduce_scatter x7 -> x0, waiting for transfers between devices: 1040 us -> none  [the longest x1 249 us: body(): lax.psum_scatter(totals[4], 'dp', scatter_dimension=0, tiled=True)]
    pallas_call x0 -> x4, Pallas kernels: none -> 469 us  [the longest x1 167 us: gather(): pl.pallas_call(functools.partial(gather_kernel, dp_size), out_shape=shape...]
    all_gather x7 -> x0, waiting for transfers between devices: 434 us -> none  [the longest x1 98.2 us: body(): full_gate = lax.all_gather(w_gate, 'dp', axis=0, tiled=True)]
    psum x3 -> x0, waiting for transfers between devices: 154 us -> none  [the longest x1 59 us: body(): attn_out = lax.psum(matmul(context_half, full_o.T), 'mp')]
    dot_general x21, matrix products: 140 us -> 73 us  [matmul(): return jnp.dot(left_op, right_op, preferred_element_type=jnp.float32)]
    unnamed x1 -> x0, blocking collectives: 61.9 us -> none
    psum x1, blocking collectives: 5.45 us -> 42.8 us  [body(): summed = lax.psum(jnp.concatenate(gains), ('dp', 'mp'))]
  transfers between devices with their start and end apart: 17 -> 0, of which waited for: 17 -> 0; matrix products, arithmetic and copies ran while one was open for 7% -> 0% of each run, Pallas kernels for 0% -> 0%
where the time goes in v1:
time: 646 us; the launch traced here: 638 us
  Pallas kernels  469 us (73%)
  matrix products  78.8 us (12%)
  blocking collectives  42.8 us (7%)
  local copies, waits for them, and re-layouts  36.2 us (6%)
  other arithmetic  9.03 us (1%)
    pallas_call x1, Pallas kernels, gather(): pl.pallas_call(functools.partial(gather_kernel, dp_size), out_shape=shape...  167 us
    pallas_call x1, Pallas kernels, ffn_reduce(): pl.pallas_call(functools.partial(ffn_reduce_kernel, dp_size), out_shape=[...  157 us
    pallas_call x1, Pallas kernels, attn_reduce(): pl.pallas_call(functools.partial(attn_reduce_kernel, dp_size), out_shape=...  81 us
    dot_general x21, matrix products, matmul(): return jnp.dot(left_op, right_op, preferred_element_type=jnp.float32)  73 us
    pallas_call x1, Pallas kernels, middle(): pl.pallas_call(functools.partial(middle_kernel, dp_size), out_shape=[jax....  64.4 us
    psum x1, blocking collectives, body(): summed = lax.psum(jnp.concatenate(gains), ('dp', 'mp'))  42.8 us
    unnamed x124, local copies, waits for them, and re-layouts  17.8 us

profile of v1, /device:TPU:0, one launch (start us, length us, event | category | flops | bytes accessed | tf_op | source)
XLA Modules:
  0.0 638.0 jit_solution(1902048679026818896)
XLA Ops:
  0.6 167.1 %shard_map.237 = (bf16[4,2,2,128,1024]{4,3,2,1,0:T(8,128)(2,1)}, bf16[4,2,2,128,512]{4,3,2,1,0:T(8,128)(2,1)}, bf16[4,2,2,128,512]{4,3,2,1,0:T(8,128)(2,1)}, bf1...) custom-call(bf16[128,1024]{1,0:T(8,128)(2,1)} %w_q.1, ...), custom_call_target="tpu_custom_call" | custom-call | tf_op jit(solution)/shard_map/pallas_call | solution.py:346
  167.8 3.0 copy.41
  171.2 0.8 multiply_reduce_fusion.6
  174.0 6.6 %copy.42 = bf16[1024,2048]{1,0:T(8,128)(2,1)} copy(bf16[1024,2048]{0,1:T(8,128)(2,1)} %bitcast.173) | data formatting | bytes 8388608 | tf_op jit(solution)/shard_map/dot_general | solution.py:17
  180.6 3.6 multiply_reduce_fusion.3
  185.6 1.0 copy.43
  186.6 1.0 copy.44
  187.7 2.0 fusion.29
  190.1 1.5 convolution_convert_fusion.10
  191.6 1.0 reshape.380
  193.1 3.7 fusion.31.partial
  196.8 64.4 %shard_map.238 = (f32[128,2048]{1,0:T(8,128)S(1)}, bf16[4,2,128,2048]{3,2,1,0:T(8,128)(2,1)S(1)}) custom-call(f32[256,2048]{1,0:T(8,128)S(1)} %fusion.31.partial, bf16[256,2048]{1,0:T(8,128)(2,1)S(1)} %bitcast.158, f32[1,2048]{1,0:T(1,128)S(1)} %bitcast.160), custom_call_target="tpu_custom_call" | custom-call | tf_op jit(solution)/shard_map/pallas_call | solution.py:411
  261.3 3.4 fusion.32
  264.8 3.4 fusion.30
  268.2 5.4 multiply_convert_fusion
  273.6 7.1 %convolution_convert_fusion.3 = bf16[2048,768]{1,0:T(8,128)(2,1)} fusion(bf16[1024,2048]{1,0:T(8,128)(2,1)S(1)} %bitcast.212, bf16[1024,768]{1,0:T(8,128)(2,1)} %get-tuple-element.61), kind=kOutput, calls=%fused_computation.4 | convolution fusion | flops 3222798336 | bytes 8912896 | tf_op jit(solution)/shard_map/dot_general | solution.py:17
  280.7 5.0 convolution_convert_fusion.4
  285.7 5.1 convolution_convert_fusion.5
  290.9 5.1 convolution_convert_fusion.2
  295.9 3.4 fusion.33
  299.4 5.3 add_convert_fusion
  304.7 156.8 %shard_map.239 = (f32[128,2048]{1,0:T(8,128)}, bf16[256,2048]{1,0:T(8,128)(2,1)}, bf16[256,2048]{1,0:T(8,128)(2,1)}, f32[1,2048]{1,0:T(1,128)}, f32[128,3072]{1,...) custom-call(bf16[4,2,128,2048]{3,2,1,0:T(8,128)(2,1)} %bitcast.180, bf16[4,2,128,2048]{3,2,1,0:T(8,128)(2,1)} %bitcast.179, ...), custom_call_target="tpu_custom_call" | custom-call | tf_op jit(solution)/shard_map/pallas_call | solution.py:572
  461.5 4.6 convolution_convert_fusion.9
  466.1 2.2 reshape.393
  468.3 2.4 bitcast_convert_fusion
  470.6 2.3 copy.64
  472.9 2.2 multiply_reduce_fusion
  475.0 2.2 copy.53
  477.3 1.7 fusion.6
  480.8 1.8 copy-done.13
  482.6 1.3 fusion.34
  484.0 0.8 convolution_bitcast_fusion.1
  485.3 1.1 copy-done.5
  486.4 0.8 convolution_add_fusion.1
  488.0 1.2 copy-done.18
  489.1 2.4 fusion.3
  491.5 42.8 %psum.7 = f32[4352]{0:T(1024)S(1)} all-reduce(f32[4352]{0:T(1024)S(1)} %pad_maximum_fusion.5), channel_id=1, replica_groups=mesh['dp'=16,'mp'=2] {'dp','mp'}, use_global_device_ids=true, to_apply=%region_12.13 | all-reduce | flops 4352 | bytes 34816 | tf_op jit(solution)/shard_map/psum | solution.py:797
  535.5 3.3 convolution_convert_fusion
  538.8 2.2 convolution_convert_fusion.6
  541.0 2.2 convolution_convert_fusion.7
  543.2 3.4 convolution_convert_fusion.1
  546.6 81.0 %shard_map.240 = (bf16[256,2048]{1,0:T(8,128)(2,1)}, f32[128,1024]{1,0:T(8,128)}, f32[128,512]{1,0:T(8,128)}, f32[128,512]{1,0:T(8,128)}, f32[128,1024]{1,0:T(8,128)}) custom-call(bf16[4,2,2,128,1024]{4,3,2,1,0:T(8,128)(2,1)} %bitcast.165, bf16[4,2,2,128,512]{4,3,2,1,0:T(8,128)(2,1)} %bitcast.170, bf16[4,2,2,128,512]{4,3,2,1,0:T(8,128)(2,1)} %bitcast.169, ...), custom_call_target="tpu_custom_call" | custom-call | tf_op jit(solution)/shard_map/pallas_call | solution.py:666
  627.7 1.0 copy.91
  629.3 1.0 copy.92
  633.3 1.1 copy.97
  634.4 1.1 copy.98
  635.6 0.8 copy-done.21
  636.4 1.1 copy.99
  (147 shorter events, 12.5 us)
Async XLA Ops:
  167.8 3.1 copy-start
  167.8 3.3 copy-start.32
  171.1 9.5 %copy-start.39 = (f32[256]{0:T(256)}, f32[256]{0:T(256)S(1)}, u32[]{:S(2)}) copy-start(f32[256]{0:T(256)S(1)} %add_rsqrt_fusion.2) | copy-start | bytes 3076
  171.1 1.7 copy-start.46
  171.1 1.8 copy-start.44
  172.7 8.0 %copy-start.37 = (f32[256,4]{0,1:T(4,128)}, f32[256,4]{0,1:T(4,128)S(1)}, u32[]{:S(2)}) copy-start(f32[256,4]{0,1:T(4,128)S(1)} %get-tuple-element.79) | copy-start | bytes 12292
  174.0 13.7 %copy-start.24 = (bf16[256,4,64]{0,2,1:T(8,128)(2,1)}, bf16[256,4,64]{0,2,1:T(8,128)(2,1)S(1)}, u32[]{:S(2)}) copy-start(bf16[256,4,64]{0,2,1:T(8,128)(2,1)S(1)} %get-tuple-element.70) | copy-start | bytes 393220
  174.0 13.7 %copy-start.26 = (bf16[256,4,64]{0,2,1:T(8,128)(2,1)}, bf16[256,4,64]{0,2,1:T(8,128)(2,1)S(1)}, u32[]{:S(2)}) copy-start(bf16[256,4,64]{0,2,1:T(8,128)(2,1)S(1)} %get-tuple-element.71) | copy-start | bytes 393220
  180.6 4.6 copy-start.48
  187.7 2.4 copy-start.17
  187.7 2.4 copy-start.40
  193.1 3.7 copy-start.6
  193.1 3.7 copy-start.2
  196.8 64.4 %copy-start.52 = (bf16[4,2,2,128,768]{4,3,2,1,0:T(8,128)(2,1)S(1)}, bf16[4,2,2,128,768]{4,3,2,1,0:T(8,128)(2,1)}, u32[]{:S(2)}) copy-start(bf16[4,2,2,128,768]{4,3,2,1,0:T(8,128)(2,1)} %get-tuple-element.43) | copy-start | bytes 9437188
  261.2 3.5 copy-start.1
  261.2 3.5 copy-start.50
  261.3 3.5 copy-start.53
  264.8 3.4 copy-start.51
  273.6 7.1 %copy-start.54 = (bf16[1024,768]{1,0:T(8,128)(2,1)}, bf16[1024,768]{1,0:T(8,128)(2,1)S(1)}, u32[]{:S(2)}) copy-start(bf16[1024,768]{1,0:T(8,128)(2,1)S(1)} %get-tuple-element.63) | copy-start | bytes 4718596
  285.7 5.1 copy-start.56
  295.9 3.5 copy-start.55
  477.3 1.7 copy-start.25
  477.3 1.7 copy-start.27
  479.0 1.2 copy-start.4
  479.0 1.2 copy-start.36
  479.0 1.2 copy-start.49
  480.2 2.4 copy-start.13
  480.8 3.1 copy-start.19
  482.6 1.3 copy-start.10
  482.6 1.3 copy-start.11
  484.8 1.6 copy-start.5
  487.4 1.7 copy-start.18
  487.5 1.7 copy-start.41
  488.0 3.6 copy-start.15
  489.1 2.4 copy-start.45
  489.1 46.4 %copy-start.7 = (bf16[4,128,2,256]{3,1,2,0:T(8,128)(2,1)S(1)}, bf16[4,128,2,256]{3,1,2,0:T(8,128)(2,1)}, u32[]{:S(2)}) copy-start(bf16[4,128,2,256]{3,1,2,0:T(8,128)(2,1)} %copy-done.6) | copy-start | bytes 1572868
  489.1 46.4 %copy-start.14 = (bf16[256,2048]{1,0:T(8,128)(2,1)S(1)}, bf16[256,2048]{1,0:T(8,128)(2,1)}, u32[]{:S(2)}) copy-start(bf16[256,2048]{1,0:T(8,128)(2,1)} %get-tuple-element.46) | copy-start | bytes 3145732
  535.5 3.3 copy-start.16
  541.0 2.2 copy-start.20
  546.6 81.1 %copy-start.28 = (bf16[256,2048]{1,0:T(8,128)(2,1)S(1)}, bf16[256,2048]{1,0:T(8,128)(2,1)}, u32[]{:S(2)}) copy-start(bf16[256,2048]{1,0:T(8,128)(2,1)} %get-tuple-element.45) | copy-start | bytes 3145732
  627.7 1.6 copy-start.29
  627.7 2.6 copy-start.31
  629.3 1.8 copy-start.34
  629.3 2.5 copy-start.33
  629.3 3.2 copy-start.30
  630.3 3.0 copy-start.23
  632.5 1.9 copy-start.22
  634.4 2.0 copy-start.21
  (9 other events, 9.0 us)

commit v2 on v1

v2 whole, which is shorter than its diff:
```python
import functools
import math

import jax
import jax.numpy as jnp
from jax import lax
from jax.experimental import pallas as pl
from jax.experimental.pallas import tpu as pltpu
from jax.sharding import PartitionSpec as P

EPSILON = 1e-06
ROPE_BASE = 1000000.0
MASKED = -1e30


def matmul(left_op, right_op):
    return jnp.dot(left_op, right_op, preferred_element_type=jnp.float32)


def rms_norm(values, gain_vec):
    inv_rms = lax.rsqrt(jnp.mean(values * values, axis=-1, keepdims=True) + EPSILON)
    return (values * inv_rms * gain_vec, inv_rms)


def norm_back(grad_norm, values, inv_rms, gain_vec):
    scaled = grad_norm * gain_vec
    cubed = inv_rms * inv_rms * inv_rms
    grad_values = inv_rms * scaled - values * cubed * jnp.mean(
        scaled * values, axis=-1, keepdims=True
    )
    return (grad_values, grad_norm * values * inv_rms)


MESH = pl.DeviceIdType.MESH
ANY = pl.BlockSpec(memory_space=pl.ANY)
VMEM = pl.BlockSpec(memory_space=pltpu.VMEM)
DEPTH = 4
CORES = 2
HALVES = 2


class Place:
    def __init__(self, dp_size):
        self.wide = dp_size // (DEPTH * CORES)
        here = lax.axis_index("dp")
        self.x = lax.axis_index("mp")
        self.z = lax.div(here, jnp.int32(self.wide * CORES))
        self.y = lax.rem(lax.div(here, jnp.int32(CORES)), jnp.int32(self.wide))
        self.c = lax.rem(here, jnp.int32(CORES))

    def device(self, z=None, y=None, c=None, x=None):
        z = self.z if z is None else z
        y = self.y if y is None else y
        c = self.c if c is None else c
        x = self.x if x is None else x
        return ((z * self.wide + y) * CORES + c, x)

    def z_off(self, step):
        return lax.rem(self.z + DEPTH + step, jnp.int32(DEPTH))

    def y_off(self, step):
        return lax.rem(self.y + self.wide + step, jnp.int32(self.wide))


def snake(z, side):
    odd = lax.rem(side, jnp.int32(2))
    return side * DEPTH + z + odd * (DEPTH - 1 - 2 * z)


def unsnake(index, size):
    index = lax.rem(index + 2 * size, jnp.int32(size))
    side = lax.div(index, jnp.int32(DEPTH))
    rest = lax.rem(index, jnp.int32(DEPTH))
    return rest + lax.rem(side, jnp.int32(2)) * (DEPTH - 1 - 2 * rest), side


class Mail:
    def __init__(self, send_sems, recv_sems):
        self.send_sems, self.recv_sems = send_sems, recv_sems
        self.count = 0
        self.open = []

    def send(self, source, target, device):
        copy = pltpu.make_async_remote_copy(
            source,
            target,
            self.send_sems.at[self.count],
            self.recv_sems.at[self.count],
            device_id=device,
            device_id_type=MESH,
        )
        self.count += 1
        copy.start()
        self.open.append(copy)
        return copy

    def finish(self):
        for copy in self.open:
            copy.wait_send()


def meet(devices):
    barrier = pltpu.get_barrier_semaphore()
    for device in devices:
        pl.semaphore_signal(barrier, inc=1, device_id=device, device_id_type=MESH)
    pl.semaphore_wait(barrier, len(devices))


def receive(copies):
    for copy in copies:
        copy.wait_recv()


def own_copies(pairs, sems):
    copies = [
        pltpu.make_async_copy(source, target, sems.at[i]) for i, (source, target) in enumerate(pairs)
    ]
    for copy in copies:
        copy.start()
    return copies


def dot_nt(left_op, right_op):
    return lax.dot_general(
        left_op, right_op, (((1,), (1,)), ((), ())), preferred_element_type=jnp.float32
    )


def dot_tn(left_op, right_op):
    return lax.dot_general(
        left_op, right_op, (((0,), (0,)), ((), ())), preferred_element_type=jnp.float32
    )


def turned(values):
    return pltpu.roll(values, values.shape[-1] // 2, axis=values.ndim - 1)


def document_tables(seg_col, seg_row, head_dim):
    seq_len = seg_col.shape[0]
    rows = lax.broadcasted_iota(jnp.int32, (seq_len, seq_len), 0)
    cols = lax.broadcasted_iota(jnp.int32, (seq_len, seq_len), 1)
    same = seg_col == seg_row
    bias = jnp.where(same & (cols <= rows), 0.0, MASKED)
    before = jnp.where(same & (cols < rows), 1.0, 0.0)
    position = jnp.sum(before, axis=-1, keepdims=True)
    lane = lax.broadcasted_iota(jnp.int32, (1, head_dim), 1)
    half_dim = head_dim // 2
    slot = jnp.where(lane < half_dim, lane, lane - half_dim).astype(jnp.float32)
    frequency = jnp.exp(slot * (-2.0 * math.log(ROPE_BASE) / head_dim))
    angles = position * frequency
    sine = jnp.sin(angles)
    return bias, jnp.cos(angles), jnp.where(lane < half_dim, -sine, sine)


def matmul_tiles(left, right, write, tile=256):
    @pl.loop(0, right.shape[1] // tile)
    def _(index):
        columns = pl.ds(pl.multiple_of(index * tile, tile), tile)
        write(columns, matmul(left[...], right[:, columns]))


def forward_kernel(
    dp_size, w_q, w_k, w_v, w_o, w_g, w_u, w_d, cot, row_in, seg_col, seg_row,
    gain_one, gain_two, q_gain, k_gain,
    o_q, o_k, o_v, o_o, o_g, o_u, o_d, o_c, o_n,
    mid, normed_one, query_raw, key_raw, values_half, queries, keys, context, log_total,
    cosine, sine, bias,
    f_q, f_k, f_v, f_o, outgoing, incoming, normed, own_sems, send_sems, recv_sems,
):
    at = Place(dp_size)
    z, y, c, x = at.z, at.y, at.c, at.x
    ring = DEPTH * at.wide
    loop = DEPTH * HALVES
    spot, seat = snake(z, y), snake(z, x)
    ring_z, ring_y = unsnake(spot + 1, ring)
    back_z, back_y = unsnake(spot - 1, ring)
    ahead, behind = at.device(z=ring_z, y=ring_y), at.device(z=back_z, y=back_y)
    loop_z, loop_x = unsnake(seat + 1, loop)
    tail_z, tail_x = unsnake(seat - 1, loop)
    after, before = at.device(z=loop_z, x=loop_x), at.device(z=tail_z, x=tail_x)
    sibling, other = at.device(c=1 - c), at.device(x=1 - x)
    z_peers = [at.device(z=at.z_off(k)) for k in range(1, DEPTH)]
    y_peers = [at.device(y=at.y_off(j)) for j in range(1, at.wide)]
    meet([ahead, behind, after, before, sibling, other] + z_peers + y_peers)

    mail = Mail(send_sems, recv_sems)
    rows = w_q.shape[0]
    head_dim = q_gain.shape[1]
    part = w_g.shape[1] // DEPTH
    tokens = mid.shape[0]
    strip = tokens // 2
    ffn = ((w_g, o_g), (w_u, o_u), (w_d, o_d))
    attn = ((w_q, f_q), (w_k, f_k), (w_v, f_v), (w_o, f_o))

    def block_rows(bz, by, bc):
        return pl.ds(pl.multiple_of(((bz * at.wide + by) * CORES + bc) * rows, rows), rows)

    def columns(index):
        return pl.ds(pl.multiple_of(index * part, part), part)

    here = block_rows(z, y, c)
    rounds = [
        mail.send(weight, out.at[here], ahead if i < 2 else behind)
        for i, (weight, out) in enumerate(attn)
    ]
    attn_sibling = [mail.send(weight, out.at[here], sibling) for weight, out in attn]
    to_sibling = []
    mine = own_copies([(weight, out.at[here]) for weight, out in attn], own_sems)
    own_ffn = [
        pltpu.make_async_copy(weight.at[:, columns(z)], out.at[here], own_sems.at[4 + i])
        for i, (weight, out) in enumerate(ffn)
    ]
    own_ffn.append(
        pltpu.make_async_copy(
            cot.at[pl.ds(pl.multiple_of(x * tokens, tokens), tokens)], o_c.at[z, x], own_sems.at[7]
        )
    )
    for copy in own_ffn:
        copy.start()

    residual = row_in[...].astype(jnp.float32)
    normed_full, _ = rms_norm(residual, gain_one[...])
    normed_one[...] = normed_full.astype(jnp.bfloat16)
    bias_values, cosine[...], sine[...] = document_tables(seg_col[...], seg_row[...], head_dim)
    bias[...] = bias_values

    spread, crossing, state = {}, {}, {}

    def start_spread():
        for k in range(1, DEPTH):
            target = at.z_off(k)
            spread[k] = [
                mail.send(weight.at[:, columns(target)], out.at[here], z_peers[k - 1])
                for weight, out in ffn
            ]
        for j in range(1, at.wide):
            crossing[0, j] = [
                mail.send(weight.at[:, columns(z)], out.at[here], y_peers[j - 1])
                for weight, out in ffn
            ]
        to_sibling.extend(
            mail.send(weight.at[:, columns(z)], out.at[here], sibling) for weight, out in ffn
        )

    def start_turns(name, first, second, out):
        state[name] = [
            mail.send(first, out.at[z, x, pl.ds(0, strip)], after),
            mail.send(second, out.at[z, x, pl.ds(strip, strip)], before),
        ]

    def turn(name, out, step):
        receive(state[name])
        one_z, one_x = unsnake(seat - 1 - step, loop)
        two_z, two_x = unsnake(seat + 1 + step, loop)
        if step < loop - 2:
            first = out.at[one_z, one_x, pl.ds(0, strip)]
            second = out.at[two_z, two_x, pl.ds(strip, strip)]
            state[name] = [mail.send(first, first, after), mail.send(second, second, before)]

    def forward_spread(k):
        receive(spread[k])
        source = block_rows(at.z_off(-k), y, c)
        blocks = [out.at[source] for _, out in ffn]
        for j in range(1, at.wide):
            crossing[k, j] = [mail.send(block, block, y_peers[j - 1]) for block in blocks]
        to_sibling.extend(mail.send(block, block, sibling) for block in blocks)

    def forward_crossing(k):
        for j in range(1, at.wide):
            receive(crossing[k, j])
            source = block_rows(at.z_off(-k), at.y_off(-j), c)
            blocks = [out.at[source] for _, out in ffn]
            to_sibling.extend(mail.send(block, block, sibling) for block in blocks)

    for step in range(ring - 1):
        receive(rounds)
        one_z, one_y = unsnake(spot - 1 - step, ring)
        two_z, two_y = unsnake(spot + 1 + step, ring)
        places = [block_rows(one_z, one_y, c)] * 2 + [block_rows(two_z, two_y, c)] * 2
        blocks = [out.at[place] for (_, out), place in zip(attn, places)]
        if step < ring - 2:
            rounds = [
                mail.send(block, block, ahead if i < 2 else behind)
                for i, block in enumerate(blocks)
            ]
        attn_sibling += [mail.send(block, block, sibling) for block in blocks]
        if step == ring - 4:
            start_spread()
    cot_start = pl.multiple_of(x * tokens, tokens)
    start_turns(
        "cot", cot.at[pl.ds(cot_start, strip)], cot.at[pl.ds(cot_start + strip, strip)], o_c
    )
    for copy in mine:
        copy.wait()
    receive(attn_sibling)
    saved = [
        pltpu.make_async_copy(full, out, own_sems.at[i])
        for i, (full, out) in enumerate(((f_q, o_q), (f_k, o_k), (f_v, o_v), (f_o, o_o)))
    ]
    for copy in saved:
        copy.start()

    def write_query(cols, block):
        query_raw[:, cols] = block

    def write_key(cols, block):
        key_raw[:, cols] = block

    def write_value(cols, block):
        values_half[:, cols] = block.astype(jnp.bfloat16)

    matmul_tiles(normed_one, f_q, write_query)
    matmul_tiles(normed_one, f_k, write_key)
    matmul_tiles(normed_one, f_v, write_value)
    turn("cot", o_c, 0)

    def rotated(raw, gain):
        unit, _ = rms_norm(raw, gain)
        return (unit * cosine[...] + turned(unit) * sine[...]).astype(jnp.bfloat16)

    kv_heads = key_raw.shape[1] // head_dim
    group = query_raw.shape[1] // key_raw.shape[1]
    for j in range(kv_heads):
        kv_cols = pl.ds(j * head_dim, head_dim)
        keys[:, kv_cols] = rotated(key_raw[:, kv_cols], k_gain[...])
        for g in range(group):
            head = j * group + g
            cols = pl.ds(head * head_dim, head_dim)
            queries[:, cols] = rotated(query_raw[:, cols], q_gain[...])
            scores = dot_nt(queries[:, cols], keys[:, kv_cols]) * (1.0 / math.sqrt(head_dim))
            scores = scores + bias[...]
            row_max = jnp.max(scores, axis=-1, keepdims=True)
            weights = jnp.exp(scores - row_max)
            total = jnp.sum(weights, axis=-1, keepdims=True)
            log_total[:, head : head + 1] = row_max + jnp.log(total)
            probs = (weights * (1.0 / total)).astype(jnp.bfloat16)
            context[:, cols] = matmul(probs, values_half[:, kv_cols]).astype(jnp.bfloat16)
        if j == kv_heads // 2 - 1:
            turn("cot", o_c, 1)

    given = pl.ds(pl.multiple_of((1 - x) * tokens, tokens), tokens)
    kept = pl.ds(pl.multiple_of(x * tokens, tokens), tokens)
    width = row_in.shape[1]
    tile = 256

    def project(token_rows, target):
        @pl.loop(0, width // tile)
        def _(index):
            cols = pl.ds(pl.multiple_of(index * tile, tile), tile)
            block = dot_nt(context[token_rows, :], f_o[cols, :])
            target[:, cols] = block.astype(target.dtype)

    project(given, outgoing)
    swap = mail.send(outgoing, incoming, other)
    project(kept, mid)
    turn("cot", o_c, 2)
    forward_spread(1)
    forward_spread(2)
    swap.wait_recv()
    total = row_in[kept, :].astype(jnp.float32) + (mid[...] + incoming[...].astype(jnp.float32))
    mid[...] = total
    normed_mid, _ = rms_norm(total, gain_two[...])
    normed[...] = normed_mid.astype(jnp.bfloat16)
    last = pltpu.make_async_copy(normed, o_n.at[z, x], own_sems.at[8])
    last.start()
    start_turns("mid", normed.at[pl.ds(0, strip)], normed.at[pl.ds(strip, strip)], o_n)
    forward_spread(3)
    for step in range(loop - 1):
        turn("mid", o_n, step)
        if step + 3 < loop - 1:
            turn("cot", o_c, step + 3)
        if step < DEPTH:
            forward_crossing(step)
    receive(to_sibling)
    mail.finish()
    for copy in own_ffn + saved + [last]:
        copy.wait()


def forward(dp_size, weights, cot, row_in, seg_row, gains):
    w_q, w_k, w_v, w_o, w_g, w_u, w_d = weights
    wide = dp_size // (DEPTH * CORES)
    seq_len, width = row_in.shape
    head_dim = gains[2].shape[1]
    tokens = seq_len // HALVES
    part = w_g.shape[1] // DEPTH
    ring, loop = DEPTH * wide, DEPTH * HALVES
    half, full = jnp.bfloat16, jnp.float32
    attn_cols = [w.shape[1] for w in (w_q, w_k, w_v, w_o)]
    shapes = [jax.ShapeDtypeStruct((width, cols), half) for cols in attn_cols]
    shapes += [jax.ShapeDtypeStruct((width, part), half)] * 3
    shapes += [jax.ShapeDtypeStruct((DEPTH, HALVES, tokens, width), half)] * 2
    q_cols, kv_cols = attn_cols[0], attn_cols[1]
    for cols, kind in (
        (width, half), (q_cols, full), (kv_cols, full), (kv_cols, half), (q_cols, half),
        (kv_cols, half), (q_cols, half), (head_dim, full), (head_dim, full), (head_dim, full),
        (seq_len, full),
    ):
        shapes.append(jax.ShapeDtypeStruct((seq_len, cols), kind))
    shapes.insert(9, jax.ShapeDtypeStruct((tokens, width), full))
    copies = 4 * (ring - 1) + 4 * (loop - 1) + 1 + 9 + 3 * DEPTH * (wide - 1) + 4 * ring + 3 * ring
    return pl.pallas_call(
        functools.partial(forward_kernel, dp_size),
        out_shape=shapes,
        in_specs=[ANY] * 8 + [VMEM] * 7,
        out_specs=[ANY] * 9 + [VMEM] * 12,
        scratch_shapes=[pltpu.VMEM((width, cols), half) for cols in attn_cols]
        + [pltpu.VMEM((tokens, width), half)] * 3
        + [
            pltpu.SemaphoreType.DMA((9,)),
            pltpu.SemaphoreType.DMA((copies,)),
            pltpu.SemaphoreType.DMA((copies,)),
        ],
        compiler_params=pltpu.CompilerParams(
            collective_id=0, has_side_effects=True, vmem_limit_bytes=56 * 2**20
        ),
    )(w_q, w_k, w_v, w_o, w_g, w_u, w_d, cot, row_in, seg_row[:, None], seg_row[None, :], *gains)


def add_into(target, *others):
    total = target[...].astype(jnp.float32)
    for other in others:
        total = total + other[...].astype(jnp.float32)
    target[...] = total.astype(target.dtype)


def backward_kernel(
    dp_size, p_n, p_o, g_g, g_u, g_d, w_q, w_k, w_v, w_o,
    mid, cot, gain_two, row_in, normed_one, query_raw, key_raw, values_half, queries, keys,
    context, log_total, cosine, sine, bias, q_gain, k_gain,
    a_q, a_k, a_v, a_o,
    o_m, o_l, o_t, o_s, o_x, o_y, o_p, d_g, d_u, d_d,
    r_n, r_o, c_g, c_u, c_d, s_g, s_u, s_d, y_g, y_u, y_d, z_g, z_u, z_d,
    f_q, f_k, f_v, f_o, mid_half, context_grad, query_grad, key_grad, value_grad, flipped,
    own_sems, send_sems, recv_sems,
):
    at = Place(dp_size)
    z, y, c, x = at.z, at.y, at.c, at.x
    loop = DEPTH * HALVES
    seat = snake(z, x)
    loop_z, loop_x = unsnake(seat + 1, loop)
    tail_z, tail_x = unsnake(seat - 1, loop)
    after, before = at.device(z=loop_z, x=loop_x), at.device(z=tail_z, x=tail_x)
    other = at.device(x=1 - x)
    sibling = at.device(c=1 - c)
    z_peers = [at.device(z=at.z_off(k)) for k in range(1, DEPTH)]
    y_peers = [at.device(y=at.y_off(j)) for j in range(1, at.wide)]
    grads = (
        (g_g, c_g, s_g, y_g, z_g, d_g),
        (g_u, c_u, s_u, y_u, z_u, d_u),
        (g_d, c_d, s_d, y_d, z_d, d_d),
    )
    own_parts = [
        pltpu.make_async_copy(grad.at[:, :, c], own, own_sems.at[4 + i])
        for i, (grad, _, own, *_) in enumerate(grads)
    ]
    loads = [
        pltpu.make_async_copy(weight, full, own_sems.at[i])
        for i, (weight, full) in enumerate(((w_q, f_q), (w_k, f_k), (w_v, f_v), (w_o, f_o)))
    ]
    for copy in own_parts + loads:
        copy.start()
    meet([after, before, other, sibling] + z_peers + y_peers)
    mail = Mail(send_sems, recv_sems)
    tokens = mid.shape[0]
    strip = tokens // 2
    part = d_g.shape[1] // DEPTH
    strips = (pl.ds(0, strip), pl.ds(strip, strip))
    kept = pl.multiple_of(x * tokens, tokens)
    state = {}

    def block(array, i, step):
        shift = -1 - step if i == 0 else 1 + step
        bz, bx = unsnake(seat + shift, loop)
        return array.at[bz, bx, strips[i]]

    def ring_start(name, array, landing):
        state[name] = [
            mail.send(block(array, i, 0), landing.at[0, i], after if i == 0 else before)
            for i in range(2)
        ]

    def ring_step(name, array, landing, step):
        receive(state[name])
        turns = []
        for i in range(2):
            add_into(landing.at[step, i], block(array, i, step + 1))
            turns.append(
                mail.send(landing.at[step, i], landing.at[step + 1, i], after if i == 0 else before)
            )
        state[name] = turns

    ring_start("norm", p_n, r_n)
    order = [(k, at.z_off(k)) for k in (2, 1, 3, 0)]
    to_core = {
        k: [mail.send(grad.at[to, :, 1 - c], land.at[to], sibling) for grad, land, *_ in grads]
        for k, to in order
    }
    to_y, to_z = {}, {}

    def core_stage(k, to):
        receive(to_core[k])
        for _, land, own, *_ in grads:
            add_into(own.at[to], land.at[to])
        to_y[k] = [
            mail.send(own.at[to, at.y_off(j)], arrive.at[j - 1, to], y_peers[j - 1])
            for j in range(1, at.wide)
            for _, _, own, arrive, *_ in grads
        ]

    def y_stage(k, to):
        receive(to_y[k])
        for _, _, own, arrive, *_ in grads:
            add_into(own.at[to, y], *[arrive.at[j - 1, to] for j in range(1, at.wide)])
        if k > 0:
            to_z[k] = [
                mail.send(own.at[to, y], last.at[k - 1], z_peers[k - 1])
                for _, _, own, _, last, _ in grads
            ]

    for step in range(loop - 2):
        ring_step("norm", p_n, r_n, step)
        if step == 0:
            for copy in own_parts:
                copy.wait()
        if step < DEPTH:
            core_stage(*order[step])
        if step == loop - 3:
            y_stage(*order[0])
    receive(state["norm"])
    gain_sum = jnp.zeros(o_t.shape, jnp.float32)
    for i in range(2):
        grad_norm = r_n[loop - 2, i].astype(jnp.float32) + p_n[z, x, strips[i]].astype(jnp.float32)
        values = mid[strips[i], :]
        inv_rms = lax.rsqrt(jnp.mean(values * values, axis=-1, keepdims=True) + EPSILON)
        grad_values, terms = norm_back(grad_norm, values, inv_rms, gain_two[...])
        gain_sum = gain_sum + jnp.sum(terms, axis=0, keepdims=True)
        rows = pl.ds(pl.multiple_of(kept + i * strip, strip), strip)
        total = cot[rows, :].astype(jnp.float32) + grad_values
        o_m[strips[i], :] = total
        mid_half[rows, :] = total.astype(jnp.bfloat16)
    o_t[...] = gain_sum
    kept_rows = pl.ds(kept, tokens)
    swap_h = mail.send(mid_half.at[kept_rows], mid_half.at[kept_rows], other)
    ring_start("out", p_o, r_o)
    y_stage(*order[1])
    y_stage(*order[2])
    flipped[...] = normed_one[...].T
    for copy in loads:
        copy.wait()
    swap_h.wait_recv()

    def write_context(cols, value):
        context_grad[:, cols] = value.astype(jnp.bfloat16)

    matmul_tiles(mid_half, f_o, write_context)
    ring_step("out", p_o, r_o, 0)

    width = row_in.shape[1]
    tile = 256

    @pl.loop(0, width // tile)
    def _(index):
        rows = pl.ds(pl.multiple_of(index * tile, tile), tile)
        f_o[rows, :] = dot_tn(mid_half[:, rows], context[...]).astype(jnp.bfloat16)

    store_o = pltpu.make_async_copy(f_o, a_o, own_sems.at[3])
    store_o.start()
    y_stage(*order[3])

    head_dim = q_gain.shape[1]
    kv_heads = key_raw.shape[1] // head_dim
    group = query_raw.shape[1] // key_raw.shape[1]
    scale = 1.0 / math.sqrt(head_dim)

    def raw_grad(grad, raw, gain):
        back = grad * cosine[...] - turned(grad) * sine[...]
        inv_rms = lax.rsqrt(jnp.mean(raw * raw, axis=-1, keepdims=True) + EPSILON)
        grad_raw, terms = norm_back(back, raw, inv_rms, gain)
        return grad_raw.astype(jnp.bfloat16), jnp.sum(terms, axis=0, keepdims=True)

    q_sum = jnp.zeros(o_x.shape, jnp.float32)
    k_sum = jnp.zeros(o_y.shape, jnp.float32)
    for j in range(kv_heads):
        kv_cols = pl.ds(j * head_dim, head_dim)
        key_total = jnp.zeros((row_in.shape[0], head_dim), jnp.float32)
        value_total = jnp.zeros((row_in.shape[0], head_dim), jnp.float32)
        for g in range(group):
            head = j * group + g
            cols = pl.ds(head * head_dim, head_dim)
            scores = dot_nt(queries[:, cols], keys[:, kv_cols]) * scale + bias[...]
            probs = jnp.exp(scores - log_total[:, head : head + 1])
            grad_context = context_grad[:, cols]
            grad_probs = dot_nt(grad_context, values_half[:, kv_cols])
            delta = jnp.sum(
                grad_context.astype(jnp.float32) * context[:, cols].astype(jnp.float32),
                axis=-1,
                keepdims=True,
            )
            grad_scores = (probs * (grad_probs - delta) * scale).astype(jnp.bfloat16)
            grad_query, terms = raw_grad(
                matmul(grad_scores, keys[:, kv_cols]), query_raw[:, cols], q_gain[...]
            )
            query_grad[:, cols] = grad_query
            q_sum = q_sum + terms
            key_total = key_total + dot_tn(grad_scores, queries[:, cols])
            value_total = value_total + dot_tn(probs.astype(jnp.bfloat16), grad_context)
        grad_key, terms = raw_grad(key_total, key_raw[:, kv_cols], k_gain[...])
        key_grad[:, kv_cols] = grad_key
        k_sum = k_sum + terms
        value_grad[:, kv_cols] = value_total.astype(jnp.bfloat16)
        if j % 2 == 1:
            ring_step("out", p_o, r_o, 1 + j // 2)
    o_x[...] = q_sum
    o_y[...] = k_sum

    @pl.loop(0, width // tile)
    def _(index):
        rows = pl.ds(pl.multiple_of(index * tile, tile), tile)
        total = dot_nt(query_grad[...], f_q[rows, :])
        total = total + dot_nt(key_grad[...], f_k[rows, :])
        o_p[:, rows] = total + dot_nt(value_grad[...], f_v[rows, :])

    ring_step("out", p_o, r_o, 3)
    values = row_in[...].astype(jnp.float32)
    inv_rms = lax.rsqrt(jnp.mean(values * values, axis=-1, keepdims=True) + EPSILON)
    o_s[...] = jnp.sum(o_p[...] * values * inv_rms, axis=0, keepdims=True)

    @pl.loop(0, width // tile)
    def _(index):
        rows = pl.ds(pl.multiple_of(index * tile, tile), tile)
        lhs = flipped[rows, :]
        f_q[rows, :] = matmul(lhs, query_grad[...]).astype(jnp.bfloat16)
        f_k[rows, :] = matmul(lhs, key_grad[...]).astype(jnp.bfloat16)
        f_v[rows, :] = matmul(lhs, value_grad[...]).astype(jnp.bfloat16)

    stores = [
        pltpu.make_async_copy(full, out, own_sems.at[i])
        for i, (full, out) in enumerate(((f_q, a_q), (f_k, a_k), (f_v, a_v)))
    ]
    for copy in stores:
        copy.start()
    for step in range(4, loop - 2):
        ring_step("out", p_o, r_o, step)
    for _, _, own, _, _, out in grads:
        out[:, pl.ds(pl.multiple_of(z * part, part), part)] = own[z, y].astype(jnp.float32)
    for k in range(1, DEPTH):
        receive(to_z[k])
        columns = pl.ds(pl.multiple_of(at.z_off(-k) * part, part), part)
        for _, _, _, _, last, out in grads:
            out[:, columns] = last[k - 1].astype(jnp.float32)
    receive(state["out"])
    for i in range(2):
        rows = pl.ds(pl.multiple_of(kept + i * strip, strip), strip)
        total = r_o[loop - 2, i].astype(jnp.float32) + p_o[z, x, strips[i]].astype(jnp.float32)
        o_l[rows, :] = (mid[strips[i], :] + total).astype(jnp.bfloat16)
    swap_l = mail.send(o_l.at[kept_rows], o_l.at[kept_rows], other)
    swap_l.wait_recv()
    mail.finish()
    for copy in stores + [store_o]:
        copy.wait()


def backward(dp_size, parts, grads, weights, mid, cot, gain_two, saved, gains):
    wide = dp_size // (DEPTH * CORES)
    tokens, width = mid.shape
    seq_len = HALVES * tokens
    loop = DEPTH * HALVES
    rows, part = grads[0].shape[-2:]
    half, full = jnp.bfloat16, jnp.float32
    attn_cols = [w.shape[1] for w in weights]
    head_dim = gains[0].shape[1]
    copies = 4 * (loop - 1) + 3 * DEPTH + 3 * DEPTH * (wide - 1) + 9 + 2
    shapes = [jax.ShapeDtypeStruct((width, cols), half) for cols in attn_cols]
    shapes += [
        jax.ShapeDtypeStruct((tokens, width), full),
        jax.ShapeDtypeStruct((seq_len, width), half),
        jax.ShapeDtypeStruct((1, width), full),
        jax.ShapeDtypeStruct((1, width), full),
        jax.ShapeDtypeStruct((1, head_dim), full),
        jax.ShapeDtypeStruct((1, head_dim), full),
        jax.ShapeDtypeStruct((seq_len, width), full),
    ]
    shapes += [jax.ShapeDtypeStruct((rows, part * DEPTH), full)] * 3
    return pl.pallas_call(
        functools.partial(backward_kernel, dp_size),
        out_shape=shapes,
        in_specs=[VMEM] * 2 + [ANY] * 7 + [VMEM] * (3 + len(saved) + 2),
        out_specs=[ANY] * 4 + [VMEM] * 10,
        scratch_shapes=[pltpu.VMEM((loop - 1, 2, tokens // 2, width), half)] * 2
        + [pltpu.VMEM((DEPTH, wide, rows, part), half)] * 6
        + [pltpu.VMEM((wide - 1, DEPTH, rows, part), half)] * 3
        + [pltpu.VMEM((DEPTH - 1, rows, part), half)] * 3
        + [pltpu.VMEM((width, cols), half) for cols in attn_cols]
        + [pltpu.VMEM((seq_len, width), half)]
        + [pltpu.VMEM((seq_len, cols), half) for cols in (attn_cols[0],) + tuple(attn_cols[:3])]
        + [pltpu.VMEM((width, seq_len), half)]
        + [
            pltpu.SemaphoreType.DMA((7,)),
            pltpu.SemaphoreType.DMA((copies,)),
            pltpu.SemaphoreType.DMA((copies,)),
        ],
        compiler_params=pltpu.CompilerParams(
            collective_id=1, has_side_effects=True, vmem_limit_bytes=63 * 2**20
        ),
    )(*parts, *grads, *weights, mid, cot, gain_two, *saved, *gains)


def attn_reduce_kernel(
    dp_size, g_q, g_k, g_v, g_o, partial, row_in, grad_mid, gain, t_a, t_m, t_q, t_k,
    o_i, sums, w_q, w_k, w_v, w_o,
    gathering, arriving, outgoing, incoming, c_q, c_k, c_v, c_o, r_q, r_k, r_v, r_o, send_sems, recv_sems,
):
    at = Place(dp_size)
    z, y, c, x = at.z, at.y, at.c, at.x
    ring = DEPTH * at.wide
    spot = snake(z, y)
    ring_z, ring_y = unsnake(spot + 1, ring)
    back_z, back_y = unsnake(spot - 1, ring)
    ahead, behind = at.device(z=ring_z, y=ring_y), at.device(z=back_z, y=back_y)
    other = at.device(x=1 - x)
    sibling = at.device(c=1 - c)
    tokens = grad_mid.shape[0]
    kept = pl.ds(pl.multiple_of(x * tokens, tokens), tokens)
    given = pl.ds(pl.multiple_of((1 - x) * tokens, tokens), tokens)
    outgoing[...] = partial[given, :].astype(jnp.bfloat16)
    head_dim = t_q.shape[1]
    gathering[...] = jnp.zeros(gathering.shape, jnp.float32)
    for i, term in enumerate((t_a, t_m)):
        gathering[0, i : i + 1, :] = term[...]
    for i, term in enumerate((t_q, t_k)):
        gathering[0, i + 2 : i + 3, :head_dim] = term[...]
    pairs = pair_devices(at)
    meet([ahead, behind, other, sibling] + pairs)
    mail = Mail(send_sems, recv_sems)
    sets = ((g_q, c_q, r_q, w_q), (g_k, c_k, r_k, w_k), (g_v, c_v, r_v, w_v), (g_o, c_o, r_o, w_o))

    def spot_of(i, step):
        return unsnake(spot + (-1 - step if i < 2 else 1 + step), ring)

    to_core = []
    for step in range(ring):
        row = []
        for i, (grad, land, _, _) in enumerate(sets):
            bz, by = spot_of(i, step)
            row.append(mail.send(grad.at[bz, by, 1 - c], land.at[bz, by], sibling))
        to_core.append(row)
    swap = mail.send(outgoing, incoming, other)
    exchange = mail.send(gathering.at[0], arriving.at[0], pairs[0])
    turns = []
    for step in range(ring):
        receive(to_core[step])
        if step > 0:
            receive(turns)
        turns = []
        for i, (grad, land, arrive, out) in enumerate(sets):
            bz, by = spot_of(i, step)
            terms = [grad[bz, by, c].astype(jnp.float32), land[bz, by].astype(jnp.float32)]
            if step > 0:
                terms.append(arrive[step - 1].astype(jnp.float32))
            total = sum(terms[1:], terms[0])
            if step < ring - 1:
                land[bz, by] = total.astype(jnp.bfloat16)
                turns.append(
                    mail.send(land.at[bz, by], arrive.at[step], ahead if i < 2 else behind)
                )
            else:
                out[...] = total
        if 1 <= step <= len(pairs):
            exchange.wait_recv()
            total = gathering[step - 1] + arriving[step - 1]
            if step < len(pairs):
                gathering[step] = total
                exchange = mail.send(gathering.at[step], arriving.at[step], pairs[step])
            else:
                sums[...] = total
        if step == 1:
            swap.wait_recv()
            grad_norm = partial[kept, :] + incoming[...].astype(jnp.float32)
            values = row_in[kept, :].astype(jnp.float32)
            inv_rms = lax.rsqrt(jnp.mean(values * values, axis=-1, keepdims=True) + EPSILON)
            grad_values, _ = norm_back(grad_norm, values, inv_rms, gain[...])
            o_i[kept, :] = (grad_mid[...] + grad_values).astype(jnp.bfloat16)
            swap_back = mail.send(o_i.at[kept], o_i.at[kept], other)
    swap_back.wait_recv()
    mail.finish()


def pair_devices(at):
    def flip(index, bit):
        return index + bit - 2 * bit * lax.rem(lax.div(index, jnp.int32(bit)), jnp.int32(2))

    bits = [1 << i for i in range(at.wide.bit_length() - 1)]
    return (
        [at.device(c=1 - at.c), at.device(x=1 - at.x)]
        + [at.device(y=flip(at.y, bit)) for bit in bits]
        + [at.device(z=flip(at.z, bit)) for bit in (1, 2)]
    )


def attn_reduce(dp_size, grads, partial, row_in, grad_mid, gain, terms):
    wide = dp_size // (DEPTH * CORES)
    ring = DEPTH * wide
    tokens, width = grad_mid.shape
    half = jnp.bfloat16
    rows = grads[0].shape[-2]
    cols = [grad.shape[-1] for grad in grads]
    pairs = 4 + wide.bit_length() - 1
    copies = 4 * ring + 4 * (ring - 1) + 2 + pairs
    return pl.pallas_call(
        functools.partial(attn_reduce_kernel, dp_size),
        out_shape=[
            jax.ShapeDtypeStruct((HALVES * tokens, width), half),
            jax.ShapeDtypeStruct((8, width), jnp.float32),
        ]
        + [jax.ShapeDtypeStruct((rows, col), jnp.float32) for col in cols],
        in_specs=[VMEM] * 12,
        out_specs=[VMEM] * 6,
        scratch_shapes=[pltpu.VMEM((pairs, 8, width), jnp.float32)] * 2
        + [pltpu.VMEM((tokens, width), half)] * 2
        + [pltpu.VMEM((DEPTH, wide, rows, col), half) for col in cols]
        + [pltpu.VMEM((ring - 1, rows, col), half) for col in cols]
        + [pltpu.SemaphoreType.DMA((copies,)), pltpu.SemaphoreType.DMA((copies,))],
        compiler_params=pltpu.CompilerParams(
            collective_id=2, has_side_effects=True, vmem_limit_bytes=58 * 2**20
        ),
    )(*grads, partial, row_in, grad_mid, gain, *terms)


def body(
    dp_size,
    layer_in,
    seg_ids,
    w_q,
    w_k,
    w_v,
    w_o,
    w_gate,
    w_up,
    w_down,
    attn_gain,
    mlp_gain,
    q_gain,
    k_gain,
    cotangent,
):
    rows = w_q.shape[0]
    width = rows * dp_size
    wide = dp_size // (DEPTH * CORES)
    row_in = layer_in[0]
    row_cot = cotangent[0]
    seq_len = row_in.shape[0]
    gains = [gain[None, :] for gain in (attn_gain, mlp_gain, q_gain, k_gain)]
    outs = forward(
        dp_size, (w_q, w_k, w_v, w_o, w_gate, w_up, w_down), row_cot, row_in, seg_ids[0], gains
    )
    attn_full, (part_gate, part_up, part_down), (cots, normed_two), mid = (
        outs[:4], outs[4:7], outs[7:9], outs[9],
    )
    saved = outs[10:]
    cots, normed_two = cots.reshape(-1, width), normed_two.reshape(-1, width)

    gate_pre = matmul(normed_two, part_gate)
    up_pre = matmul(normed_two, part_up)
    sigmoid_gate = jax.nn.sigmoid(gate_pre)
    silu_val = gate_pre * sigmoid_gate
    act_half = (silu_val * up_pre).astype(jnp.bfloat16)
    out_part = matmul(act_half, part_down.T).astype(jnp.bfloat16)
    grad_act = matmul(cots, part_down)
    grad_gate_pre = (
        grad_act * up_pre * sigmoid_gate * (1.0 + gate_pre * (1.0 - sigmoid_gate))
    ).astype(jnp.bfloat16)
    grad_up_pre = (grad_act * silu_val).astype(jnp.bfloat16)
    norm_part = (
        matmul(grad_gate_pre, part_gate.T) + matmul(grad_up_pre, part_up.T)
    ).astype(jnp.bfloat16)
    grads = [
        matmul(left.T, right).astype(jnp.bfloat16).reshape(DEPTH, wide, CORES, rows, -1)
        for left, right in (
            (normed_two, grad_gate_pre),
            (normed_two, grad_up_pre),
            (cots, act_half),
        )
    ]
    shape = (DEPTH, HALVES, seq_len // HALVES, width)
    parts = (norm_part.reshape(shape), out_part.reshape(shape))
    outs = backward(
        dp_size, parts, grads, attn_full, mid, row_cot, gains[1], [row_in] + list(saved), gains[2:]
    )
    attn_grads = [grad.reshape(DEPTH, wide, CORES, rows, -1) for grad in outs[:4]]
    grad_mid, out_row, gain_two, gain_one, q_sum, k_sum, normed_part = outs[4:11]
    grad_gate, grad_up, grad_down = outs[11:]
    in_grad, sums, grad_q, grad_k, grad_v, grad_o = attn_reduce(
        dp_size, attn_grads, normed_part, row_in, grad_mid, gains[0],
        (gain_one, gain_two, q_sum, k_sum),
    )
    gain_outs = []
    for i, size in enumerate((width, width, q_gain.shape[0], k_gain.shape[0])):
        share = size // dp_size
        gain_outs.append(lax.dynamic_slice(sums[i], (lax.axis_index("dp") * share,), (share,)))
    return (
        out_row[None],
        in_grad[None],
        grad_q,
        grad_k,
        grad_v,
        grad_o,
        grad_gate,
        grad_up,
        grad_down,
        *gain_outs,
    )


def solution(mesh):
    return jax.shard_map(
        functools.partial(body, mesh.shape["dp"]),
        mesh=mesh,
        in_specs=(
            P("dp", None, None),
            P("dp", None),
            P("dp", "mp"),
            P("dp", "mp"),
            P("dp", "mp"),
            P("dp", "mp"),
            P("dp", "mp"),
            P("dp", "mp"),
            P("dp", "mp"),
            P(),
            P(),
            P(),
            P(),
            P("dp", None, None),
        ),
        out_specs=(
            P("dp", None, None),
            P("dp", None, None),
            P("dp", "mp"),
            P("dp", "mp"),
            P("dp", "mp"),
            P("dp", "mp"),
            P("dp", "mp"),
            P("dp", "mp"),
            P("dp", "mp"),
            P("dp"),
            P("dp"),
            P("dp"),
            P("dp"),
        ),
        check_vma=False,
    )
```

time: 646 us -> 540 us (0.84)
  blocking collectives: 42.8 us -> 0 us
  matrix products: 78.8 us -> 43.1 us
  local copies, waits for them, and re-layouts: 36.2 us -> 13.5 us
  other arithmetic: 9.03 us -> 0 us
  Pallas kernels: 469 us -> 476 us
    psum x1 -> x0, blocking collectives: 42.8 us -> none  [body(): summed = lax.psum(jnp.concatenate(gains), ('dp', 'mp'))]
    dot_general x21 -> x9, matrix products: 73 us -> 43.1 us  [matmul(): return jnp.dot(left_op, right_op, preferred_element_type=jnp.float32)]
    dot_general x2 -> x0, local copies, waits for them, and re-layouts: 9.62 us -> none  [matmul(): return jnp.dot(left_op, right_op, preferred_element_type=jnp.float32)]
    unnamed x124 -> x35, local copies, waits for them, and re-layouts: 17.8 us -> 9.86 us
    pallas_call x3 -> x2, Pallas kernels: 388 us -> 393 us  [the longest x1 224 us: forward(): pl.pallas_call(functools.partial(forward_kernel, dp_size), out_shape=shap...]
where the time goes in v2:
time: 540 us; the launch traced here: 533 us
  Pallas kernels  476 us (88%)
  matrix products  43.1 us (8%)
  local copies, waits for them, and re-layouts  13.5 us (2%)
    pallas_call x1, Pallas kernels, forward(): pl.pallas_call(functools.partial(forward_kernel, dp_size), out_shape=shap...  224 us
    pallas_call x1, Pallas kernels, backward(): pl.pallas_call(functools.partial(backward_kernel, dp_size), out_shape=sha...  169 us
    pallas_call x1, Pallas kernels, attn_reduce(): pl.pallas_call(functools.partial(attn_reduce_kernel, dp_size), out_shape=...  82.5 us
    dot_general x9, matrix products, matmul(): return jnp.dot(left_op, right_op, preferred_element_type=jnp.float32)  43.1 us

profile of v2, /device:TPU:0, one launch (start us, length us, event | category | flops | bytes accessed | tf_op | source)
XLA Modules:
  0.0 533.4 jit_solution(7498219232265888409)
XLA Ops:
  0.6 1.5 copy.27.seg_col
  2.1 224.3 %shard_map.237 = (bf16[2048,1024]{1,0:T(8,128)(2,1)}, bf16[2048,512]{1,0:T(8,128)(2,1)}, bf16[2048,512]{1,0:T(8,128)(2,1)}, bf16[2048,1024]{1,0:T(8,128)(2,1)}, ...) custom-call(bf16[128,1024]{1,0:T(8,128)(2,1)} %w_q.1, ...), custom_call_target="tpu_custom_call" | custom-call | tf_op jit(solution)/shard_map/pallas_call | solution.py:403
  226.4 0.0 copy-start.9
  226.5 0.0 copy-start.12
  226.5 6.5 %fusion.7 = f32[1024,768]{1,0:T(8,128)S(1)} fusion(bf16[1024,2048]{1,0:T(8,128)(2,1)} %bitcast.71, bf16[2048,768]{1,0:T(8,128)(2,1)} %get-tuple-element.58), kind=kOutput, calls=%fused_computation.20 | convolution fusion | flops 3221225472 | bytes 10485760 | tf_op jit(solution)/shard_map/dot_general | solution.py:17
  232.9 0.0 copy-done.9
  232.9 0.0 copy-done.12
  232.9 0.0 copy-start.8
  233.0 0.0 copy-start.10
  233.0 3.4 fusion.6
  236.4 0.0 copy-done.8
  236.4 0.0 copy-done.10
  236.4 4.5 multiply_convert_fusion
  240.9 5.0 convolution_convert_fusion.1
  245.9 5.0 convolution_convert_fusion.2
  250.9 5.0 convolution_convert_fusion.3
  255.8 0.0 copy-start.11
  255.8 5.2 convolution_convert_fusion
  261.1 0.0 copy-done.11
  261.1 3.4 fusion.8
  264.6 5.1 add_convert_fusion
  269.6 168.7 %shard_map.238 = (bf16[2048,1024]{1,0:T(8,128)(2,1)}, bf16[2048,512]{1,0:T(8,128)(2,1)}, bf16[2048,512]{1,0:T(8,128)(2,1)}, bf16[2048,1024]{1,0:T(8,128)(2,1)}, ...) custom-call(bf16[4,2,128,2048]{3,2,1,0:T(8,128)(2,1)} %bitcast.52, ...), custom_call_target="tpu_custom_call" | custom-call | tf_op jit(solution)/shard_map/pallas_call | solution.py:686
  438.4 0.0 copy-start.3
  438.4 82.5 %shard_map.239 = (bf16[256,2048]{1,0:T(8,128)(2,1)}, f32[8,2048]{1,0:T(8,128)}, f32[128,1024]{1,0:T(8,128)}, f32[128,512]{1,0:T(8,128)}, f32[128,512]{1,0:T(8,128)}, /*index=5*/f32[128,1024]{1,0:T(8,128)}) custom-call(bf16[4,2,2,128,1024]{4,3,2,1,0:T(8,128)(2,1)} %bitcast.50, bf16[4,2,2,128,512]{4,3,2,1,0:T(8,128)(2,1)} %bitcast.58, ...), custom_call_target="tpu_custom_call" | custom-call | tf_op jit(solution)/shard_map/pallas_call | solution.py:811
  520.9 0.0 copy-start.5
  520.9 0.0 copy-start.7
  520.9 0.0 copy-start.6
  520.9 1.0 fusion.5
  521.9 0.6 fusion.3
  522.5 0.5 fusion.1
  523.1 0.0 copy-done.3
  523.1 0.0 copy-start.4
  523.1 1.0 copy.37
  524.0 2.4 copy.38
  526.5 0.0 copy-done.5
  526.5 0.8 copy.39
  527.3 0.0 copy-done.7
  527.3 0.7 copy.40
  528.0 0.0 copy-done.6
  528.0 0.7 copy.41
  528.7 0.0 copy-done.4
  528.7 0.8 copy.42
  529.5 0.0 copy-done.2
  529.5 1.1 copy.43
  530.6 0.0 copy-done.1
  530.6 1.1 copy.44
  531.8 0.0 copy-done
  531.8 1.1 copy.45
  (3 shorter events, 0.0 us)
Async XLA Ops:
  226.4 6.5 %copy-start.9 = (bf16[4,2,128,2048]{3,2,1,0:T(8,128)(2,1)S(1)}, bf16[4,2,128,2048]{3,2,1,0:T(8,128)(2,1)}, u32[]{:S(2)}) copy-start(bf16[4,2,128,2048]{3,2,1,0:T(8,128)(2,1)} %get-tuple-element.54) | copy-start | bytes 12582916
  226.5 6.5 %copy-start.12 = (bf16[2048,768]{1,0:T(8,128)(2,1)S(1)}, bf16[2048,768]{1,0:T(8,128)(2,1)}, u32[]{:S(2)}) copy-start(bf16[2048,768]{1,0:T(8,128)(2,1)} %get-tuple-element.55) | copy-start | bytes 9437188
  232.9 3.5 copy-start.8
  233.0 3.5 copy-start.10
  255.8 5.3 copy-start.11
  438.4 84.7 %copy-start.3 = (bf16[256,2048]{1,0:T(8,128)(2,1)S(1)}, bf16[256,2048]{1,0:T(8,128)(2,1)}, u32[]{:S(2)}) copy-start(bf16[256,2048]{1,0:T(8,128)(2,1)} %get-tuple-element.75) | copy-start | bytes 3145732
  520.9 5.6 %copy-start.5 = (f32[128,1024]{1,0:T(8,128)S(1)}, f32[128,1024]{1,0:T(8,128)}, u32[]{:S(2)}) copy-start(f32[128,1024]{1,0:T(8,128)} %get-tuple-element.121) | copy-start | bytes 1572868
  520.9 6.4 %copy-start.7 = (f32[128,512]{1,0:T(8,128)S(1)}, f32[128,512]{1,0:T(8,128)}, u32[]{:S(2)}) copy-start(f32[128,512]{1,0:T(8,128)} %get-tuple-element.122) | copy-start | bytes 786436
  520.9 7.1 %copy-start.6 = (f32[128,512]{1,0:T(8,128)S(1)}, f32[128,512]{1,0:T(8,128)}, u32[]{:S(2)}) copy-start(f32[128,512]{1,0:T(8,128)} %get-tuple-element.123) | copy-start | bytes 786436
  523.1 5.6 %copy-start.4 = (f32[128,1024]{1,0:T(8,128)S(1)}, f32[128,1024]{1,0:T(8,128)}, u32[]{:S(2)}) copy-start(f32[128,1024]{1,0:T(8,128)} %get-tuple-element.124) | copy-start | bytes 1572868
  524.0 5.4 %copy-start.2 = (f32[128,3072]{1,0:T(8,128)S(1)}, f32[128,3072]{1,0:T(8,128)}, u32[]{:S(2)}) copy-start(f32[128,3072]{1,0:T(8,128)} %get-tuple-element.125) | copy-start | bytes 4718596
  526.5 4.2 copy-start.1
  529.5 2.3 copy-start

commit v3 on v0

v3 whole, which is shorter than its diff:
```python
import functools
import math

import jax
import jax.numpy as jnp
from jax import lax
from jax.experimental import pallas as pl
from jax.experimental.pallas import tpu as pltpu
from jax.sharding import PartitionSpec as P

EPSILON = 1e-06
ROPE_BASE = 1000000.0
MASKED = -1e30


def matmul(left_op, right_op):
    return jnp.dot(left_op, right_op, preferred_element_type=jnp.float32)


def rms_norm(values, gain_vec):
    inv_rms = lax.rsqrt(jnp.mean(values * values, axis=-1, keepdims=True) + EPSILON)
    return (values * inv_rms * gain_vec, inv_rms)


def norm_back(grad_norm, values, inv_rms, gain_vec):
    scaled = grad_norm * gain_vec
    cubed = inv_rms * inv_rms * inv_rms
    grad_values = inv_rms * scaled - values * cubed * jnp.mean(
        scaled * values, axis=-1, keepdims=True
    )
    return (grad_values, grad_norm * values * inv_rms)


MESH = pl.DeviceIdType.MESH
ANY = pl.BlockSpec(memory_space=pl.ANY)
VMEM = pl.BlockSpec(memory_space=pltpu.VMEM)
DEPTH = 4
CORES = 2
HALVES = 2
UP, DOWN = 0, 1
TILE = 256


def split(index, size):
    size = jnp.int32(size)
    return lax.div(index, size), lax.rem(index, size)


class Place:
    def __init__(self, dp_size):
        self.wide = dp_size // (DEPTH * CORES)
        self.x = lax.axis_index("mp")
        rest, self.c = split(lax.axis_index("dp"), CORES)
        self.z, self.y = split(rest, self.wide)

    def device(self, z=None, y=None, c=None, x=None):
        z = self.z if z is None else z
        y = self.y if y is None else y
        c = self.c if c is None else c
        x = self.x if x is None else x
        return ((z * self.wide + y) * CORES + c, x)

    def z_off(self, step):
        return lax.rem(self.z + DEPTH + step, jnp.int32(DEPTH))

    def y_off(self, step):
        return lax.rem(self.y + self.wide + step, jnp.int32(self.wide))

    def rows(self, z, y, c, count):
        return pl.ds(pl.multiple_of(((z * self.wide + y) * CORES + c) * count, count), count)

    def line(self):
        return [self.device(z=self.z_off(1)), self.device(z=self.z_off(-1))]

    def z_peers(self):
        return [self.device(z=self.z_off(k)) for k in range(1, DEPTH)]

    def y_peers(self):
        return [self.device(y=self.y_off(j)) for j in range(1, self.wide)]

    def order(self):
        low = 1 - lax.div(self.z, jnp.int32(2))
        return [3 * low, 1 + low, low * (1 - self.z) + (1 - low) * (5 - self.z), self.z]


def guarded(when, action):
    if when is None:
        action()
    else:
        pl.when(when)(action)


class Mail:
    def __init__(self, send_sems, recv_sems):
        self.send_sems, self.recv_sems = send_sems, recv_sems
        self.count = 0
        self.open = []

    def reserve(self, count):
        first = self.count
        self.count += count
        return first

    def describe(self, source, target, device, slot):
        return pltpu.make_async_remote_copy(
            source,
            target,
            self.send_sems.at[slot],
            self.recv_sems.at[slot],
            device_id=device,
            device_id_type=MESH,
        )

    def make(self, source, target, device, when=None, slot=None):
        copy = self.describe(source, target, device, self.reserve(1) if slot is None else slot)
        self.open.append((copy, when))
        return copy

    def send(self, source, target, device, when=None):
        copy = self.make(source, target, device, when)
        guarded(when, copy.start)
        return copy

    def finish(self):
        for copy, when in self.open:
            guarded(when, copy.wait_send)


def meet(devices):
    barrier = pltpu.get_barrier_semaphore()
    for device in devices:
        pl.semaphore_signal(barrier, inc=1, device_id=device, device_id_type=MESH)
    pl.semaphore_wait(barrier, len(devices))


def receive(copies):
    for copy in copies:
        copy.wait_recv()


def start_all(copies):
    for copy in copies:
        copy.start()


class LineGather:
    def __init__(self, mail, at, own, place, sides, sibling=None, share_own=True):
        self.mail, self.at, self.place = mail, at, place
        self.sides, self.sibling = sides, sibling
        self.neighbours = at.line()
        self.open_end = [at.z < DEPTH - 1, at.z > 0]
        pairs = list(zip(own, place(at.z, 0)))
        self.hops = [
            [mail.send(source, target, self.neighbours[way], self.open_end[way]) for source, target in pairs]
            for way in (UP, DOWN)
        ]
        self.over, self.cores = {}, []
        if share_own:
            self.over["own"] = [
                [mail.send(source, target, side) for source, target in pairs] for side in sides
            ]
        if sibling is not None:
            self.cores.append(
                (None, [mail.send(source, target, sibling) for source, target in pairs])
            )

    def where(self, way, step):
        z = self.at.z
        if way == UP:
            return z >= step + 1, self.at.z_off(-1 - step)
        return z + 1 + step < DEPTH, self.at.z_off(1 + step)

    def step(self, step):
        for way in (UP, DOWN):
            got, index = self.where(way, step)
            refs = self.place(index, 0)
            arrived = self.hops[way]
            onward = []
            if step < DEPTH - 2:
                more = got & self.open_end[way]
                onward = [self.mail.make(ref, ref, self.neighbours[way], more) for ref in refs]
            over = [[self.mail.make(ref, ref, side, got) for ref in refs] for side in self.sides]
            cores = []
            if self.sibling is not None:
                cores = [self.mail.make(ref, ref, self.sibling, got) for ref in refs]

            def pass_on(way=way, arrived=arrived, onward=onward, over=over, cores=cores):
                receive(arrived)
                pl.when(self.open_end[way])(lambda: start_all(onward))
                for copies in over:
                    start_all(copies)
                start_all(cores)

            pl.when(got)(pass_on)
            self.hops[way] = onward
            self.over[way, step] = over
            if cores:
                self.cores.append((got, cores))

    def side_step(self, key):
        got, index = (None, self.at.z) if key == "own" else self.where(*key)
        cores = []
        for j in range(1, len(self.sides) + 1):
            if self.sibling is not None:
                refs = self.place(index, j)
                cores += [self.mail.make(ref, ref, self.sibling, got) for ref in refs]

        def pass_on():
            for copies in self.over[key]:
                receive(copies)
            start_all(cores)

        guarded(got, pass_on)
        if cores:
            self.cores.append((got, cores))

    def side_steps(self, step):
        self.side_step((UP, step))
        self.side_step((DOWN, step))

    def finish(self):
        for got, cores in self.cores:
            guarded(got, lambda cores=cores: receive(cores))


class LineReduce:
    slots = 2 * (DEPTH - 1)

    def __init__(self, mail, at, pieces, part, land):
        self.mail, self.at, self.pieces, self.part, self.land = mail, at, pieces, part, land
        self.base = mail.reserve(self.slots * pieces)

    def copies(self, index, sources, device):
        slots = [self.base + index * self.pieces + i for i in range(self.pieces)]
        return [
            self.mail.describe(source, target, device, slot)
            for source, target, slot in zip(sources, self.land(index), slots)
        ]

    def pass_on(self, turn):
        z = self.at.z
        low = 1 - lax.div(z, jnp.int32(2))
        up = low if turn < 2 else 1 - lax.rem(z, jnp.int32(2))
        target = self.at.order()[turn]
        index = up * (target - 1) + (1 - up) * (DEPTH - 1 + target)
        device = self.at.device(z=z + 2 * up - 1)
        sources = self.part(target)
        copies = self.copies(index, sources, device)
        has_in = up * jnp.where(z > 0, 1, 0) + (1 - up) * jnp.where(z < DEPTH - 1, 1, 0)

        @pl.when(has_in > 0)
        def _():
            receive(copies)
            for source, landed in zip(sources, self.land(index)):
                add_into(source, landed)

        start_all(copies)
        self.mail.open += [(copy, None) for copy in copies]

    def last(self, use):
        z = self.at.z
        sources = self.part(z)
        for when, index, neighbour in (
            (z > 0, lax.max(z - 1, 0), self.at.z_off(-1)),
            (z < DEPTH - 1, lax.min(DEPTH - 1 + z, self.slots - 1), self.at.z_off(1)),
        ):
            copies = self.copies(index, sources, self.at.device(z=neighbour))

            @pl.when(when)
            def _(copies=copies, index=index):
                receive(copies)
                for i, landed in enumerate(self.land(index)):
                    use(i, landed)


def own_copies(pairs, sems, first=0):
    copies = [
        pltpu.make_async_copy(source, target, sems.at[first + i])
        for i, (source, target) in enumerate(pairs)
    ]
    start_all(copies)
    return copies


def finish_own(copies):
    for copy in copies:
        copy.wait()


def add_into(target, *others):
    total = target[...].astype(jnp.float32)
    for other in others:
        total = total + other[...].astype(jnp.float32)
    target[...] = total.astype(target.dtype)


def dot_nt(left_op, right_op):
    return lax.dot_general(
        left_op, right_op, (((1,), (1,)), ((), ())), preferred_element_type=jnp.float32
    )


def dot_tn(left_op, right_op):
    return lax.dot_general(
        left_op, right_op, (((0,), (0,)), ((), ())), preferred_element_type=jnp.float32
    )


def turned(values):
    return pltpu.roll(values, values.shape[-1] // 2, axis=values.ndim - 1)


def document_tables(seg_col, seg_row, head_dim):
    seq_len = seg_col.shape[0]
    rows = lax.broadcasted_iota(jnp.int32, (seq_len, seq_len), 0)
    cols = lax.broadcasted_iota(jnp.int32, (seq_len, seq_len), 1)
    same = seg_col == seg_row
    bias = jnp.where(same & (cols <= rows), 0.0, MASKED)
    before = jnp.where(same & (cols < rows), 1.0, 0.0)
    position = jnp.sum(before, axis=-1, keepdims=True)
    lane = lax.broadcasted_iota(jnp.int32, (1, head_dim), 1)
    half_dim = head_dim // 2
    slot = jnp.where(lane < half_dim, lane, lane - half_dim).astype(jnp.float32)
    frequency = jnp.exp(slot * (-2.0 * math.log(ROPE_BASE) / head_dim))
    angles = position * frequency
    sine = jnp.sin(angles)
    return bias, jnp.cos(angles), jnp.where(lane < half_dim, -sine, sine)


def matmul_tiles(left, right, write, tile=256):
    @pl.loop(0, right.shape[1] // tile)
    def _(index):
        columns = pl.ds(pl.multiple_of(index * tile, tile), tile)
        write(columns, matmul(left[...], right[:, columns]))


def forward_kernel(
    dp_size, w_q, w_k, w_v, w_o, w_g, w_u, w_d, cot, row_in, seg_col, seg_row,
    gain_one, gain_two, q_gain, k_gain,
    o_attn, o_ffn, o_c, o_n,
    mid, normed_one, query_raw, key_raw, values_half, queries, keys, context, log_total,
    cosine, sine, bias,
    full, outgoing, incoming, normed, own_sems, send_sems, recv_sems,
):
    at = Place(dp_size)
    z, y, c, x = at.z, at.y, at.c, at.x
    sibling, other = at.device(c=1 - c), at.device(x=1 - x)
    z_peers, y_peers = at.z_peers(), at.y_peers()
    meet([sibling, other] + z_peers + y_peers)

    mail = Mail(send_sems, recv_sems)
    rows = w_q.shape[0]
    head_dim = q_gain.shape[1]
    part = w_g.shape[1] // DEPTH
    tokens = mid.shape[0]
    here = at.rows(z, y, c, rows)
    spans, start = [], 0
    for weight in (w_q, w_k, w_v, w_o):
        spans.append(pl.ds(start, weight.shape[1]))
        start += weight.shape[1]
    q_span, k_span, v_span, o_span = spans
    ffn = [(weight, pl.ds(i * part, part)) for i, weight in enumerate((w_g, w_u, w_d))]

    def columns(index):
        return pl.ds(pl.multiple_of(index * part, part), part)

    def half_rows(index):
        return pl.ds(pl.multiple_of(index * tokens, tokens), tokens)

    mine = own_copies(
        [(weight, full.at[here, span]) for weight, span in zip((w_q, w_k, w_v, w_o), spans)],
        own_sems,
    )
    own_ffn = own_copies(
        [(weight.at[:, columns(z)], o_ffn.at[here, span]) for weight, span in ffn]
        + [(cot.at[half_rows(i)], o_c.at[z, i]) for i in range(2)],
        own_sems,
        4,
    )
    finish_own(mine)
    attn = LineGather(
        mail,
        at,
        (full.at[here],),
        lambda zb, j: [full.at[at.rows(zb, at.y_off(-j), c, rows)]],
        y_peers,
        sibling,
    )

    residual = row_in[...].astype(jnp.float32)
    normed_full, _ = rms_norm(residual, gain_one[...])
    normed_one[...] = normed_full.astype(jnp.bfloat16)
    bias_values, cosine[...], sine[...] = document_tables(seg_col[...], seg_row[...], head_dim)
    bias[...] = bias_values

    spread, crossing, to_sibling = {}, {}, []

    def start_spread():
        for k in range(1, DEPTH):
            target = at.z_off(k)
            spread[k] = [
                mail.send(weight.at[:, columns(target)], o_ffn.at[here, span], z_peers[k - 1])
                for weight, span in ffn
            ]
        finish_own(own_ffn)
        block = o_ffn.at[here]
        for j in range(1, at.wide):
            crossing[0, j] = mail.send(block, block, y_peers[j - 1])
        to_sibling.append(mail.send(block, block, sibling))

    def forward_spread(k):
        receive(spread[k])
        block = o_ffn.at[at.rows(at.z_off(-k), y, c, rows)]
        for j in range(1, at.wide):
            crossing[k, j] = mail.send(block, block, y_peers[j - 1])
        to_sibling.append(mail.send(block, block, sibling))

    def forward_crossing(k):
        for j in range(1, at.wide):
            crossing[k, j].wait_recv()
            block = o_ffn.at[at.rows(at.z_off(-k), at.y_off(-j), c, rows)]
            to_sibling.append(mail.send(block, block, sibling))

    def half_place(out):
        return lambda zb, j: [out.at[zb, x if j == 0 else 1 - x]]

    attn.step(0)
    attn.side_step("own")
    attn.step(1)
    start_spread()
    attn.side_steps(0)
    attn.step(2)
    cots = LineGather(
        mail, at, (cot.at[half_rows(x)],), half_place(o_c), [other], share_own=False
    )
    attn.side_steps(1)
    attn.side_steps(2)
    attn.finish()
    saved = own_copies([(full, o_attn)], own_sems)

    def write_query(cols, block):
        query_raw[:, cols] = block

    def write_key(cols, block):
        key_raw[:, cols] = block

    def write_value(cols, block):
        values_half[:, cols] = block.astype(jnp.bfloat16)

    matmul_tiles(normed_one, full.at[:, q_span], write_query)
    matmul_tiles(normed_one, full.at[:, k_span], write_key)
    matmul_tiles(normed_one, full.at[:, v_span], write_value)
    cots.step(0)
    forward_spread(1)

    def rotated(raw, gain):
        unit, _ = rms_norm(raw, gain)
        return (unit * cosine[...] + turned(unit) * sine[...]).astype(jnp.bfloat16)

    kv_heads = key_raw.shape[1] // head_dim
    group = query_raw.shape[1] // key_raw.shape[1]
    for j in range(kv_heads):
        kv_cols = pl.ds(j * head_dim, head_dim)
        keys[:, kv_cols] = rotated(key_raw[:, kv_cols], k_gain[...])
        for g in range(group):
            head = j * group + g
            cols = pl.ds(head * head_dim, head_dim)
            queries[:, cols] = rotated(query_raw[:, cols], q_gain[...])
            scores = dot_nt(queries[:, cols], keys[:, kv_cols]) * (1.0 / math.sqrt(head_dim))
            scores = scores + bias[...]
            row_max = jnp.max(scores, axis=-1, keepdims=True)
            weights = jnp.exp(scores - row_max)
            total = jnp.sum(weights, axis=-1, keepdims=True)
            log_total[:, head : head + 1] = row_max + jnp.log(total)
            probs = (weights * (1.0 / total)).astype(jnp.bfloat16)
            context[:, cols] = matmul(probs, values_half[:, kv_cols]).astype(jnp.bfloat16)
        if j == kv_heads // 2 - 1:
            cots.step(1)
            forward_spread(3)

    given, kept = half_rows(1 - x), half_rows(x)
    width = row_in.shape[1]

    def project(token_rows, target):
        @pl.loop(0, width // TILE)
        def _(index):
            cols = pl.ds(pl.multiple_of(index * TILE, TILE), TILE)
            block = dot_nt(context[token_rows, :], full[cols, o_span])
            target[:, cols] = block.astype(target.dtype)

    project(given, outgoing)
    swap = mail.send(outgoing, incoming, other)
    project(kept, mid)
    forward_spread(2)
    cots.step(2)
    swap.wait_recv()
    total = row_in[kept, :].astype(jnp.float32) + (mid[...] + incoming[...].astype(jnp.float32))
    mid[...] = total
    normed_mid, _ = rms_norm(total, gain_two[...])
    normed[...] = normed_mid.astype(jnp.bfloat16)
    last = own_copies([(normed, o_n.at[z, x])], own_sems, 9)
    norms = LineGather(mail, at, (normed,), half_place(o_n), [other])
    cots.side_steps(0)
    forward_crossing(0)
    norms.step(0)
    forward_crossing(1)
    norms.step(1)
    forward_crossing(3)
    cots.side_steps(1)
    norms.step(2)
    forward_crossing(2)
    cots.side_steps(2)
    norms.side_step("own")
    for step in range(DEPTH - 1):
        norms.side_steps(step)
    receive(to_sibling)
    mail.finish()
    finish_own(saved + last)


def forward(dp_size, weights, cot, row_in, seg_row, gains):
    w_q, w_k, w_v, w_o, w_g, w_u, w_d = weights
    wide = dp_size // (DEPTH * CORES)
    seq_len, width = row_in.shape
    head_dim = gains[2].shape[1]
    tokens = seq_len // HALVES
    part = w_g.shape[1] // DEPTH
    half, whole = jnp.bfloat16, jnp.float32
    attn_cols = [w.shape[1] for w in (w_q, w_k, w_v, w_o)]
    shapes = [jax.ShapeDtypeStruct((width, cols), half) for cols in (sum(attn_cols), 3 * part)]
    shapes += [jax.ShapeDtypeStruct((DEPTH, HALVES, tokens, width), half)] * 2
    q_cols, kv_cols = attn_cols[0], attn_cols[1]
    for cols, kind in (
        (width, half), (q_cols, whole), (kv_cols, whole), (kv_cols, half), (q_cols, half),
        (kv_cols, half), (q_cols, half), (head_dim, whole), (head_dim, whole), (head_dim, whole),
        (seq_len, whole),
    ):
        shapes.append(jax.ShapeDtypeStruct((seq_len, cols), kind))
    shapes.insert(4, jax.ShapeDtypeStruct((tokens, width), whole))
    hops = 2 * (DEPTH - 1)
    spots = 1 + hops
    copies = (hops + spots * (2 * wide - 1)) + 2 * (2 * hops + 1) + 1
    copies += 9 + DEPTH * (2 * wide - 1)
    return pl.pallas_call(
        functools.partial(forward_kernel, dp_size),
        out_shape=shapes,
        in_specs=[ANY] * 8 + [VMEM] * 7,
        out_specs=[ANY] * 4 + [VMEM] * 12,
        scratch_shapes=[pltpu.VMEM((width, sum(attn_cols)), half)]
        + [pltpu.VMEM((tokens, width), half)] * 3
        + [
            pltpu.SemaphoreType.DMA((10,)),
            pltpu.SemaphoreType.DMA((copies,)),
            pltpu.SemaphoreType.DMA((copies,)),
        ],
        compiler_params=pltpu.CompilerParams(
            collective_id=0, has_side_effects=True, vmem_limit_bytes=56 * 2**20
        ),
    )(w_q, w_k, w_v, w_o, w_g, w_u, w_d, cot, row_in, seg_row[:, None], seg_row[None, :], *gains)


def mlp_kernel(
    dp_size, weights, n_all, c_all, mid, cot, gain,
    o_m, o_h, o_l, o_t, shares,
    full, x_n, x_c, hidden, p_n, p_o, h_n, h_o, l_n, l_o, from_core, from_y,
    own_sems, send_sems, recv_sems,
):
    at = Place(dp_size)
    z, y, c, x = at.z, at.y, at.c, at.x
    other, sibling = at.device(x=1 - x), at.device(c=1 - c)
    y_peers = at.y_peers()
    order = at.order()
    tokens = mid.shape[0]
    block_rows = HALVES * tokens
    rows = from_core.shape[2]
    part = full.shape[1] // 3
    gate_up, down = pl.ds(0, 2 * part), pl.ds(2 * part, part)
    width = mid.shape[1]

    def band(index, size):
        return pl.ds(pl.multiple_of(index * size, size), size)

    loads = {}
    for i, name in enumerate("gud"):
        span = pl.ds(i * part, part)
        loads[name] = pltpu.make_async_copy(weights.at[:, span], full.at[:, span], own_sems.at[i])
    for i, index in enumerate(order):
        block = band(index, block_rows)
        loads["n", i] = pltpu.make_async_copy(n_all.at[block], x_n.at[block], own_sems.at[3 + i])
        loads["c", i] = pltpu.make_async_copy(c_all.at[block], x_c.at[block], own_sems.at[7 + i])
    for key in ("g", "u", ("n", 0), "d", ("c", 0)):
        loads[key].start()
    for i in range(1, DEPTH):
        loads["n", i].start()
        loads["c", i].start()
    meet([other, sibling] + at.line() + y_peers)
    mail = Mail(send_sems, recv_sems)

    def half_rows(index, side):
        return band(index * HALVES + side, tokens)

    norm_line = LineReduce(
        mail, at, 1, lambda index: [p_n.at[half_rows(index, x)]], lambda slot: [l_n.at[slot]]
    )
    out_line = LineReduce(
        mail, at, 1, lambda index: [p_o.at[half_rows(index, x)]], lambda slot: [l_o.at[slot]]
    )
    norm_swaps, out_swaps = [], []

    def compute(i):
        block = band(order[i], block_rows)
        if i == 0:
            for name in ("g", "u", "d"):
                loads[name].wait()
        loads["n", i].wait()
        loads["c", i].wait()

        @pl.loop(0, part // TILE)
        def _(index):
            g_cols, u_cols, d_cols = [
                pl.ds(pl.multiple_of(i * part + index * TILE, TILE), TILE) for i in range(3)
            ]
            gate = matmul(x_n[block, :], full[:, g_cols])
            up = matmul(x_n[block, :], full[:, u_cols])
            grad_act = matmul(x_c[block, :], full[:, d_cols])
            sigmoid_gate = 1.0 / (1.0 + jnp.exp(-gate))
            silu_val = gate * sigmoid_gate
            hidden[block, g_cols] = (
                grad_act * up * sigmoid_gate * (1.0 + gate * (1.0 - sigmoid_gate))
            ).astype(jnp.bfloat16)
            hidden[block, u_cols] = (grad_act * silu_val).astype(jnp.bfloat16)
            hidden[block, d_cols] = (silu_val * up).astype(jnp.bfloat16)

        @pl.loop(0, width // TILE)
        def _(index):
            cols = band(index, TILE)
            p_n[block, cols] = dot_nt(hidden[block, gate_up], full[cols, gate_up]).astype(jnp.bfloat16)

        norm_swaps.append(mail.send(p_n.at[half_rows(order[i], 1 - x)], h_n.at[i], other))

        @pl.loop(0, width // TILE)
        def _(index):
            cols = band(index, TILE)
            p_o[block, cols] = dot_nt(hidden[block, down], full[cols, down]).astype(jnp.bfloat16)

    def reduce_step(line, partial, swaps, landed, i):
        swaps[i].wait_recv()
        add_into(partial.at[half_rows(order[i], x)], landed.at[i])
        line.pass_on(i)

    def weight_grads(i):
        @pl.loop(0, width // DEPTH // TILE)
        def _(index):
            cols = pl.ds(pl.multiple_of(order[i] * (width // DEPTH) + index * TILE, TILE), TILE)
            full[cols, gate_up] = matmul(x_n[:, cols].T, hidden[:, gate_up]).astype(jnp.bfloat16)
            full[cols, down] = matmul(x_c[:, cols].T, hidden[:, down]).astype(jnp.bfloat16)

        return [
            mail.send(
                full.at[at.rows(order[i], side, 1 - c, rows)], from_core.at[order[i], side], sibling
            )
            for side in range(at.wide)
        ]

    to_core, to_y = {}, {}

    def core_stage(i):
        receive(to_core[i])
        for side in range(at.wide):
            add_into(full.at[at.rows(order[i], side, c, rows)], from_core.at[order[i], side])
        to_y[i] = [
            mail.send(
                full.at[at.rows(order[i], at.y_off(j), c, rows)],
                from_y.at[j - 1, order[i]],
                y_peers[j - 1],
            )
            for j in range(1, at.wide)
        ]

    def y_stage(i):
        receive(to_y[i])
        total = full[at.rows(order[i], y, c, rows), :].astype(jnp.float32)
        for j in range(1, at.wide):
            total = total + from_y[j - 1, order[i]].astype(jnp.float32)
        shares[order[i]] = total.astype(jnp.bfloat16)

    compute(0)
    compute(1)
    reduce_step(norm_line, p_n, norm_swaps, h_n, 0)
    compute(2)
    compute(3)
    reduce_step(norm_line, p_n, norm_swaps, h_n, 1)
    to_core[0] = weight_grads(0)
    to_core[1] = weight_grads(1)
    core_stage(0)
    reduce_step(norm_line, p_n, norm_swaps, h_n, 2)
    to_core[2] = weight_grads(2)
    core_stage(1)
    to_core[3] = weight_grads(3)
    core_stage(2)
    norm_swaps[3].wait_recv()
    for i in range(DEPTH):
        out_swaps.append(mail.send(p_o.at[half_rows(order[i], 1 - x)], h_o.at[i], other))
    core_stage(3)
    o_m[...] = p_n[half_rows(z, x), :].astype(jnp.float32) + h_n[3].astype(jnp.float32)

    def add_norm(_, landed):
        o_m[...] = o_m[...] + landed[...].astype(jnp.float32)

    norm_line.last(add_norm)
    grad_norm = o_m[...]
    values = mid[...]
    inv_rms = lax.rsqrt(jnp.mean(values * values, axis=-1, keepdims=True) + EPSILON)
    grad_values, terms = norm_back(grad_norm, values, inv_rms, gain[...])
    o_t[...] = jnp.sum(terms, axis=0, keepdims=True)
    kept = band(x, tokens)
    total = cot[kept, :].astype(jnp.float32) + grad_values
    o_m[...] = total
    o_h[kept, :] = total.astype(jnp.bfloat16)
    swap_h = mail.send(o_h.at[kept], o_h.at[kept], other)
    for i in range(DEPTH - 1):
        reduce_step(out_line, p_o, out_swaps, h_o, i)
        y_stage(i)
    y_stage(DEPTH - 1)
    out_swaps[3].wait_recv()
    o_l[...] = mid[...] + (
        p_o[half_rows(z, x), :].astype(jnp.float32) + h_o[3].astype(jnp.float32)
    )

    def add_out(_, landed):
        o_l[...] = o_l[...] + landed[...].astype(jnp.float32)

    out_line.last(add_out)
    swap_h.wait_recv()
    mail.finish()


def mlp(dp_size, weights, normed, cots, mid, cot, gain):
    wide = dp_size // (DEPTH * CORES)
    tokens, width = mid.shape
    cols = weights.shape[1]
    rows = width // dp_size
    every = DEPTH * HALVES * tokens
    half, full = jnp.bfloat16, jnp.float32
    copies = 2 * LineReduce.slots + 2 * DEPTH + DEPTH * (2 * wide - 1) + 1
    shapes = [
        jax.ShapeDtypeStruct((tokens, width), full),
        jax.ShapeDtypeStruct((HALVES * tokens, width), half),
        jax.ShapeDtypeStruct((tokens, width), full),
        jax.ShapeDtypeStruct((1, width), full),
        jax.ShapeDtypeStruct((DEPTH, rows, cols), half),
    ]
    return pl.pallas_call(
        functools.partial(mlp_kernel, dp_size),
        out_shape=shapes,
        in_specs=[ANY] * 3 + [VMEM] * 3,
        out_specs=[VMEM] * 5,
        scratch_shapes=[pltpu.VMEM((width, cols), half)]
        + [pltpu.VMEM((every, width), half)] * 2
        + [pltpu.VMEM((every, cols), half)]
        + [pltpu.VMEM((every, width), half)] * 2
        + [pltpu.VMEM((DEPTH, tokens, width), half)] * 2
        + [pltpu.VMEM((LineReduce.slots, tokens, width), half)] * 2
        + [
            pltpu.VMEM((DEPTH, wide, rows, cols), half),
            pltpu.VMEM((wide - 1, DEPTH, rows, cols), half),
            pltpu.SemaphoreType.DMA((11,)),
            pltpu.SemaphoreType.DMA((copies,)),
            pltpu.SemaphoreType.DMA((copies,)),
        ],
        compiler_params=pltpu.CompilerParams(
            collective_id=1, has_side_effects=True, vmem_limit_bytes=63 * 2**20
        ),
    )(weights, normed, cots, mid, cot, gain)


def pair_devices(at):
    def flip(index, bit):
        return index + bit - 2 * bit * lax.rem(lax.div(index, jnp.int32(bit)), jnp.int32(2))

    bits = [1 << i for i in range(at.wide.bit_length() - 1)]
    return (
        [at.device(c=1 - at.c), at.device(x=1 - at.x)]
        + [at.device(y=flip(at.y, bit)) for bit in bits]
        + [at.device(z=flip(at.z, bit)) for bit in (1, 2)]
    )


def backward_kernel(
    dp_size, shares, weights,
    grad_mid, mid_half, out_half, t_m, gain_one, row_in, normed_one, query_raw, key_raw,
    values_half, queries, keys, context, log_total, cosine, sine, bias, q_gain, k_gain,
    o_l, o_i, sums, d_q, d_k, d_v, d_o, d_g, d_u, d_d,
    full, from_core, from_y, from_z, from_spread, context_grad, raw_half, flipped, partial,
    outgoing, incoming, gathering, arriving, own_sems, send_sems, recv_sems,
):
    at = Place(dp_size)
    z, y, c, x = at.z, at.y, at.c, at.x
    other, sibling = at.device(x=1 - x), at.device(c=1 - c)
    y_peers, z_peers = at.y_peers(), at.z_peers()
    order = at.order()
    pairs = pair_devices(at)
    tokens, width = grad_mid.shape
    rows = d_q.shape[0]
    part = shares.shape[2] // 3
    spans, start = [], 0
    for out in (d_q, d_k, d_v, d_o):
        spans.append(pl.ds(start, out.shape[1]))
        start += out.shape[1]
    q_span, k_span, v_span, o_span = spans
    qkv_span = pl.ds(0, start - d_o.shape[1])
    q_cols, kv_width = d_q.shape[1], d_k.shape[1]
    head_dim = q_gain.shape[1]

    def band(index, size):
        return pl.ds(pl.multiple_of(index * size, size), size)

    kept, given = band(x, tokens), band(1 - x, tokens)
    loads = own_copies(
        [(weights.at[:, span], full.at[:, span]) for span in (o_span, qkv_span)], own_sems
    )
    o_l[kept, :] = out_half[...].astype(jnp.bfloat16)
    meet([other, sibling] + y_peers + z_peers + pairs)
    mail = Mail(send_sems, recv_sems)
    to_z = {
        k: mail.send(shares.at[at.z_off(k)], from_spread.at[k - 1], z_peers[k - 1])
        for k in (2, 1, 3)
    }
    swap_l = mail.send(o_l.at[kept], o_l.at[kept], other)
    flipped[...] = normed_one[...].T
    sets = {"o": (o_span, ((d_o, o_span),)), "qkv": (qkv_span, tuple(zip((d_q, d_k, d_v), spans)))}
    lines = {
        name: LineReduce(
            mail,
            at,
            1,
            lambda index, span=span: [full.at[at.rows(index, y, c, rows), span]],
            lambda slot, span=span: [from_z.at[slot, :, span]],
        )
        for name, (span, _) in sets.items()
    }
    to_core, to_y = {}, {}

    def core_sends(name, i):
        span, _ = sets[name]
        to_core[name, i] = [
            mail.send(
                full.at[at.rows(order[i], side, 1 - c, rows), span],
                from_core.at[order[i], side, :, span],
                sibling,
            )
            for side in range(at.wide)
        ]

    def core_stage(name, i):
        span, _ = sets[name]
        receive(to_core[name, i])
        for side in range(at.wide):
            add_into(
                full.at[at.rows(order[i], side, c, rows), span], from_core.at[order[i], side, :, span]
            )
        to_y[name, i] = [
            mail.send(
                full.at[at.rows(order[i], at.y_off(j), c, rows), span],
                from_y.at[j - 1, order[i], :, span],
                y_peers[j - 1],
            )
            for j in range(1, at.wide)
        ]

    def y_stage(name, i):
        span, outs = sets[name]
        receive(to_y[name, i])
        if i < DEPTH - 1:
            terms = [from_y.at[j - 1, order[i], :, span] for j in range(1, at.wide)]
            add_into(full.at[at.rows(order[i], y, c, rows), span], *terms)
            lines[name].pass_on(i)
            return
        for out, own in outs:
            out[...] = full[at.rows(z, y, c, rows), own].astype(jnp.float32)
            add_into(out, *[from_y.at[j - 1, z, :, own] for j in range(1, at.wide)])

    def finish_line(name):
        span, outs = sets[name]

        def use(_, landed):
            for out, own in outs:
                first = own.start - span.start
                add_into(out, landed.at[:, pl.ds(first, own.size)])

        lines[name].last(use)

    gathering[...] = jnp.zeros(gathering.shape, jnp.float32)
    loads[0].wait()

    def write_context(cols, value):
        context_grad[:, cols] = value.astype(jnp.bfloat16)

    matmul_tiles(mid_half, full.at[:, o_span], write_context)

    quarter = width // DEPTH
    for i in range(DEPTH):

        @pl.loop(0, quarter // TILE)
        def _(index, i=i):
            cols = pl.ds(pl.multiple_of(order[i] * quarter + index * TILE, TILE), TILE)
            full[cols, o_span] = dot_tn(mid_half[:, cols], context[...]).astype(jnp.bfloat16)

        core_sends("o", i)

    kv_heads = key_raw.shape[1] // head_dim
    group = query_raw.shape[1] // key_raw.shape[1]
    scale = 1.0 / math.sqrt(head_dim)

    def raw_grad(grad, raw, gain):
        back = grad * cosine[...] - turned(grad) * sine[...]
        inv_rms = lax.rsqrt(jnp.mean(raw * raw, axis=-1, keepdims=True) + EPSILON)
        grad_raw, terms = norm_back(back, raw, inv_rms, gain)
        return grad_raw.astype(jnp.bfloat16), jnp.sum(terms, axis=0, keepdims=True)

    q_sum = jnp.zeros((1, head_dim), jnp.float32)
    k_sum = jnp.zeros((1, head_dim), jnp.float32)
    for j in range(kv_heads):
        kv_cols = pl.ds(j * head_dim, head_dim)
        key_total = jnp.zeros((row_in.shape[0], head_dim), jnp.float32)
        value_total = jnp.zeros((row_in.shape[0], head_dim), jnp.float32)
        for g in range(group):
            head = j * group + g
            cols = pl.ds(head * head_dim, head_dim)
            scores = dot_nt(queries[:, cols], keys[:, kv_cols]) * scale + bias[...]
            probs = jnp.exp(scores - log_total[:, head : head + 1])
            grad_context = context_grad[:, cols]
            grad_probs = dot_nt(grad_context, values_half[:, kv_cols])
            delta = jnp.sum(
                grad_context.astype(jnp.float32) * context[:, cols].astype(jnp.float32),
                axis=-1,
                keepdims=True,
            )
            grad_scores = (probs * (grad_probs - delta) * scale).astype(jnp.bfloat16)
            grad_query, terms = raw_grad(
                matmul(grad_scores, keys[:, kv_cols]), query_raw[:, cols], q_gain[...]
            )
            raw_half[:, cols] = grad_query
            q_sum = q_sum + terms
            key_total = key_total + dot_tn(grad_scores, queries[:, cols])
            value_total = value_total + dot_tn(probs.astype(jnp.bfloat16), grad_context)
        grad_key, terms = raw_grad(key_total, key_raw[:, kv_cols], k_gain[...])
        raw_half[:, pl.ds(q_cols + j * head_dim, head_dim)] = grad_key
        k_sum = k_sum + terms
        raw_half[:, pl.ds(q_cols + kv_width + j * head_dim, head_dim)] = value_total.astype(
            jnp.bfloat16
        )
        if j < DEPTH:
            core_stage("o", j)
    gathering[0, 2:3, :head_dim] = q_sum
    gathering[0, 3:4, :head_dim] = k_sum
    for j in range(kv_heads, DEPTH):
        core_stage("o", j)
    finish_own(loads[1:])

    def project(token_rows, target):
        @pl.loop(0, width // TILE)
        def _(index):
            cols = band(index, TILE)
            total = dot_nt(raw_half[token_rows, :], full[cols, qkv_span])
            partial[token_rows, cols] = total
            if target is not None:
                target[:, cols] = total.astype(target.dtype)

    project(given, outgoing)
    swap = mail.send(outgoing, incoming, other)
    project(kept, None)
    y_stage("o", 0)
    for i in range(DEPTH):

        @pl.loop(0, quarter // TILE)
        def _(index, i=i):
            cols = pl.ds(pl.multiple_of(order[i] * quarter + index * TILE, TILE), TILE)
            full[cols, qkv_span] = matmul(flipped[cols, :], raw_half[...]).astype(jnp.bfloat16)

        core_sends("qkv", i)
        if i > 0:
            core_stage("qkv", i - 1)
    core_stage("qkv", DEPTH - 1)
    y_stage("o", 1)
    swap.wait_recv()
    grad_norm = partial[kept, :] + incoming[...].astype(jnp.float32)
    values = row_in[kept, :].astype(jnp.float32)
    inv_rms = lax.rsqrt(jnp.mean(values * values, axis=-1, keepdims=True) + EPSILON)
    grad_values, _ = norm_back(grad_norm, values, inv_rms, gain_one[...])
    o_i[kept, :] = (grad_mid[...] + grad_values).astype(jnp.bfloat16)
    swap_back = mail.send(o_i.at[kept], o_i.at[kept], other)

    values = row_in[...].astype(jnp.float32)
    inv_rms = lax.rsqrt(jnp.mean(values * values, axis=-1, keepdims=True) + EPSILON)
    gathering[0, 0:1, :] = jnp.sum(partial[...] * values * inv_rms, axis=0, keepdims=True)
    gathering[0, 1:2, :] = t_m[...]
    exchange = mail.send(gathering.at[0], arriving.at[0], pairs[0])

    def pair_step(step):
        total = gathering[step] + arriving[step]
        if step + 1 < len(pairs):
            gathering[step + 1] = total
            return mail.send(gathering.at[step + 1], arriving.at[step + 1], pairs[step + 1])
        sums[...] = total
        return None

    y_stage("o", 2)
    y_stage("o", 3)
    for step in range(len(pairs)):
        exchange.wait_recv()
        exchange = pair_step(step)
        if step < DEPTH:
            y_stage("qkv", step)
        if step == 1:
            finish_line("o")
    for k in range(DEPTH):
        if k > 0:
            to_z[k].wait_recv()
        for i, out in enumerate((d_g, d_u, d_d)):
            span = pl.ds(i * part, part)
            share = shares[z, :, span] if k == 0 else from_spread[k - 1, :, span]
            out[:, band(at.z_off(-k), part)] = share.astype(jnp.float32)
    finish_line("qkv")
    receive([swap_l, swap_back])
    mail.finish()


def backward(dp_size, shares, weights, cols, grad_mid, mid_half, out_half, gain_terms, saved, gains):
    wide = dp_size // (DEPTH * CORES)
    tokens, width = grad_mid.shape
    seq_len = HALVES * tokens
    part = shares.shape[2] // 3
    rows = width // dp_size
    half, full = jnp.bfloat16, jnp.float32
    every = sum(cols)
    pairs = 4 + wide.bit_length() - 1
    copies = 3 + 3 + 2 * LineReduce.slots + 2 * DEPTH * (2 * wide - 1) + pairs
    shapes = [jax.ShapeDtypeStruct((seq_len, width), half)] * 2
    shapes += [jax.ShapeDtypeStruct((8, width), full)]
    shapes += [jax.ShapeDtypeStruct((rows, col), full) for col in cols]
    shapes += [jax.ShapeDtypeStruct((rows, part * DEPTH), full)] * 3
    inputs = [grad_mid, mid_half, out_half, gain_terms, gains[0], *saved, *gains[2:]]
    return pl.pallas_call(
        functools.partial(backward_kernel, dp_size),
        out_shape=shapes,
        in_specs=[VMEM, ANY] + [VMEM] * len(inputs),
        out_specs=[VMEM] * 10,
        scratch_shapes=[
            pltpu.VMEM((width, every), half),
            pltpu.VMEM((DEPTH, wide, rows, every), half),
            pltpu.VMEM((wide - 1, DEPTH, rows, every), half),
            pltpu.VMEM((LineReduce.slots, rows, every), half),
            pltpu.VMEM((DEPTH - 1, rows, 3 * part), half),
            pltpu.VMEM((seq_len, cols[0]), half),
            pltpu.VMEM((seq_len, every - cols[3]), half),
            pltpu.VMEM((width, seq_len), half),
            pltpu.VMEM((seq_len, width), full),
            pltpu.VMEM((tokens, width), half),
            pltpu.VMEM((tokens, width), half),
            pltpu.VMEM((pairs, 8, width), full),
            pltpu.VMEM((pairs, 8, width), full),
            pltpu.SemaphoreType.DMA((2,)),
            pltpu.SemaphoreType.DMA((copies,)),
            pltpu.SemaphoreType.DMA((copies,)),
        ],
        compiler_params=pltpu.CompilerParams(
            collective_id=2, has_side_effects=True, vmem_limit_bytes=63 * 2**20
        ),
    )(shares, weights, *inputs)


def body(
    dp_size,
    layer_in,
    seg_ids,
    w_q,
    w_k,
    w_v,
    w_o,
    w_gate,
    w_up,
    w_down,
    attn_gain,
    mlp_gain,
    q_gain,
    k_gain,
    cotangent,
):
    row_in = layer_in[0]
    row_cot = cotangent[0]
    width = row_in.shape[1]
    gains = [gain[None, :] for gain in (attn_gain, mlp_gain, q_gain, k_gain)]
    outs = forward(
        dp_size, (w_q, w_k, w_v, w_o, w_gate, w_up, w_down), row_cot, row_in, seg_ids[0], gains
    )
    attn_full, ffn_full, cots, normed, mid = outs[:5]
    saved = outs[5:]
    outs = mlp(
        dp_size, ffn_full, normed.reshape(-1, width), cots.reshape(-1, width), mid, row_cot, gains[1]
    )
    grad_mid, mid_half, out_half, gain_terms, shares = outs
    cols = [weight.shape[1] for weight in (w_q, w_k, w_v, w_o)]
    outs = backward(
        dp_size, shares, attn_full, cols, grad_mid, mid_half, out_half, gain_terms,
        [row_in] + list(saved), gains,
    )
    out_row, in_grad, sums = outs[:3]
    gain_outs = []
    for i, size in enumerate((width, width, q_gain.shape[0], k_gain.shape[0])):
        share = size // dp_size
        gain_outs.append(lax.dynamic_slice(sums[i], (lax.axis_index("dp") * share,), (share,)))
    return (out_row[None], in_grad[None], *outs[3:], *gain_outs)


def solution(mesh):
    return jax.shard_map(
        functools.partial(body, mesh.shape["dp"]),
        mesh=mesh,
        in_specs=(
            P("dp", None, None),
            P("dp", None),
            P("dp", "mp"),
            P("dp", "mp"),
            P("dp", "mp"),
            P("dp", "mp"),
            P("dp", "mp"),
            P("dp", "mp"),
            P("dp", "mp"),
            P(),
            P(),
            P(),
            P(),
            P("dp", None, None),
        ),
        out_specs=(
            P("dp", None, None),
            P("dp", None, None),
            P("dp", "mp"),
            P("dp", "mp"),
            P("dp", "mp"),
            P("dp", "mp"),
            P("dp", "mp"),
            P("dp", "mp"),
            P("dp", "mp"),
            P("dp"),
            P("dp"),
            P("dp"),
            P("dp"),
        ),
        check_vma=False,
    )
```

time: 1940 us -> 481 us (0.25)
  waiting for transfers between devices: 1630 us -> 0 us
  Pallas kernels: 0 us -> 455 us
  matrix products: 149 us -> 0 us
  blocking collectives: 67.4 us -> 0 us
  other arithmetic: 29.2 us -> 0 us
  local copies, waits for them, and re-layouts: 34.9 us -> 15.3 us
    reduce_scatter x7 -> x0, waiting for transfers between devices: 1040 us -> none  [the longest x1 249 us: body(): lax.psum_scatter(totals[4], 'dp', scatter_dimension=0, tiled=True)]
    pallas_call x0 -> x3, Pallas kernels: none -> 455 us  [the longest x1 207 us: forward(): pl.pallas_call(functools.partial(forward_kernel, dp_size), out_shape=shap...]
    all_gather x7 -> x0, waiting for transfers between devices: 434 us -> none  [the longest x1 98.2 us: body(): full_gate = lax.all_gather(w_gate, 'dp', axis=0, tiled=True)]
    psum x3 -> x0, waiting for transfers between devices: 154 us -> none  [the longest x1 59 us: body(): attn_out = lax.psum(matmul(context_half, full_o.T), 'mp')]
    dot_general x27 -> x0, matrix products: 149 us -> none  [the longest x21 140 us: matmul(): return jnp.dot(left_op, right_op, preferred_element_type=jnp.float32)]
    unnamed x1 -> x0, blocking collectives: 61.9 us -> none
  transfers between devices with their start and end apart: 17 -> 0, of which waited for: 17 -> 0; matrix products, arithmetic and copies ran while one was open for 7% -> 0% of each run, Pallas kernels for 0% -> 0%
where the time goes in v3:
time: 481 us; the launch traced here: 472 us
  Pallas kernels  455 us (95%)
  local copies, waits for them, and re-layouts  15.3 us (3%)
    pallas_call x1, Pallas kernels, forward(): pl.pallas_call(functools.partial(forward_kernel, dp_size), out_shape=shap...  207 us
    pallas_call x1, Pallas kernels, backward(): pl.pallas_call(functools.partial(backward_kernel, dp_size), out_shape=sha...  131 us
    pallas_call x1, Pallas kernels, mlp(): pl.pallas_call(functools.partial(mlp_kernel, dp_size), out_shape=shapes,...  118 us
    unnamed x25, local copies, waits for them, and re-layouts  11.7 us

profile of v3, /device:TPU:0, one launch (start us, length us, event | category | flops | bytes accessed | tf_op | source)
XLA Modules:
  0.0 471.7 jit_solution(1577873409973742315)
XLA Ops:
  0.6 1.5 copy.27.seg_col
  2.1 206.6 %shard_map.237 = (bf16[2048,3072]{1,0:T(8,128)(2,1)}, bf16[2048,2304]{1,0:T(8,128)(2,1)}, bf16[4,2,128,2048]{3,2,1,0:T(8,128)(2,1)}, bf16[4,2,128,2048]{3,2,1,0:...) custom-call(bf16[128,1024]{1,0:T(8,128)(2,1)} %w_q.1, ...), custom_call_target="tpu_custom_call" | custom-call | tf_op jit(solution)/shard_map/pallas_call | solution.py:544
  208.7 118.1 %shard_map.238 = (f32[128,2048]{1,0:T(8,128)}, bf16[256,2048]{1,0:T(8,128)(2,1)}, f32[128,2048]{1,0:T(8,128)}, f32[1,2048]{1,0:T(1,128)}, bf16[4,128,2304]{2,1,0:T(8,128)(2,1)}) custom-call(bf16[2048,2304]{1,0:T(8,128)(2,1)} %get-tuple-element.44.weights, bf16[1024,2048]{1,0:T(8,128)(2,1)} %bitcast.22, bf16[1024,2048]{1,0:T(8,128)(2,1)} %bitcast.21, ...), custom_call_target="tpu_custom_call" | custom-call | tf_op jit(solution)/shard_map/pallas_call | solution.py:753
  326.8 130.6 %shard_map.239 = (bf16[256,2048]{1,0:T(8,128)(2,1)}, bf16[256,2048]{1,0:T(8,128)(2,1)}, f32[8,2048]{1,0:T(8,128)}, f32[128,1024]{1,0:T(8,128)}, f32[128,512]{1,0...) custom-call(bf16[4,128,2304]{2,1,0:T(8,128)(2,1)} %get-tuple-element, ...), custom_call_target="tpu_custom_call" | custom-call | tf_op jit(solution)/shard_map/pallas_call | solution.py:1044
  457.4 0.0 copy-start.3
  457.4 1.1 fusion.4
  458.4 0.6 fusion.2
  459.0 0.5 fusion
  459.6 2.3 copy.37
  461.9 0.0 copy-done.3
  461.9 0.0 copy-start.5
  461.9 0.0 copy-start.7
  461.9 0.0 copy-start.6
  461.9 0.0 copy-start.4
  461.9 1.0 copy.38
  462.9 0.3 copy-done.5
  463.2 0.0 copy-start.2
  463.2 0.8 copy.39
  464.0 0.0 copy-done.7
  464.0 0.7 copy.40
  464.7 0.0 copy-done.6
  464.7 0.7 copy.41
  465.4 0.0 copy-done.4
  465.4 0.8 copy.42
  466.2 0.0 copy-done.2
  466.2 0.0 copy-start.1
  466.2 1.1 copy.43
  467.3 0.8 copy-done.1
  468.2 0.0 copy-start
  468.2 1.1 copy.44
  469.3 0.8 copy-done
  470.1 1.1 copy.45
Async XLA Ops:
  457.4 4.5 copy-start.3
  461.9 1.3 copy-start.5
  461.9 2.1 copy-start.7
  461.9 2.8 copy-start.6
  461.9 3.5 copy-start.4
  463.2 3.0 copy-start.2
  466.2 2.0 copy-start.1
  468.2 2.0 copy-start

commit v4 on v3

--- a/solution.py
+++ b/solution.py
@@ -62,6 +62,12 @@
 
     def z_off(self, step):
         return lax.rem(self.z + DEPTH + step, jnp.int32(DEPTH))
+
+    def z_flip(self, bits):
+        z = self.z
+        if bits == DEPTH - 1:
+            return DEPTH - 1 - z
+        return z + bits - 2 * bits * lax.rem(lax.div(z, jnp.int32(bits)), jnp.int32(2))
 
     def y_off(self, step):
         return lax.rem(self.y + self.wide + step, jnp.int32(self.wide))
@@ -340,7 +346,7 @@
     o_attn, o_ffn, o_c, o_n,
     mid, normed_one, query_raw, key_raw, values_half, queries, keys, context, log_total,
     cosine, sine, bias,
-    full, outgoing, incoming, normed, own_sems, send_sems, recv_sems,
+    full, own_part, outgoing, incoming, normed, own_sems, send_sems, recv_sems,
 ):
     at = Place(dp_size)
     z, y, c, x = at.z, at.y, at.c, at.x
@@ -372,11 +378,9 @@
         own_sems,
     )
     own_ffn = own_copies(
-        [(weight.at[:, columns(z)], o_ffn.at[here, span]) for weight, span in ffn]
-        + [(cot.at[half_rows(i)], o_c.at[z, i]) for i in range(2)],
-        own_sems,
-        4,
-    )
+        [(weight.at[:, columns(z)], own_part.at[:, span]) for weight, span in ffn], own_sems, 4
+    )
+    own_cot = own_copies([(cot.at[half_rows(i)], o_c.at[z, i]) for i in range(2)], own_sems, 7)
     finish_own(mine)
     attn = LineGather(
         mail,
@@ -397,20 +401,21 @@
 
     def start_spread():
         for k in range(1, DEPTH):
-            target = at.z_off(k)
+            target = at.z_flip(k)
             spread[k] = [
-                mail.send(weight.at[:, columns(target)], o_ffn.at[here, span], z_peers[k - 1])
+                mail.send(
+                    weight.at[:, columns(target)], o_ffn.at[here, span], at.device(z=target)
+                )
                 for weight, span in ffn
             ]
-        finish_own(own_ffn)
         block = o_ffn.at[here]
         for j in range(1, at.wide):
-            crossing[0, j] = mail.send(block, block, y_peers[j - 1])
-        to_sibling.append(mail.send(block, block, sibling))
+            crossing[0, j] = mail.send(own_part, block, y_peers[j - 1])
+        to_sibling.append(mail.send(own_part, block, sibling))
 
     def forward_spread(k):
         receive(spread[k])
-        block = o_ffn.at[at.rows(at.z_off(-k), y, c, rows)]
+        block = o_ffn.at[at.rows(at.z_flip(k), y, c, rows)]
         for j in range(1, at.wide):
             crossing[k, j] = mail.send(block, block, y_peers[j - 1])
         to_sibling.append(mail.send(block, block, sibling))
@@ -418,22 +423,26 @@
     def forward_crossing(k):
         for j in range(1, at.wide):
             crossing[k, j].wait_recv()
-            block = o_ffn.at[at.rows(at.z_off(-k), at.y_off(-j), c, rows)]
+            block = o_ffn.at[at.rows(at.z_flip(k), at.y_off(-j), c, rows)]
             to_sibling.append(mail.send(block, block, sibling))
 
     def half_place(out):
         return lambda zb, j: [out.at[zb, x if j == 0 else 1 - x]]
 
     attn.step(0)
+    finish_own(own_ffn)
+    own_copy = own_copies([(own_part, o_ffn.at[here])], own_sems, 4)
     attn.side_step("own")
     attn.step(1)
-    start_spread()
+    cots = LineGather(
+        mail, at, (cot.at[half_rows(x)],), half_place(o_c), [other], share_own=False
+    )
     attn.side_steps(0)
     attn.step(2)
-    cots = LineGather(
-        mail, at, (cot.at[half_rows(x)],), half_place(o_c), [other], share_own=False
-    )
+    cots.step(0)
     attn.side_steps(1)
+    cots.step(1)
+    start_spread()
     attn.side_steps(2)
     attn.finish()
     saved = own_copies([(full, o_attn)], own_sems)
@@ -450,8 +459,6 @@
     matmul_tiles(normed_one, full.at[:, q_span], write_query)
     matmul_tiles(normed_one, full.at[:, k_span], write_key)
     matmul_tiles(normed_one, full.at[:, v_span], write_value)
-    cots.step(0)
-    forward_spread(1)
 
     def rotated(raw, gain):
         unit, _ = rms_norm(raw, gain)
@@ -475,8 +482,7 @@
             probs = (weights * (1.0 / total)).astype(jnp.bfloat16)
             context[:, cols] = matmul(probs, values_half[:, kv_cols]).astype(jnp.bfloat16)
         if j == kv_heads // 2 - 1:
-            cots.step(1)
-            forward_spread(3)
+            cots.step(2)
 
     given, kept = half_rows(1 - x), half_rows(x)
     width = row_in.shape[1]
@@ -491,31 +497,42 @@
     project(given, outgoing)
     swap = mail.send(outgoing, incoming, other)
     project(kept, mid)
-    forward_spread(2)
-    cots.step(2)
     swap.wait_recv()
     total = row_in[kept, :].astype(jnp.float32) + (mid[...] + incoming[...].astype(jnp.float32))
     mid[...] = total
     normed_mid, _ = rms_norm(total, gain_two[...])
     normed[...] = normed_mid.astype(jnp.bfloat16)
     last = own_copies([(normed, o_n.at[z, x])], own_sems, 9)
-    norms = LineGather(mail, at, (normed,), half_place(o_n), [other])
-    cots.side_steps(0)
+    strip = tokens // 2
+    norms = []
+    for i in range(2):
+        rows_of = pl.ds(i * strip, strip)
+        norms.append(
+            LineGather(
+                mail,
+                at,
+                (normed.at[rows_of],),
+                lambda zb, j, rows_of=rows_of: [o_n.at[zb, x if j == 0 else 1 - x, rows_of]],
+                [other],
+            )
+        )
+    forward_spread(1)
     forward_crossing(0)
-    norms.step(0)
-    forward_crossing(1)
-    norms.step(1)
-    forward_crossing(3)
-    cots.side_steps(1)
-    norms.step(2)
-    forward_crossing(2)
-    cots.side_steps(2)
-    norms.side_step("own")
     for step in range(DEPTH - 1):
-        norms.side_steps(step)
+        if step < DEPTH - 2:
+            forward_spread(step + 2)
+        for line in norms:
+            line.step(step)
+        forward_crossing(step + 1)
+    for step in range(DEPTH - 1):
+        cots.side_steps(step)
+    for line in norms:
+        line.side_step("own")
+        for step in range(DEPTH - 1):
+            line.side_steps(step)
     receive(to_sibling)
     mail.finish()
-    finish_own(saved + last)
+    finish_own(saved + last + own_cot + own_copy)
 
 
 def forward(dp_size, weights, cot, row_in, seg_row, gains):
@@ -539,14 +556,15 @@
     shapes.insert(4, jax.ShapeDtypeStruct((tokens, width), whole))
     hops = 2 * (DEPTH - 1)
     spots = 1 + hops
-    copies = (hops + spots * (2 * wide - 1)) + 2 * (2 * hops + 1) + 1
+    copies = (hops + spots * (2 * wide - 1)) + 3 * (2 * hops + 1) + 1
     copies += 9 + DEPTH * (2 * wide - 1)
     return pl.pallas_call(
         functools.partial(forward_kernel, dp_size),
         out_shape=shapes,
-        in_specs=[ANY] * 8 + [VMEM] * 7,
+        in_specs=[ANY] * 7 + [VMEM] * 8,
         out_specs=[ANY] * 4 + [VMEM] * 12,
         scratch_shapes=[pltpu.VMEM((width, sum(attn_cols)), half)]
+        + [pltpu.VMEM((w_g.shape[0], 3 * part), half)]
         + [pltpu.VMEM((tokens, width), half)] * 3
         + [
             pltpu.SemaphoreType.DMA((10,)),
@@ -562,7 +580,7 @@
 def mlp_kernel(
     dp_size, weights, n_all, c_all, mid, cot, gain,
     o_m, o_h, o_l, o_t, shares,
-    full, x_n, x_c, hidden, p_n, p_o, h_n, h_o, l_n, l_o, from_core, from_y,
+    full, x_n, x_c, hidden, p_n, p_o, h_n, h_o, h_l, l_n, l_o, l_z, outgoing, from_core, from_y,
     own_sems, send_sems, recv_sems,
 ):
     at = Place(dp_size)
@@ -599,11 +617,15 @@
     def half_rows(index, side):
         return band(index * HALVES + side, tokens)
 
+    first, second = pl.ds(0, width // 2), pl.ds(width // 2, width // 2)
     norm_line = LineReduce(
         mail, at, 1, lambda index: [p_n.at[half_rows(index, x)]], lambda slot: [l_n.at[slot]]
     )
     out_line = LineReduce(
-        mail, at, 1, lambda index: [p_o.at[half_rows(index, x)]], lambda slot: [l_o.at[slot]]
+        mail, at, 1, lambda index: [p_o.at[half_rows(index, x), first]], lambda slot: [l_o.at[slot]]
+    )
+    late_line = LineReduce(
+        mail, at, 1, lambda index: [p_o.at[band(index, block_rows), second]], lambda slot: [l_z.at[slot]]
     )
     norm_swaps, out_swaps = [], []
 
@@ -638,70 +660,94 @@
 
         norm_swaps.append(mail.send(p_n.at[half_rows(order[i], 1 - x)], h_n.at[i], other))
 
+    def compute_out(i):
+        block = band(order[i], block_rows)
+
         @pl.loop(0, width // TILE)
         def _(index):
             cols = band(index, TILE)
             p_o[block, cols] = dot_nt(hidden[block, down], full[cols, down]).astype(jnp.bfloat16)
 
-    def reduce_step(line, partial, swaps, landed, i):
-        swaps[i].wait_recv()
-        add_into(partial.at[half_rows(order[i], x)], landed.at[i])
-        line.pass_on(i)
-
-    def weight_grads(i):
+    def norm_step(i):
+        norm_swaps[i].wait_recv()
+        add_into(p_n.at[half_rows(order[i], x)], h_n.at[i])
+        norm_line.pass_on(i)
+
+    def out_step(i):
+        out_swaps[i].wait_recv()
+        add_into(p_o.at[half_rows(order[i], x), first], h_o.at[i])
+        out_line.pass_on(i)
+
+    def weight_grads(span, i):
+        left = x_n if span is gate_up else x_c
+
         @pl.loop(0, width // DEPTH // TILE)
         def _(index):
             cols = pl.ds(pl.multiple_of(order[i] * (width // DEPTH) + index * TILE, TILE), TILE)
-            full[cols, gate_up] = matmul(x_n[:, cols].T, hidden[:, gate_up]).astype(jnp.bfloat16)
-            full[cols, down] = matmul(x_c[:, cols].T, hidden[:, down]).astype(jnp.bfloat16)
-
-        return [
+            full[cols, span] = matmul(left[:, cols].T, hidden[:, span]).astype(jnp.bfloat16)
+
+        to_core[span.start, i] = [
             mail.send(
-                full.at[at.rows(order[i], side, 1 - c, rows)], from_core.at[order[i], side], sibling
+                full.at[at.rows(order[i], side, 1 - c, rows), span],
+                from_core.at[order[i], side, :, span],
+                sibling,
             )
             for side in range(at.wide)
         ]
 
     to_core, to_y = {}, {}
 
-    def core_stage(i):
-        receive(to_core[i])
+    def core_stage(span, i):
+        receive(to_core[span.start, i])
         for side in range(at.wide):
-            add_into(full.at[at.rows(order[i], side, c, rows)], from_core.at[order[i], side])
-        to_y[i] = [
+            add_into(
+                full.at[at.rows(order[i], side, c, rows), span], from_core.at[order[i], side, :, span]
+            )
+        to_y[span.start, i] = [
             mail.send(
-                full.at[at.rows(order[i], at.y_off(j), c, rows)],
-                from_y.at[j - 1, order[i]],
+                full.at[at.rows(order[i], at.y_off(j), c, rows), span],
+                from_y.at[j - 1, order[i], :, span],
                 y_peers[j - 1],
             )
             for j in range(1, at.wide)
         ]
 
-    def y_stage(i):
-        receive(to_y[i])
-        total = full[at.rows(order[i], y, c, rows), :].astype(jnp.float32)
+    def y_stage(span, i):
+        receive(to_y[span.start, i])
+        total = full[at.rows(order[i], y, c, rows), span].astype(jnp.float32)
         for j in range(1, at.wide):
-            total = total + from_y[j - 1, order[i]].astype(jnp.float32)
-        shares[order[i]] = total.astype(jnp.bfloat16)
+            total = total + from_y[j - 1, order[i], :, span].astype(jnp.float32)
+        shares[order[i], :, span] = total.astype(jnp.bfloat16)
 
     compute(0)
     compute(1)
-    reduce_step(norm_line, p_n, norm_swaps, h_n, 0)
     compute(2)
+    norm_step(0)
     compute(3)
-    reduce_step(norm_line, p_n, norm_swaps, h_n, 1)
-    to_core[0] = weight_grads(0)
-    to_core[1] = weight_grads(1)
-    core_stage(0)
-    reduce_step(norm_line, p_n, norm_swaps, h_n, 2)
-    to_core[2] = weight_grads(2)
-    core_stage(1)
-    to_core[3] = weight_grads(3)
-    core_stage(2)
+    weight_grads(gate_up, 0)
+    norm_step(1)
+    weight_grads(gate_up, 1)
+    core_stage(gate_up, 0)
+    weight_grads(gate_up, 2)
+    core_stage(gate_up, 1)
+    norm_step(2)
+    weight_grads(gate_up, 3)
+    core_stage(gate_up, 2)
+    compute_out(0)
+    late_line.pass_on(0)
+    core_stage(gate_up, 3)
+    compute_out(1)
+    late_line.pass_on(1)
+    compute_out(2)
+    compute_out(3)
     norm_swaps[3].wait_recv()
     for i in range(DEPTH):
-        out_swaps.append(mail.send(p_o.at[half_rows(order[i], 1 - x)], h_o.at[i], other))
-    core_stage(3)
+        out_swaps.append(
+            mail.send(p_o.at[half_rows(order[i], 1 - x), first], h_o.at[i], other)
+        )
+    weight_grads(down, 0)
+    weight_grads(down, 1)
+    core_stage(down, 0)
     o_m[...] = p_n[half_rows(z, x), :].astype(jnp.float32) + h_n[3].astype(jnp.float32)
 
     def add_norm(_, landed):
@@ -718,19 +764,40 @@
     o_m[...] = total
     o_h[kept, :] = total.astype(jnp.bfloat16)
     swap_h = mail.send(o_h.at[kept], o_h.at[kept], other)
+    late_line.pass_on(2)
+    weight_grads(down, 2)
+    core_stage(down, 1)
+    weight_grads(down, 3)
+    core_stage(down, 2)
+    core_stage(down, 3)
     for i in range(DEPTH - 1):
-        reduce_step(out_line, p_o, out_swaps, h_o, i)
-        y_stage(i)
-    y_stage(DEPTH - 1)
+        out_step(i)
+        y_stage(gate_up, i)
+
+    def add_late(_, landed):
+        for i in range(HALVES):
+            rows_of = band(z * HALVES + i, tokens)
+            add_into(p_o.at[rows_of, second], landed.at[pl.ds(i * tokens, tokens)])
+
+    late_line.last(add_late)
+    outgoing[...] = p_o[half_rows(z, 1 - x), second]
+    swap_l = mail.send(outgoing, h_l, other)
+    y_stage(gate_up, DEPTH - 1)
+    for i in range(DEPTH):
+        y_stage(down, i)
     out_swaps[3].wait_recv()
-    o_l[...] = mid[...] + (
-        p_o[half_rows(z, x), :].astype(jnp.float32) + h_o[3].astype(jnp.float32)
+    o_l[:, first] = mid[:, first] + (
+        p_o[half_rows(z, x), first].astype(jnp.float32) + h_o[3].astype(jnp.float32)
     )
 
     def add_out(_, landed):
-        o_l[...] = o_l[...] + landed[...].astype(jnp.float32)
+        o_l[:, first] = o_l[:, first] + landed[...].astype(jnp.float32)
 
     out_line.last(add_out)
+    swap_l.wait_recv()
+    o_l[:, second] = mid[:, second] + (
+        p_o[half_rows(z, x), second].astype(jnp.float32) + h_l[...].astype(jnp.float32)
+    )
     swap_h.wait_recv()
     mail.finish()
 
@@ -742,7 +809,7 @@
     rows = width // dp_size
     every = DEPTH * HALVES * tokens
     half, full = jnp.bfloat16, jnp.float32
-    copies = 2 * LineReduce.slots + 2 * DEPTH + DEPTH * (2 * wide - 1) + 1
+    copies = 3 * LineReduce.slots + 2 * DEPTH + 2 * DEPTH * (2 * wide - 1) + 2
     shapes = [
         jax.ShapeDtypeStruct((tokens, width), full),
         jax.ShapeDtypeStruct((HALVES * tokens, width), half),
@@ -759,8 +826,15 @@
         + [pltpu.VMEM((every, width), half)] * 2
         + [pltpu.VMEM((every, cols), half)]
         + [pltpu.VMEM((every, width), half)] * 2
-        + [pltpu.VMEM((DEPTH, tokens, width), half)] * 2
-        + [pltpu.VMEM((LineReduce.slots, tokens, width), half)] * 2
+        + [
+            pltpu.VMEM((DEPTH, tokens, width), half),
+            pltpu.VMEM((DEPTH, tokens, width // 2), half),
+            pltpu.VMEM((tokens, width // 2), half),
+            pltpu.VMEM((LineReduce.slots, tokens, width), half),
+            pltpu.VMEM((LineReduce.slots, tokens, width // 2), half),
+            pltpu.VMEM((LineReduce.slots, HALVES * tokens, width // 2), half),
+            pltpu.VMEM((tokens, width // 2), half),
+        ]
         + [
             pltpu.VMEM((DEPTH, wide, rows, cols), half),
             pltpu.VMEM((wide - 1, DEPTH, rows, cols), half),
@@ -970,6 +1044,28 @@
     project(given, outgoing)
     swap = mail.send(outgoing, incoming, other)
     project(kept, None)
+
+    values = row_in[...].astype(jnp.float32)
+    inv_rms = lax.rsqrt(jnp.mean(values * values, axis=-1, keepdims=True) + EPSILON)
+    gathering[0, 0:1, :] = jnp.sum(partial[...] * values * inv_rms, axis=0, keepdims=True)
+    gathering[0, 1:2, :] = t_m[...]
+    exchange = [mail.send(gathering.at[0], arriving.at[0], pairs[0])]
+
+    def pair_step():
+        step = len(exchange) - 1
+        if step == len(pairs):
+            return
+        exchange[step].wait_recv()
+        total = gathering[step] + arriving[step]
+        if step + 1 < len(pairs):
+            gathering[step + 1] = total
+            exchange.append(
+                mail.send(gathering.at[step + 1], arriving.at[step + 1], pairs[step + 1])
+            )
+        else:
+            sums[...] = total
+            exchange.append(None)
+
     y_stage("o", 0)
     for i in range(DEPTH):
 
@@ -979,10 +1075,13 @@
             full[cols, qkv_span] = matmul(flipped[cols, :], raw_half[...]).astype(jnp.bfloat16)
 
         core_sends("qkv", i)
-        if i > 0:
+        if i == 0:
+            pair_step()
+        else:
             core_stage("qkv", i - 1)
     core_stage("qkv", DEPTH - 1)
     y_stage("o", 1)
+    pair_step()
     swap.wait_recv()
     grad_norm = partial[kept, :] + incoming[...].astype(jnp.float32)
     values = row_in[kept, :].astype(jnp.float32)
@@ -991,29 +1090,16 @@
     o_i[kept, :] = (grad_mid[...] + grad_values).astype(jnp.bfloat16)
     swap_back = mail.send(o_i.at[kept], o_i.at[kept], other)
 
-    values = row_in[...].astype(jnp.float32)
-    inv_rms = lax.rsqrt(jnp.mean(values * values, axis=-1, keepdims=True) + EPSILON)
-    gathering[0, 0:1, :] = jnp.sum(partial[...] * values * inv_rms, axis=0, keepdims=True)
-    gathering[0, 1:2, :] = t_m[...]
-    exchange = mail.send(gathering.at[0], arriving.at[0], pairs[0])
-
-    def pair_step(step):
-        total = gathering[step] + arriving[step]
-        if step + 1 < len(pairs):
-            gathering[step + 1] = total
-            return mail.send(gathering.at[step + 1], arriving.at[step + 1], pairs[step + 1])
-        sums[...] = total
-        return None
-
     y_stage("o", 2)
     y_stage("o", 3)
-    for step in range(len(pairs)):
-        exchange.wait_recv()
-        exchange = pair_step(step)
-        if step < DEPTH:
-            y_stage("qkv", step)
-        if step == 1:
-            finish_line("o")
+    for i in range(DEPTH - 1):
+        y_stage("qkv", i)
+        if i > 0:
+            pair_step()
+    finish_line("o")
+    y_stage("qkv", DEPTH - 1)
+    while exchange[-1] is not None:
+        pair_step()
     for k in range(DEPTH):
         if k > 0:
             to_z[k].wait_recv()

time: 481 us -> 455 us (0.946)
  Pallas kernels: 455 us -> 431 us
    pallas_call x1, Pallas kernels: 207 us -> 182 us  [forward(): pl.pallas_call(functools.partial(forward_kernel, dp_size), out_shape=shap...]
where the time goes in v4:
time: 455 us; the launch traced here: 448 us
  Pallas kernels  431 us (95%)
  local copies, waits for them, and re-layouts  15.3 us (3%)
    pallas_call x1, Pallas kernels, forward(): pl.pallas_call(functools.partial(forward_kernel, dp_size), out_shape=shap...  182 us
    pallas_call x1, Pallas kernels, backward(): pl.pallas_call(functools.partial(backward_kernel, dp_size), out_shape=sha...  130 us
    pallas_call x1, Pallas kernels, mlp(): pl.pallas_call(functools.partial(mlp_kernel, dp_size), out_shape=shapes,...  119 us
    unnamed x25, local copies, waits for them, and re-layouts  11.7 us

profile of v4, /device:TPU:0, one launch (start us, length us, event | category | flops | bytes accessed | tf_op | source)
XLA Modules:
  0.0 447.5 jit_solution(2073460050493242619)
XLA Ops:
  0.6 1.5 copy.27.seg_col
  2.1 182.4 %shard_map.237 = (bf16[2048,3072]{1,0:T(8,128)(2,1)}, bf16[2048,2304]{1,0:T(8,128)(2,1)}, bf16[4,2,128,2048]{3,2,1,0:T(8,128)(2,1)}, bf16[4,2,128,2048]{3,2,1,0:...) custom-call(bf16[128,1024]{1,0:T(8,128)(2,1)} %w_q.1, ...), custom_call_target="tpu_custom_call" | custom-call | tf_op jit(solution)/shard_map/pallas_call | solution.py:561
  184.5 119.0 %shard_map.238 = (f32[128,2048]{1,0:T(8,128)}, bf16[256,2048]{1,0:T(8,128)(2,1)}, f32[128,2048]{1,0:T(8,128)}, f32[1,2048]{1,0:T(1,128)}, bf16[4,128,2304]{2,1,0:T(8,128)(2,1)}) custom-call(bf16[2048,2304]{1,0:T(8,128)(2,1)} %get-tuple-element.44.weights, bf16[1024,2048]{1,0:T(8,128)(2,1)} %bitcast.22, bf16[1024,2048]{1,0:T(8,128)(2,1)} %bitcast.21, ...), custom_call_target="tpu_custom_call" | custom-call | tf_op jit(solution)/shard_map/pallas_call | solution.py:820
  303.5 129.6 %shard_map.239 = (bf16[256,2048]{1,0:T(8,128)(2,1)}, bf16[256,2048]{1,0:T(8,128)(2,1)}, f32[8,2048]{1,0:T(8,128)}, f32[128,1024]{1,0:T(8,128)}, f32[128,512]{1,0...) custom-call(bf16[4,128,2304]{2,1,0:T(8,128)(2,1)} %get-tuple-element, ...), custom_call_target="tpu_custom_call" | custom-call | tf_op jit(solution)/shard_map/pallas_call | solution.py:1130
  433.2 0.0 copy-start.3
  433.2 1.1 fusion.4
  434.2 0.6 fusion.2
  434.8 0.5 fusion
  435.3 2.3 copy.37
  437.6 0.0 copy-done.3
  437.6 0.0 copy-start.5
  437.6 0.0 copy-start.7
  437.6 0.0 copy-start.6
  437.6 0.0 copy-start.4
  437.7 1.0 copy.38
  438.6 0.3 copy-done.5
  439.0 0.0 copy-start.2
  439.0 0.8 copy.39
  439.8 0.0 copy-done.7
  439.8 0.7 copy.40
  440.5 0.0 copy-done.6
  440.5 0.7 copy.41
  441.2 0.0 copy-done.4
  441.2 0.8 copy.42
  442.0 0.0 copy-done.2
  442.0 0.0 copy-start.1
  442.0 1.1 copy.43
  443.1 0.8 copy-done.1
  443.9 0.0 copy-start
  444.0 1.1 copy.44
  445.1 0.8 copy-done
  445.9 1.1 copy.45
Async XLA Ops:
  433.2 4.5 %copy-start.3 = (bf16[256,2048]{1,0:T(8,128)(2,1)S(1)}, bf16[256,2048]{1,0:T(8,128)(2,1)}, u32[]{:S(2)}) copy-start(bf16[256,2048]{1,0:T(8,128)(2,1)} %get-tuple-element.66) | copy-start | bytes 3145732
  437.6 1.3 copy-start.5
  437.6 2.1 copy-start.7
  437.6 2.8 copy-start.6
  437.6 3.5 copy-start.4
  439.0 3.0 copy-start.2
  442.0 2.0 copy-start.1
  443.9 2.0 copy-start

commit v5 on v4

--- a/solution.py
+++ b/solution.py
@@ -340,14 +340,20 @@
         write(columns, matmul(left[...], right[:, columns]))
 
 
+SAVED = 11
+
+
 def forward_kernel(
     dp_size, w_q, w_k, w_v, w_o, w_g, w_u, w_d, cot, row_in, seg_col, seg_row,
     gain_one, gain_two, q_gain, k_gain,
-    o_attn, o_ffn, o_c, o_n,
-    mid, normed_one, query_raw, key_raw, values_half, queries, keys, context, log_total,
-    cosine, sine, bias,
-    full, own_part, outgoing, incoming, normed, own_sems, send_sems, recv_sems,
+    *refs,
 ):
+    o_attn, o_ffn, o_c, o_n, o_mid = refs[:5]
+    stored, held = refs[5 : 5 + SAVED], refs[6 + SAVED : 6 + 2 * SAVED]
+    mid = refs[5 + SAVED]
+    normed_one, query_raw, key_raw, values_half, queries, keys, context, log_total = held[:8]
+    cosine, sine, bias = held[8:]
+    full, own_part, outgoing, incoming, normed, own_sems, send_sems, recv_sems = refs[6 + 2 * SAVED :]
     at = Place(dp_size)
     z, y, c, x = at.z, at.y, at.c, at.x
     sibling, other = at.device(c=1 - c), at.device(x=1 - x)
@@ -484,6 +490,7 @@
         if j == kv_heads // 2 - 1:
             cots.step(2)
 
+    saved += own_copies(list(zip(held, stored)), own_sems, 11)
     given, kept = half_rows(1 - x), half_rows(x)
     width = row_in.shape[1]
 
@@ -500,6 +507,7 @@
     swap.wait_recv()
     total = row_in[kept, :].astype(jnp.float32) + (mid[...] + incoming[...].astype(jnp.float32))
     mid[...] = total
+    saved += own_copies([(mid, o_mid)], own_sems, 10)
     normed_mid, _ = rms_norm(total, gain_two[...])
     normed[...] = normed_mid.astype(jnp.bfloat16)
     last = own_copies([(normed, o_n.at[z, x])], own_sems, 9)
@@ -562,12 +570,13 @@
         functools.partial(forward_kernel, dp_size),
         out_shape=shapes,
         in_specs=[ANY] * 7 + [VMEM] * 8,
-        out_specs=[ANY] * 4 + [VMEM] * 12,
-        scratch_shapes=[pltpu.VMEM((width, sum(attn_cols)), half)]
+        out_specs=[ANY] * (5 + SAVED),
+        scratch_shapes=[pltpu.VMEM(shape.shape, shape.dtype) for shape in shapes[4:]]
+        + [pltpu.VMEM((width, sum(attn_cols)), half)]
         + [pltpu.VMEM((w_g.shape[0], 3 * part), half)]
         + [pltpu.VMEM((tokens, width), half)] * 3
         + [
-            pltpu.SemaphoreType.DMA((10,)),
+            pltpu.SemaphoreType.DMA((11 + SAVED,)),
             pltpu.SemaphoreType.DMA((copies,)),
             pltpu.SemaphoreType.DMA((copies,)),
         ],
@@ -578,9 +587,9 @@
 
 
 def mlp_kernel(
-    dp_size, weights, n_all, c_all, mid, cot, gain,
-    o_m, o_h, o_l, o_t, shares,
-    full, x_n, x_c, hidden, p_n, p_o, h_n, h_o, h_l, l_n, l_o, l_z, outgoing, from_core, from_y,
+    dp_size, weights, n_all, c_all, a_mid, a_cot, gain,
+    a_m, a_h, a_l, o_t, a_shares,
+    mid, cot, o_m, o_h, o_l, o_b, shares, full, x_n, x_c, hidden, p_n, p_o, h_n, h_o, h_l, l_n, l_o, l_z, outgoing, from_core, from_y,
     own_sems, send_sems, recv_sems,
 ):
     at = Place(dp_size)
@@ -611,6 +620,7 @@
     for i in range(1, DEPTH):
         loads["n", i].start()
         loads["c", i].start()
+    late = own_copies([(a_mid, mid), (a_cot, cot)], own_sems, 11)
     meet([other, sibling] + at.line() + y_peers)
     mail = Mail(send_sems, recv_sems)
 
@@ -748,6 +758,7 @@
     weight_grads(down, 0)
     weight_grads(down, 1)
     core_stage(down, 0)
+    finish_own(late)
     o_m[...] = p_n[half_rows(z, x), :].astype(jnp.float32) + h_n[3].astype(jnp.float32)
 
     def add_norm(_, landed):
@@ -764,6 +775,7 @@
     o_m[...] = total
     o_h[kept, :] = total.astype(jnp.bfloat16)
     swap_h = mail.send(o_h.at[kept], o_h.at[kept], other)
+    stores = own_copies([(o_m, a_m)], own_sems, 0)
     late_line.pass_on(2)
     weight_grads(down, 2)
     core_stage(down, 1)
@@ -785,6 +797,7 @@
     y_stage(gate_up, DEPTH - 1)
     for i in range(DEPTH):
         y_stage(down, i)
+        stores.extend(own_copies([(shares.at[order[i]], a_shares.at[order[i]])], own_sems, 3 + i))
     out_swaps[3].wait_recv()
     o_l[:, first] = mid[:, first] + (
         p_o[half_rows(z, x), first].astype(jnp.float32) + h_o[3].astype(jnp.float32)
@@ -798,8 +811,12 @@
     o_l[:, second] = mid[:, second] + (
         p_o[half_rows(z, x), second].astype(jnp.float32) + h_l[...].astype(jnp.float32)
     )
+    o_b[...] = o_l[...].astype(jnp.bfloat16)
+    stores += own_copies([(o_b, a_l)], own_sems, 1)
     swap_h.wait_recv()
+    stores += own_copies([(o_h, a_h)], own_sems, 2)
     mail.finish()
+    finish_own(stores)
 
 
 def mlp(dp_size, weights, normed, cots, mid, cot, gain):
@@ -813,16 +830,25 @@
     shapes = [
         jax.ShapeDtypeStruct((tokens, width), full),
         jax.ShapeDtypeStruct((HALVES * tokens, width), half),
-        jax.ShapeDtypeStruct((tokens, width), full),
+        jax.ShapeDtypeStruct((tokens, width), half),
         jax.ShapeDtypeStruct((1, width), full),
         jax.ShapeDtypeStruct((DEPTH, rows, cols), half),
     ]
     return pl.pallas_call(
         functools.partial(mlp_kernel, dp_size),
         out_shape=shapes,
-        in_specs=[ANY] * 3 + [VMEM] * 3,
-        out_specs=[VMEM] * 5,
-        scratch_shapes=[pltpu.VMEM((width, cols), half)]
+        in_specs=[ANY] * 5 + [VMEM],
+        out_specs=[ANY] * 3 + [VMEM, ANY],
+        scratch_shapes=[
+            pltpu.VMEM((tokens, width), full),
+            pltpu.VMEM((HALVES * tokens, width), half),
+            pltpu.VMEM((tokens, width), full),
+            pltpu.VMEM((HALVES * tokens, width), half),
+            pltpu.VMEM((tokens, width), full),
+            pltpu.VMEM((tokens, width), half),
+            pltpu.VMEM((DEPTH, rows, cols), half),
+        ]
+        + [pltpu.VMEM((width, cols), half)]
         + [pltpu.VMEM((every, width), half)] * 2
         + [pltpu.VMEM((every, cols), half)]
         + [pltpu.VMEM((every, width), half)] * 2
@@ -838,7 +864,7 @@
         + [
             pltpu.VMEM((DEPTH, wide, rows, cols), half),
             pltpu.VMEM((wide - 1, DEPTH, rows, cols), half),
-            pltpu.SemaphoreType.DMA((11,)),
+            pltpu.SemaphoreType.DMA((13,)),
             pltpu.SemaphoreType.DMA((copies,)),
             pltpu.SemaphoreType.DMA((copies,)),
         ],
@@ -848,32 +874,21 @@
     )(weights, normed, cots, mid, cot, gain)
 
 
-def pair_devices(at):
-    def flip(index, bit):
-        return index + bit - 2 * bit * lax.rem(lax.div(index, jnp.int32(bit)), jnp.int32(2))
-
-    bits = [1 << i for i in range(at.wide.bit_length() - 1)]
-    return (
-        [at.device(c=1 - at.c), at.device(x=1 - at.x)]
-        + [at.device(y=flip(at.y, bit)) for bit in bits]
-        + [at.device(z=flip(at.z, bit)) for bit in (1, 2)]
-    )
-
-
 def backward_kernel(
-    dp_size, shares, weights,
-    grad_mid, mid_half, out_half, t_m, gain_one, row_in, normed_one, query_raw, key_raw,
-    values_half, queries, keys, context, log_total, cosine, sine, bias, q_gain, k_gain,
+    dp_size, shares, weights, a_mid, mid_half, a_out, t_m, gain_one, a_row, a_normed, a_query,
+    a_key, a_values, a_queries, a_keys, context, a_log, a_cosine, a_sine, a_bias, q_gain, k_gain,
     o_l, o_i, sums, d_q, d_k, d_v, d_o, d_g, d_u, d_d,
-    full, from_core, from_y, from_z, from_spread, context_grad, raw_half, flipped, partial,
-    outgoing, incoming, gathering, arriving, own_sems, send_sems, recv_sems,
+    grad_mid, out_half, row_in, normed_one, query_raw, key_raw, values_half, queries, keys,
+    log_total, cosine, sine, bias,
+    full, head_grads, gains, from_other, totals, core_o, core_h, core_s, y_o, y_h, y_s, z_o, z_h, z_s,
+    spare, context_grad, raw_half, raw_head, flipped, partial,
+    outgoing, incoming, own_sems, send_sems, recv_sems,
 ):
     at = Place(dp_size)
     z, y, c, x = at.z, at.y, at.c, at.x
     other, sibling = at.device(x=1 - x), at.device(c=1 - c)
     y_peers, z_peers = at.y_peers(), at.z_peers()
     order = at.order()
-    pairs = pair_devices(at)
     tokens, width = grad_mid.shape
     rows = d_q.shape[0]
     part = shares.shape[2] // 3
@@ -893,78 +908,101 @@
     loads = own_copies(
         [(weights.at[:, span], full.at[:, span]) for span in (o_span, qkv_span)], own_sems
     )
-    o_l[kept, :] = out_half[...].astype(jnp.bfloat16)
-    meet([other, sibling] + y_peers + z_peers + pairs)
+    late = own_copies(
+        [
+            (a_normed, normed_one), (a_query, query_raw), (a_key, key_raw), (a_values, values_half),
+            (a_queries, queries), (a_keys, keys), (a_log, log_total), (a_cosine, cosine),
+            (a_sine, sine), (a_bias, bias), (a_out, out_half), (a_mid, grad_mid), (a_row, row_in),
+        ],
+        own_sems,
+        2,
+    )
+    meet([other, sibling] + y_peers + z_peers)
     mail = Mail(send_sems, recv_sems)
-    to_z = {
-        k: mail.send(shares.at[at.z_off(k)], from_spread.at[k - 1], z_peers[k - 1])
+    ffn = [(out, pl.ds(i * part, part)) for i, out in enumerate((d_g, d_u, d_d))]
+    to_z = [
+        mail.send(
+            shares.at[at.z_off(k), :, span], out.at[:, band(z, part)], z_peers[k - 1]
+        )
         for k in (2, 1, 3)
-    }
-    swap_l = mail.send(o_l.at[kept], o_l.at[kept], other)
-    flipped[...] = normed_one[...].T
-    sets = {"o": (o_span, ((d_o, o_span),)), "qkv": (qkv_span, tuple(zip((d_q, d_k, d_v), spans)))}
-    lines = {
-        name: LineReduce(
-            mail,
-            at,
-            1,
-            lambda index, span=span: [full.at[at.rows(index, y, c, rows), span]],
-            lambda slot, span=span: [from_z.at[slot, :, span]],
+        for out, span in ffn
+    ]
+    kv_heads = key_raw.shape[1] // head_dim
+    group = query_raw.shape[1] // key_raw.shape[1]
+    q_part = group * head_dim
+
+    def block_of(zb, side, core):
+        return (zb * at.wide + side) * CORES + core
+
+    class Sums:
+        def __init__(self, held, core_land, y_land, z_land, outs):
+            self.held, self.core_land, self.y_land, self.outs = held, core_land, y_land, outs
+            self.line = LineReduce(
+                mail, at, 1, lambda zb: [held(zb, y, c)], lambda slot: [z_land.at[slot]]
+            )
+            self.to_core, self.to_y = {}, {}
+
+        def core_sends(self, i):
+            self.to_core[i] = [
+                mail.send(
+                    self.held(order[i], side, 1 - c), self.core_land.at[order[i], side], sibling
+                )
+                for side in range(at.wide)
+            ]
+
+        def core_stage(self, i):
+            receive(self.to_core[i])
+            for side in range(at.wide):
+                add_into(self.held(order[i], side, c), self.core_land.at[order[i], side])
+            self.to_y[i] = [
+                mail.send(
+                    self.held(order[i], at.y_off(j), c), self.y_land.at[j - 1, order[i]], y_peers[j - 1]
+                )
+                for j in range(1, at.wide)
+            ]
+
+        def y_stage(self, i):
+            receive(self.to_y[i])
+            terms = [self.y_land.at[j - 1, order[i]] for j in range(1, at.wide)]
+            own = self.held(order[i], y, c)
+            if i < DEPTH - 1:
+                add_into(own, *terms)
+                return
+            for out, span in self.outs:
+                out[...] = own[:, span].astype(jnp.float32)
+                add_into(out, *[term.at[:, span] for term in terms])
+
+        def finish(self):
+            def use(_, landed):
+                for out, span in self.outs:
+                    add_into(out, landed.at[:, span])
+
+            self.line.last(use)
+
+    out_sums = Sums(
+        lambda zb, side, core: full.at[at.rows(zb, side, core, rows), o_span],
+        core_o, y_o, z_o, [(d_o, pl.ds(0, d_o.shape[1]))],
+    )
+    head_sums = []
+    for j in range(kv_heads):
+        kv_cols = pl.ds(j * head_dim, head_dim)
+        head_sums.append(
+            Sums(
+                lambda zb, side, core, j=j: head_grads.at[j, at.rows(zb, side, core, rows)],
+                core_h.at[j], y_h.at[j], z_h.at[j],
+                [
+                    (d_q.at[:, pl.ds(j * q_part, q_part)], pl.ds(0, q_part)),
+                    (d_k.at[:, kv_cols], pl.ds(q_part, head_dim)),
+                    (d_v.at[:, kv_cols], pl.ds(q_part + head_dim, head_dim)),
+                ],
+            )
         )
-        for name, (span, _) in sets.items()
-    }
-    to_core, to_y = {}, {}
-
-    def core_sends(name, i):
-        span, _ = sets[name]
-        to_core[name, i] = [
-            mail.send(
-                full.at[at.rows(order[i], side, 1 - c, rows), span],
-                from_core.at[order[i], side, :, span],
-                sibling,
-            )
-            for side in range(at.wide)
-        ]
-
-    def core_stage(name, i):
-        span, _ = sets[name]
-        receive(to_core[name, i])
-        for side in range(at.wide):
-            add_into(
-                full.at[at.rows(order[i], side, c, rows), span], from_core.at[order[i], side, :, span]
-            )
-        to_y[name, i] = [
-            mail.send(
-                full.at[at.rows(order[i], at.y_off(j), c, rows), span],
-                from_y.at[j - 1, order[i], :, span],
-                y_peers[j - 1],
-            )
-            for j in range(1, at.wide)
-        ]
-
-    def y_stage(name, i):
-        span, outs = sets[name]
-        receive(to_y[name, i])
-        if i < DEPTH - 1:
-            terms = [from_y.at[j - 1, order[i], :, span] for j in range(1, at.wide)]
-            add_into(full.at[at.rows(order[i], y, c, rows), span], *terms)
-            lines[name].pass_on(i)
-            return
-        for out, own in outs:
-            out[...] = full[at.rows(z, y, c, rows), own].astype(jnp.float32)
-            add_into(out, *[from_y.at[j - 1, z, :, own] for j in range(1, at.wide)])
-
-    def finish_line(name):
-        span, outs = sets[name]
-
-        def use(_, landed):
-            for out, own in outs:
-                first = own.start - span.start
-                add_into(out, landed.at[:, pl.ds(first, own.size)])
-
-        lines[name].last(use)
-
-    gathering[...] = jnp.zeros(gathering.shape, jnp.float32)
+    gain_sums = Sums(
+        lambda zb, side, core: totals.at[block_of(zb, side, core)],
+        core_s, y_s, z_s, [(sums, pl.ds(0, sums.shape[1]))],
+    )
+
+    gains[...] = jnp.zeros(gains.shape, jnp.float32)
     loads[0].wait()
 
     def write_context(cols, value):
@@ -980,10 +1018,19 @@
             cols = pl.ds(pl.multiple_of(order[i] * quarter + index * TILE, TILE), TILE)
             full[cols, o_span] = dot_tn(mid_half[:, cols], context[...]).astype(jnp.bfloat16)
 
-        core_sends("o", i)
-
-    kv_heads = key_raw.shape[1] // head_dim
-    group = query_raw.shape[1] // key_raw.shape[1]
+        out_sums.core_sends(i)
+    own_share = own_copies([(shares.at[z], spare)], own_sems, 15)
+    for i in range(DEPTH):
+        out_sums.core_stage(i)
+    finish_own(late)
+    finish_own(own_share)
+    own_share = own_copies(
+        [(spare.at[:, span], out.at[:, band(z, part)]) for out, span in ffn], own_sems, 15
+    )
+    flipped[...] = normed_one[...].T
+    o_l[kept, :] = out_half[...]
+    swap_l = mail.send(o_l.at[kept], o_l.at[kept], other)
+
     scale = 1.0 / math.sqrt(head_dim)
 
     def raw_grad(grad, raw, gain):
@@ -992,9 +1039,9 @@
         grad_raw, terms = norm_back(back, raw, inv_rms, gain)
         return grad_raw.astype(jnp.bfloat16), jnp.sum(terms, axis=0, keepdims=True)
 
-    q_sum = jnp.zeros((1, head_dim), jnp.float32)
-    k_sum = jnp.zeros((1, head_dim), jnp.float32)
     for j in range(kv_heads):
+        q_sum = jnp.zeros((1, head_dim), jnp.float32)
+        k_sum = jnp.zeros((1, head_dim), jnp.float32)
         kv_cols = pl.ds(j * head_dim, head_dim)
         key_total = jnp.zeros((row_in.shape[0], head_dim), jnp.float32)
         value_total = jnp.zeros((row_in.shape[0], head_dim), jnp.float32)
@@ -1015,21 +1062,39 @@
                 matmul(grad_scores, keys[:, kv_cols]), query_raw[:, cols], q_gain[...]
             )
             raw_half[:, cols] = grad_query
+            raw_head[:, pl.ds(g * head_dim, head_dim)] = grad_query
             q_sum = q_sum + terms
             key_total = key_total + dot_tn(grad_scores, queries[:, cols])
             value_total = value_total + dot_tn(probs.astype(jnp.bfloat16), grad_context)
         grad_key, terms = raw_grad(key_total, key_raw[:, kv_cols], k_gain[...])
+        grad_value = value_total.astype(jnp.bfloat16)
         raw_half[:, pl.ds(q_cols + j * head_dim, head_dim)] = grad_key
+        raw_half[:, pl.ds(q_cols + kv_width + j * head_dim, head_dim)] = grad_value
+        raw_head[:, pl.ds(q_part, head_dim)] = grad_key
+        raw_head[:, pl.ds(q_part + head_dim, head_dim)] = grad_value
         k_sum = k_sum + terms
-        raw_half[:, pl.ds(q_cols + kv_width + j * head_dim, head_dim)] = value_total.astype(
-            jnp.bfloat16
-        )
-        if j < DEPTH:
-            core_stage("o", j)
-    gathering[0, 2:3, :head_dim] = q_sum
-    gathering[0, 3:4, :head_dim] = k_sum
-    for j in range(kv_heads, DEPTH):
-        core_stage("o", j)
+        gains[0, 2:3, :head_dim] = gains[0, 2:3, :head_dim] + q_sum
+        gains[0, 3:4, :head_dim] = gains[0, 3:4, :head_dim] + k_sum
+        for i in range(DEPTH):
+
+            @pl.loop(0, quarter // TILE)
+            def _(index, i=i, j=j):
+                cols = pl.ds(pl.multiple_of(order[i] * quarter + index * TILE, TILE), TILE)
+                head_grads[j, cols, :] = matmul(flipped[cols, :], raw_head[...]).astype(jnp.bfloat16)
+
+            head_sums[j].core_sends(i)
+        if 1 <= j < DEPTH:
+            out_sums.y_stage(j - 1)
+            out_sums.line.pass_on(j - 1)
+        if j > 0:
+            for i in range(DEPTH):
+                head_sums[j - 1].core_stage(i)
+    for j in range(max(kv_heads - 1, 0), DEPTH - 1):
+        out_sums.y_stage(j)
+        out_sums.line.pass_on(j)
+    out_sums.y_stage(DEPTH - 1)
+    for i in range(DEPTH):
+        head_sums[kv_heads - 1].core_stage(i)
     finish_own(loads[1:])
 
     def project(token_rows, target):
@@ -1047,41 +1112,15 @@
 
     values = row_in[...].astype(jnp.float32)
     inv_rms = lax.rsqrt(jnp.mean(values * values, axis=-1, keepdims=True) + EPSILON)
-    gathering[0, 0:1, :] = jnp.sum(partial[...] * values * inv_rms, axis=0, keepdims=True)
-    gathering[0, 1:2, :] = t_m[...]
-    exchange = [mail.send(gathering.at[0], arriving.at[0], pairs[0])]
-
-    def pair_step():
-        step = len(exchange) - 1
-        if step == len(pairs):
-            return
-        exchange[step].wait_recv()
-        total = gathering[step] + arriving[step]
-        if step + 1 < len(pairs):
-            gathering[step + 1] = total
-            exchange.append(
-                mail.send(gathering.at[step + 1], arriving.at[step + 1], pairs[step + 1])
-            )
-        else:
-            sums[...] = total
-            exchange.append(None)
-
-    y_stage("o", 0)
-    for i in range(DEPTH):
-
-        @pl.loop(0, quarter // TILE)
-        def _(index, i=i):
-            cols = pl.ds(pl.multiple_of(order[i] * quarter + index * TILE, TILE), TILE)
-            full[cols, qkv_span] = matmul(flipped[cols, :], raw_half[...]).astype(jnp.bfloat16)
-
-        core_sends("qkv", i)
-        if i == 0:
-            pair_step()
-        else:
-            core_stage("qkv", i - 1)
-    core_stage("qkv", DEPTH - 1)
-    y_stage("o", 1)
-    pair_step()
+    gain_terms = jnp.sum(partial[...] * values * inv_rms, axis=0, keepdims=True)
+    blocks = gains.shape[0]
+    share = width // blocks
+    head_terms = gains[0, 2:4, :]
+    for index in range(blocks):
+        gains[index, 0:1, :share] = gain_terms[:, index * share : (index + 1) * share]
+        gains[index, 1:2, :share] = t_m[:, index * share : (index + 1) * share]
+        gains[index, 2:4, :] = head_terms
+    swap_gains = mail.send(gains, from_other, other)
     swap.wait_recv()
     grad_norm = partial[kept, :] + incoming[...].astype(jnp.float32)
     values = row_in[kept, :].astype(jnp.float32)
@@ -1090,25 +1129,26 @@
     o_i[kept, :] = (grad_mid[...] + grad_values).astype(jnp.bfloat16)
     swap_back = mail.send(o_i.at[kept], o_i.at[kept], other)
 
-    y_stage("o", 2)
-    y_stage("o", 3)
-    for i in range(DEPTH - 1):
-        y_stage("qkv", i)
-        if i > 0:
-            pair_step()
-    finish_line("o")
-    y_stage("qkv", DEPTH - 1)
-    while exchange[-1] is not None:
-        pair_step()
-    for k in range(DEPTH):
-        if k > 0:
-            to_z[k].wait_recv()
-        for i, out in enumerate((d_g, d_u, d_d)):
-            span = pl.ds(i * part, part)
-            share = shares[z, :, span] if k == 0 else from_spread[k - 1, :, span]
-            out[:, band(at.z_off(-k), part)] = share.astype(jnp.float32)
-    finish_line("qkv")
-    receive([swap_l, swap_back])
+    swap_gains.wait_recv()
+    totals[...] = gains[...] + from_other[...]
+    for i in range(DEPTH):
+        gain_sums.core_sends(i)
+    for i in range(DEPTH):
+        gain_sums.core_stage(i)
+    every = head_sums + [gain_sums]
+    for index in range(len(every) + DEPTH - 2):
+        if index < len(every):
+            for i in range(DEPTH):
+                every[index].y_stage(i)
+        for turn in range(DEPTH - 1):
+            if 0 <= index - turn < len(every):
+                every[index - turn].line.pass_on(turn)
+    out_sums.finish()
+    for one in every[:-1]:
+        one.finish()
+    every[-1].finish()
+    receive([swap_l, swap_back] + to_z)
+    finish_own(own_share)
     mail.finish()
 
 
@@ -1120,33 +1160,46 @@
     rows = width // dp_size
     half, full = jnp.bfloat16, jnp.float32
     every = sum(cols)
-    pairs = 4 + wide.bit_length() - 1
-    copies = 3 + 3 + 2 * LineReduce.slots + 2 * DEPTH * (2 * wide - 1) + pairs
+    kv_heads = cols[1] // gains[2].shape[1]
+    head_cols = (every - cols[3]) // kv_heads
+    passes = kv_heads + 2
+    copies = 9 + 4 + passes * (LineReduce.slots + DEPTH * (2 * wide - 1))
     shapes = [jax.ShapeDtypeStruct((seq_len, width), half)] * 2
-    shapes += [jax.ShapeDtypeStruct((8, width), full)]
+    shapes += [jax.ShapeDtypeStruct((8, 128), full)]
     shapes += [jax.ShapeDtypeStruct((rows, col), full) for col in cols]
-    shapes += [jax.ShapeDtypeStruct((rows, part * DEPTH), full)] * 3
+    shapes += [jax.ShapeDtypeStruct((rows, DEPTH * part), half)] * 3
+    lazy = [grad_mid, out_half] + [one for i, one in enumerate(saved) if i != 7]
     inputs = [grad_mid, mid_half, out_half, gain_terms, gains[0], *saved, *gains[2:]]
     return pl.pallas_call(
         functools.partial(backward_kernel, dp_size),
         out_shape=shapes,
-        in_specs=[VMEM, ANY] + [VMEM] * len(inputs),
-        out_specs=[VMEM] * 10,
-        scratch_shapes=[
+        in_specs=[ANY] * 3 + [VMEM, ANY, VMEM, VMEM] + [ANY] * 7 + [VMEM] + [ANY] * 4 + [VMEM] * 2,
+        out_specs=[VMEM] * 7 + [ANY] * 3,
+        scratch_shapes=[pltpu.VMEM(one.shape, one.dtype) for one in lazy]
+        + [
             pltpu.VMEM((width, every), half),
-            pltpu.VMEM((DEPTH, wide, rows, every), half),
-            pltpu.VMEM((wide - 1, DEPTH, rows, every), half),
-            pltpu.VMEM((LineReduce.slots, rows, every), half),
-            pltpu.VMEM((DEPTH - 1, rows, 3 * part), half),
+            pltpu.VMEM((kv_heads, width, head_cols), half),
+            pltpu.VMEM((dp_size, 8, 128), full),
+            pltpu.VMEM((dp_size, 8, 128), full),
+            pltpu.VMEM((dp_size, 8, 128), full),
+            pltpu.VMEM((DEPTH, wide, rows, cols[3]), half),
+            pltpu.VMEM((kv_heads, DEPTH, wide, rows, head_cols), half),
+            pltpu.VMEM((DEPTH, wide, 8, 128), full),
+            pltpu.VMEM((wide - 1, DEPTH, rows, cols[3]), half),
+            pltpu.VMEM((kv_heads, wide - 1, DEPTH, rows, head_cols), half),
+            pltpu.VMEM((wide - 1, DEPTH, 8, 128), full),
+            pltpu.VMEM((LineReduce.slots, rows, cols[3]), half),
+            pltpu.VMEM((kv_heads, LineReduce.slots, rows, head_cols), half),
+            pltpu.VMEM((LineReduce.slots, 8, 128), full),
+            pltpu.VMEM((rows, 3 * part), half),
             pltpu.VMEM((seq_len, cols[0]), half),
             pltpu.VMEM((seq_len, every - cols[3]), half),
+            pltpu.VMEM((seq_len, head_cols), half),
             pltpu.VMEM((width, seq_len), half),
             pltpu.VMEM((seq_len, width), full),
             pltpu.VMEM((tokens, width), half),
             pltpu.VMEM((tokens, width), half),
-            pltpu.VMEM((pairs, 8, width), full),
-            pltpu.VMEM((pairs, 8, width), full),
-            pltpu.SemaphoreType.DMA((2,)),
+            pltpu.SemaphoreType.DMA((18,)),
             pltpu.SemaphoreType.DMA((copies,)),
             pltpu.SemaphoreType.DMA((copies,)),
         ],
@@ -1192,11 +1245,13 @@
         [row_in] + list(saved), gains,
     )
     out_row, in_grad, sums = outs[:3]
-    gain_outs = []
-    for i, size in enumerate((width, width, q_gain.shape[0], k_gain.shape[0])):
-        share = size // dp_size
-        gain_outs.append(lax.dynamic_slice(sums[i], (lax.axis_index("dp") * share,), (share,)))
-    return (out_row[None], in_grad[None], *outs[3:], *gain_outs)
+    share = width // dp_size
+    gain_outs = [sums[0, :share], sums[1, :share]]
+    for i, gain in enumerate((q_gain, k_gain)):
+        share = gain.shape[0] // dp_size
+        gain_outs.append(lax.dynamic_slice(sums[2 + i], (lax.axis_index("dp") * share,), (share,)))
+    ffn_grads = [grad.astype(jnp.float32) for grad in outs[7:]]
+    return (out_row[None], in_grad[None], *outs[3:7], *ffn_grads, *gain_outs)
 
 
 def solution(mesh):

time: 455 us -> 433 us (0.952)
  Pallas kernels: 431 us -> 409 us
  local copies, waits for them, and re-layouts: 15.3 us -> 8.37 us
  other arithmetic: 0 us -> 6.3 us
    pallas_call x1, Pallas kernels: 130 us -> 111 us  [backward(): pl.pallas_call(functools.partial(backward_kernel, dp_size), out_shape=sha...]
    unnamed x25 -> x20, local copies, waits for them, and re-layouts: 11.7 us -> 4.96 us
    convert_element_type x0 -> x3, other arithmetic: none -> 6.3 us  [body(): ffn_grads = [grad.astype(jnp.float32) for grad in outs[7:]]]
where the time goes in v5:
time: 433 us; the launch traced here: 424 us
  Pallas kernels  409 us (94%)
  local copies, waits for them, and re-layouts  8.37 us (2%)
  other arithmetic  6.3 us (1%)
    pallas_call x1, Pallas kernels, forward(): pl.pallas_call(functools.partial(forward_kernel, dp_size), out_shape=shap...  180 us
    pallas_call x1, Pallas kernels, mlp(): pl.pallas_call(functools.partial(mlp_kernel, dp_size), out_shape=shapes,...  117 us
    pallas_call x1, Pallas kernels, backward(): pl.pallas_call(functools.partial(backward_kernel, dp_size), out_shape=sha...  111 us

profile of v5, /device:TPU:0, one launch (start us, length us, event | category | flops | bytes accessed | tf_op | source)
XLA Modules:
  0.0 424.3 jit_solution(7684921531207246495)
XLA Ops:
  0.6 1.5 copy.27.seg_col
  2.1 180.0 %shard_map.237 = (bf16[2048,3072]{1,0:T(8,128)(2,1)}, bf16[2048,2304]{1,0:T(8,128)(2,1)}, bf16[4,2,128,2048]{3,2,1,0:T(8,128)(2,1)}, bf16[4,2,128,2048]{3,2,1,0:...) custom-call(bf16[128,1024]{1,0:T(8,128)(2,1)} %w_q.1, ...), custom_call_target="tpu_custom_call" | custom-call | tf_op jit(solution)/shard_map/pallas_call | solution.py:569
  182.1 117.5 %shard_map.238 = (f32[128,2048]{1,0:T(8,128)}, bf16[256,2048]{1,0:T(8,128)(2,1)}, bf16[128,2048]{1,0:T(8,128)(2,1)}, f32[1,2048]{1,0:T(1,128)}, bf16[4,128,2304]{2,1,0:T(8,128)(2,1)}) custom-call(bf16[2048,2304]{1,0:T(8,128)(2,1)} %get-tuple-element.44.weights, bf16[1024,2048]{1,0:T(8,128)(2,1)} %bitcast.24, bf16[1024,2048]{1,0:T(8,128)(2,1)} %bitcast.23, ...), custom_call_target="tpu_custom_call" | custom-call | tf_op jit(solution)/shard_map/pallas_call | solution.py:837
  299.6 111.1 %shard_map.239 = (bf16[256,2048]{1,0:T(8,128)(2,1)}, bf16[256,2048]{1,0:T(8,128)(2,1)}, f32[8,128]{1,0:T(8,128)}, f32[128,1024]{1,0:T(8,128)}, f32[128,512]{1,0:...) custom-call(bf16[4,128,2304]{2,1,0:T(8,128)(2,1)} %get-tuple-element, ...), custom_call_target="tpu_custom_call" | custom-call | tf_op jit(solution)/shard_map/pallas_call | solution.py:1173
  410.7 0.0 copy-start.2
  410.7 0.0 copy-start.1
  410.7 1.3 fusion
  412.1 0.6 dynamic-slice_bitcast_fusion
  412.6 0.0 copy-start
  412.6 2.5 convert_element_type.10
  415.2 0.0 copy-start.4
  415.2 2.5 convert_element_type.11
  417.6 0.0 copy-start.6
  417.7 0.0 copy-start.5
  417.7 0.0 copy-done.2
  417.7 0.0 copy-start.3
  417.7 1.3 convert_element_type.9
  419.0 0.0 copy-done.1
  419.0 1.0 copy.34
  419.9 0.0 copy-done
  419.9 1.0 copy.35
  420.9 0.0 copy-done.4
  420.9 0.8 copy.36
  421.7 0.0 copy-done.6
  421.7 0.7 copy.37
  422.4 0.0 copy-done.5
  422.4 0.7 copy.38
  423.1 0.0 copy-done.3
  423.1 0.8 copy.39
Async XLA Ops:
  410.7 7.0 %copy-start.2 = (bf16[128,3072]{1,0:T(8,128)(2,1)S(1)}, bf16[128,3072]{1,0:T(8,128)(2,1)}, u32[]{:S(2)}) copy-start(bf16[128,3072]{1,0:T(8,128)(2,1)} %get-tuple-element.71) | copy-start | bytes 2359300
  410.7 8.3 %copy-start.1 = (bf16[256,2048]{1,0:T(8,128)(2,1)S(1)}, bf16[256,2048]{1,0:T(8,128)(2,1)}, u32[]{:S(2)}) copy-start(bf16[256,2048]{1,0:T(8,128)(2,1)} %get-tuple-element.65) | copy-start | bytes 3145732
  412.6 7.3 %copy-start = (bf16[256,2048]{1,0:T(8,128)(2,1)S(1)}, bf16[256,2048]{1,0:T(8,128)(2,1)}, u32[]{:S(2)}) copy-start(bf16[256,2048]{1,0:T(8,128)(2,1)} %get-tuple-element.66) | copy-start | bytes 3145732
  415.2 5.7 %copy-start.4 = (f32[128,1024]{1,0:T(8,128)S(1)}, f32[128,1024]{1,0:T(8,128)}, u32[]{:S(2)}) copy-start(f32[128,1024]{1,0:T(8,128)} %get-tuple-element.96) | copy-start | bytes 1572868
  417.6 4.1 copy-start.6
  417.7 4.8 %copy-start.5 = (f32[128,512]{1,0:T(8,128)S(1)}, f32[128,512]{1,0:T(8,128)}, u32[]{:S(2)}) copy-start(f32[128,512]{1,0:T(8,128)} %get-tuple-element.98) | copy-start | bytes 786436
  417.7 5.5 %copy-start.3 = (f32[128,1024]{1,0:T(8,128)S(1)}, f32[128,1024]{1,0:T(8,128)}, u32[]{:S(2)}) copy-start(f32[128,1024]{1,0:T(8,128)} %get-tuple-element.99) | copy-start | bytes 1572868

commit v6 on v5

--- a/solution.py
+++ b/solution.py
@@ -588,8 +588,8 @@
 
 def mlp_kernel(
     dp_size, weights, n_all, c_all, a_mid, a_cot, gain,
-    a_m, a_h, a_l, o_t, a_shares,
-    mid, cot, o_m, o_h, o_l, o_b, shares, full, x_n, x_c, hidden, p_n, p_o, h_n, h_o, h_l, l_n, l_o, l_z, outgoing, from_core, from_y,
+    a_m, a_h, a_p, o_t, a_shares, d_g, d_u,
+    mid, cot, o_m, o_h, shares, full, x_n, x_c, hidden, p_n, p_o, h_n, l_n, from_core, from_y,
     own_sems, send_sems, recv_sems,
 ):
     at = Place(dp_size)
@@ -621,23 +621,16 @@
         loads["n", i].start()
         loads["c", i].start()
     late = own_copies([(a_mid, mid), (a_cot, cot)], own_sems, 11)
-    meet([other, sibling] + at.line() + y_peers)
+    meet([other, sibling] + at.z_peers() + y_peers)
     mail = Mail(send_sems, recv_sems)
 
     def half_rows(index, side):
         return band(index * HALVES + side, tokens)
 
-    first, second = pl.ds(0, width // 2), pl.ds(width // 2, width // 2)
     norm_line = LineReduce(
         mail, at, 1, lambda index: [p_n.at[half_rows(index, x)]], lambda slot: [l_n.at[slot]]
     )
-    out_line = LineReduce(
-        mail, at, 1, lambda index: [p_o.at[half_rows(index, x), first]], lambda slot: [l_o.at[slot]]
-    )
-    late_line = LineReduce(
-        mail, at, 1, lambda index: [p_o.at[band(index, block_rows), second]], lambda slot: [l_z.at[slot]]
-    )
-    norm_swaps, out_swaps = [], []
+    norm_swaps = []
 
     def compute(i):
         block = band(order[i], block_rows)
@@ -678,15 +671,12 @@
             cols = band(index, TILE)
             p_o[block, cols] = dot_nt(hidden[block, down], full[cols, down]).astype(jnp.bfloat16)
 
+        stores.extend(own_copies([(p_o.at[block], a_p.at[block])], own_sems, 7 + i))
+
     def norm_step(i):
         norm_swaps[i].wait_recv()
         add_into(p_n.at[half_rows(order[i], x)], h_n.at[i])
         norm_line.pass_on(i)
-
-    def out_step(i):
-        out_swaps[i].wait_recv()
-        add_into(p_o.at[half_rows(order[i], x), first], h_o.at[i])
-        out_line.pass_on(i)
 
     def weight_grads(span, i):
         left = x_n if span is gate_up else x_c
@@ -729,6 +719,27 @@
             total = total + from_y[j - 1, order[i], :, span].astype(jnp.float32)
         shares[order[i], :, span] = total.astype(jnp.bfloat16)
 
+    spread_base = mail.reserve(2 * DEPTH)
+
+    def spread_copies(i, source, target, device):
+        return [
+            pltpu.make_async_remote_copy(
+                shares.at[target, :, pl.ds(w * part, part)],
+                out.at[:, band(source, part)],
+                mail.send_sems.at[spread_base + 2 * i + w],
+                mail.recv_sems.at[spread_base + 2 * source + w],
+                device_id=device,
+                device_id_type=MESH,
+            )
+            for w, out in enumerate((d_g, d_u))
+        ]
+
+    def spread(i):
+        copies = spread_copies(i, z, order[i], at.device(z=order[i]))
+        start_all(copies)
+        mail.open += [(copy, None) for copy in copies]
+
+    stores = []
     compute(0)
     compute(1)
     compute(2)
@@ -744,20 +755,21 @@
     weight_grads(gate_up, 3)
     core_stage(gate_up, 2)
     compute_out(0)
-    late_line.pass_on(0)
+    compute_out(1)
     core_stage(gate_up, 3)
-    compute_out(1)
-    late_line.pass_on(1)
     compute_out(2)
     compute_out(3)
-    norm_swaps[3].wait_recv()
-    for i in range(DEPTH):
-        out_swaps.append(
-            mail.send(p_o.at[half_rows(order[i], 1 - x), first], h_o.at[i], other)
-        )
     weight_grads(down, 0)
     weight_grads(down, 1)
     core_stage(down, 0)
+    weight_grads(down, 2)
+    core_stage(down, 1)
+    y_stage(gate_up, 0)
+    spread(0)
+    weight_grads(down, 3)
+    core_stage(down, 2)
+    core_stage(down, 3)
+    norm_swaps[3].wait_recv()
     finish_own(late)
     o_m[...] = p_n[half_rows(z, x), :].astype(jnp.float32) + h_n[3].astype(jnp.float32)
 
@@ -775,46 +787,27 @@
     o_m[...] = total
     o_h[kept, :] = total.astype(jnp.bfloat16)
     swap_h = mail.send(o_h.at[kept], o_h.at[kept], other)
-    stores = own_copies([(o_m, a_m)], own_sems, 0)
-    late_line.pass_on(2)
-    weight_grads(down, 2)
-    core_stage(down, 1)
-    weight_grads(down, 3)
-    core_stage(down, 2)
-    core_stage(down, 3)
-    for i in range(DEPTH - 1):
-        out_step(i)
+    stores += own_copies([(o_m, a_m)], own_sems, 0)
+    for i in range(1, DEPTH):
         y_stage(gate_up, i)
-
-    def add_late(_, landed):
-        for i in range(HALVES):
-            rows_of = band(z * HALVES + i, tokens)
-            add_into(p_o.at[rows_of, second], landed.at[pl.ds(i * tokens, tokens)])
-
-    late_line.last(add_late)
-    outgoing[...] = p_o[half_rows(z, 1 - x), second]
-    swap_l = mail.send(outgoing, h_l, other)
-    y_stage(gate_up, DEPTH - 1)
+        if i < DEPTH - 1:
+            spread(i)
+    stores += own_copies(
+        [
+            (shares.at[z, :, pl.ds(w * part, part)], out.at[:, band(z, part)])
+            for w, out in enumerate((d_g, d_u))
+        ],
+        own_sems,
+        1,
+    )
     for i in range(DEPTH):
         y_stage(down, i)
-        stores.extend(own_copies([(shares.at[order[i]], a_shares.at[order[i]])], own_sems, 3 + i))
-    out_swaps[3].wait_recv()
-    o_l[:, first] = mid[:, first] + (
-        p_o[half_rows(z, x), first].astype(jnp.float32) + h_o[3].astype(jnp.float32)
-    )
-
-    def add_out(_, landed):
-        o_l[:, first] = o_l[:, first] + landed[...].astype(jnp.float32)
-
-    out_line.last(add_out)
-    swap_l.wait_recv()
-    o_l[:, second] = mid[:, second] + (
-        p_o[half_rows(z, x), second].astype(jnp.float32) + h_l[...].astype(jnp.float32)
-    )
-    o_b[...] = o_l[...].astype(jnp.bfloat16)
-    stores += own_copies([(o_b, a_l)], own_sems, 1)
+        stores += own_copies([(shares.at[order[i], :, down], a_shares.at[order[i]])], own_sems, 3 + i)
     swap_h.wait_recv()
-    stores += own_copies([(o_h, a_h)], own_sems, 2)
+    stores += own_copies([(o_h, a_h)], own_sems, 11)
+    for k in range(1, DEPTH):
+        source = at.z_off(-k)
+        receive(spread_copies(0, source, z, at.device(z=source)))
     mail.finish()
     finish_own(stores)
 
@@ -826,26 +819,24 @@
     rows = width // dp_size
     every = DEPTH * HALVES * tokens
     half, full = jnp.bfloat16, jnp.float32
-    copies = 3 * LineReduce.slots + 2 * DEPTH + 2 * DEPTH * (2 * wide - 1) + 2
+    copies = LineReduce.slots + DEPTH + 2 * DEPTH * (2 * wide - 1) + 1 + 2 * DEPTH
     shapes = [
         jax.ShapeDtypeStruct((tokens, width), full),
         jax.ShapeDtypeStruct((HALVES * tokens, width), half),
-        jax.ShapeDtypeStruct((tokens, width), half),
+        jax.ShapeDtypeStruct((every, width), half),
         jax.ShapeDtypeStruct((1, width), full),
-        jax.ShapeDtypeStruct((DEPTH, rows, cols), half),
-    ]
+        jax.ShapeDtypeStruct((DEPTH, rows, cols // 3), half),
+    ] + [jax.ShapeDtypeStruct((rows, DEPTH * cols // 3), half)] * 2
     return pl.pallas_call(
         functools.partial(mlp_kernel, dp_size),
         out_shape=shapes,
         in_specs=[ANY] * 5 + [VMEM],
-        out_specs=[ANY] * 3 + [VMEM, ANY],
+        out_specs=[ANY] * 3 + [VMEM] + [ANY] * 3,
         scratch_shapes=[
             pltpu.VMEM((tokens, width), full),
             pltpu.VMEM((HALVES * tokens, width), half),
             pltpu.VMEM((tokens, width), full),
             pltpu.VMEM((HALVES * tokens, width), half),
-            pltpu.VMEM((tokens, width), full),
-            pltpu.VMEM((tokens, width), half),
             pltpu.VMEM((DEPTH, rows, cols), half),
         ]
         + [pltpu.VMEM((width, cols), half)]
@@ -854,12 +845,7 @@
         + [pltpu.VMEM((every, width), half)] * 2
         + [
             pltpu.VMEM((DEPTH, tokens, width), half),
-            pltpu.VMEM((DEPTH, tokens, width // 2), half),
-            pltpu.VMEM((tokens, width // 2), half),
             pltpu.VMEM((LineReduce.slots, tokens, width), half),
-            pltpu.VMEM((LineReduce.slots, tokens, width // 2), half),
-            pltpu.VMEM((LineReduce.slots, HALVES * tokens, width // 2), half),
-            pltpu.VMEM((tokens, width // 2), half),
         ]
         + [
             pltpu.VMEM((DEPTH, wide, rows, cols), half),
@@ -875,13 +861,13 @@
 
 
 def backward_kernel(
-    dp_size, shares, weights, a_mid, mid_half, a_out, t_m, gain_one, a_row, a_normed, a_query,
+    dp_size, shares, weights, a_mid, mid_half, a_out, a_part, t_m, gain_one, a_row, a_normed, a_query,
     a_key, a_values, a_queries, a_keys, context, a_log, a_cosine, a_sine, a_bias, q_gain, k_gain,
-    o_l, o_i, sums, d_q, d_k, d_v, d_o, d_g, d_u, d_d,
-    grad_mid, out_half, row_in, normed_one, query_raw, key_raw, values_half, queries, keys,
+    o_l, o_i, sums, d_q, d_k, d_v, d_o, d_d,
+    grad_mid, layer_mid, row_in, normed_one, query_raw, key_raw, values_half, queries, keys,
     log_total, cosine, sine, bias,
     full, head_grads, gains, from_other, totals, core_o, core_h, core_s, y_o, y_h, y_s, z_o, z_h, z_s,
-    spare, context_grad, raw_half, raw_head, flipped, partial,
+    part_own, part_other, part_line, spare, context_grad, raw_half, raw_head, flipped, partial,
     outgoing, incoming, own_sems, send_sems, recv_sems,
 ):
     at = Place(dp_size)
@@ -891,7 +877,7 @@
     order = at.order()
     tokens, width = grad_mid.shape
     rows = d_q.shape[0]
-    part = shares.shape[2] // 3
+    part = shares.shape[2]
     spans, start = [], 0
     for out in (d_q, d_k, d_v, d_o):
         spans.append(pl.ds(start, out.shape[1]))
@@ -912,20 +898,36 @@
         [
             (a_normed, normed_one), (a_query, query_raw), (a_key, key_raw), (a_values, values_half),
             (a_queries, queries), (a_keys, keys), (a_log, log_total), (a_cosine, cosine),
-            (a_sine, sine), (a_bias, bias), (a_out, out_half), (a_mid, grad_mid), (a_row, row_in),
+            (a_sine, sine), (a_bias, bias), (a_out, layer_mid), (a_mid, grad_mid), (a_row, row_in),
         ],
         own_sems,
         2,
     )
+    part_loads = own_copies(
+        [(a_part.at[band(index * HALVES + x, tokens)], part_own.at[index]) for index in order],
+        own_sems,
+        16,
+    )
     meet([other, sibling] + y_peers + z_peers)
     mail = Mail(send_sems, recv_sems)
-    ffn = [(out, pl.ds(i * part, part)) for i, out in enumerate((d_g, d_u, d_d))]
+    part_swaps = [
+        mail.send(a_part.at[band(index * HALVES + 1 - x, tokens)], part_other.at[i], other)
+        for i, index in enumerate(order)
+    ]
+    part_sums = LineReduce(
+        mail, at, 1, lambda index: [part_own.at[index]], lambda slot: [part_line.at[slot]]
+    )
+
+    def part_step(i):
+        part_swaps[i].wait_recv()
+        part_loads[i].wait()
+        add_into(part_own.at[order[i]], part_other.at[i])
+        if i < DEPTH - 1:
+            part_sums.pass_on(i)
+
     to_z = [
-        mail.send(
-            shares.at[at.z_off(k), :, span], out.at[:, band(z, part)], z_peers[k - 1]
-        )
+        mail.send(shares.at[at.z_off(k)], d_d.at[:, band(z, part)], z_peers[k - 1])
         for k in (2, 1, 3)
-        for out, span in ffn
     ]
     kv_heads = key_raw.shape[1] // head_dim
     group = query_raw.shape[1] // key_raw.shape[1]
@@ -1024,12 +1026,8 @@
         out_sums.core_stage(i)
     finish_own(late)
     finish_own(own_share)
-    own_share = own_copies(
-        [(spare.at[:, span], out.at[:, band(z, part)]) for out, span in ffn], own_sems, 15
-    )
+    own_share = own_copies([(spare, d_d.at[:, band(z, part)])], own_sems, 15)
     flipped[...] = normed_one[...].T
-    o_l[kept, :] = out_half[...]
-    swap_l = mail.send(o_l.at[kept], o_l.at[kept], other)
 
     scale = 1.0 / math.sqrt(head_dim)
 
@@ -1086,6 +1084,10 @@
         if 1 <= j < DEPTH:
             out_sums.y_stage(j - 1)
             out_sums.line.pass_on(j - 1)
+        if j == 0:
+            part_step(0)
+        if j == DEPTH - 2:
+            part_step(1)
         if j > 0:
             for i in range(DEPTH):
                 head_sums[j - 1].core_stage(i)
@@ -1129,6 +1131,9 @@
     o_i[kept, :] = (grad_mid[...] + grad_values).astype(jnp.bfloat16)
     swap_back = mail.send(o_i.at[kept], o_i.at[kept], other)
 
+    if kv_heads < DEPTH - 1:
+        part_step(1)
+    part_step(2)
     swap_gains.wait_recv()
     totals[...] = gains[...] + from_other[...]
     for i in range(DEPTH):
@@ -1136,6 +1141,7 @@
     for i in range(DEPTH):
         gain_sums.core_stage(i)
     every = head_sums + [gain_sums]
+    part_step(3)
     for index in range(len(every) + DEPTH - 2):
         if index < len(every):
             for i in range(DEPTH):
@@ -1144,6 +1150,14 @@
             if 0 <= index - turn < len(every):
                 every[index - turn].line.pass_on(turn)
     out_sums.finish()
+    layer_mid[...] = layer_mid[...] + part_own[z].astype(jnp.float32)
+
+    def add_part(_, landed):
+        layer_mid[...] = layer_mid[...] + landed[...].astype(jnp.float32)
+
+    part_sums.last(add_part)
+    o_l[kept, :] = layer_mid[...].astype(jnp.bfloat16)
+    swap_l = mail.send(o_l.at[kept], o_l.at[kept], other)
     for one in every[:-1]:
         one.finish()
     every[-1].finish()
@@ -1152,29 +1166,29 @@
     mail.finish()
 
 
-def backward(dp_size, shares, weights, cols, grad_mid, mid_half, out_half, gain_terms, saved, gains):
+def backward(dp_size, shares, weights, cols, grad_mid, mid_half, layer_mid, part_out, gain_terms, saved, gains):
     wide = dp_size // (DEPTH * CORES)
     tokens, width = grad_mid.shape
     seq_len = HALVES * tokens
-    part = shares.shape[2] // 3
+    part = shares.shape[2]
     rows = width // dp_size
     half, full = jnp.bfloat16, jnp.float32
     every = sum(cols)
     kv_heads = cols[1] // gains[2].shape[1]
     head_cols = (every - cols[3]) // kv_heads
     passes = kv_heads + 2
-    copies = 9 + 4 + passes * (LineReduce.slots + DEPTH * (2 * wide - 1))
+    copies = 3 + 4 + DEPTH + LineReduce.slots + passes * (LineReduce.slots + DEPTH * (2 * wide - 1))
     shapes = [jax.ShapeDtypeStruct((seq_len, width), half)] * 2
     shapes += [jax.ShapeDtypeStruct((8, 128), full)]
     shapes += [jax.ShapeDtypeStruct((rows, col), full) for col in cols]
-    shapes += [jax.ShapeDtypeStruct((rows, DEPTH * part), half)] * 3
-    lazy = [grad_mid, out_half] + [one for i, one in enumerate(saved) if i != 7]
-    inputs = [grad_mid, mid_half, out_half, gain_terms, gains[0], *saved, *gains[2:]]
+    shapes += [jax.ShapeDtypeStruct((rows, DEPTH * part), half)]
+    lazy = [grad_mid, layer_mid] + [one for i, one in enumerate(saved) if i != 7]
+    inputs = [grad_mid, mid_half, layer_mid, part_out, gain_terms, gains[0], *saved, *gains[2:]]
     return pl.pallas_call(
         functools.partial(backward_kernel, dp_size),
         out_shape=shapes,
-        in_specs=[ANY] * 3 + [VMEM, ANY, VMEM, VMEM] + [ANY] * 7 + [VMEM] + [ANY] * 4 + [VMEM] * 2,
-        out_specs=[VMEM] * 7 + [ANY] * 3,
+        in_specs=[ANY] * 3 + [VMEM, ANY, ANY, VMEM, VMEM] + [ANY] * 7 + [VMEM] + [ANY] * 4 + [VMEM] * 2,
+        out_specs=[VMEM] * 7 + [ANY],
         scratch_shapes=[pltpu.VMEM(one.shape, one.dtype) for one in lazy]
         + [
             pltpu.VMEM((width, every), half),
@@ -1191,7 +1205,10 @@
             pltpu.VMEM((LineReduce.slots, rows, cols[3]), half),
             pltpu.VMEM((kv_heads, LineReduce.slots, rows, head_cols), half),
             pltpu.VMEM((LineReduce.slots, 8, 128), full),
-            pltpu.VMEM((rows, 3 * part), half),
+            pltpu.VMEM((DEPTH, tokens, width), half),
+            pltpu.VMEM((DEPTH, tokens, width), half),
+            pltpu.VMEM((LineReduce.slots, tokens, width), half),
+            pltpu.VMEM((rows, part), half),
             pltpu.VMEM((seq_len, cols[0]), half),
             pltpu.VMEM((seq_len, every - cols[3]), half),
             pltpu.VMEM((seq_len, head_cols), half),
@@ -1199,7 +1216,7 @@
             pltpu.VMEM((seq_len, width), full),
             pltpu.VMEM((tokens, width), half),
             pltpu.VMEM((tokens, width), half),
-            pltpu.SemaphoreType.DMA((18,)),
+            pltpu.SemaphoreType.DMA((20,)),
             pltpu.SemaphoreType.DMA((copies,)),
             pltpu.SemaphoreType.DMA((copies,)),
         ],
@@ -1238,10 +1255,10 @@
     outs = mlp(
         dp_size, ffn_full, normed.reshape(-1, width), cots.reshape(-1, width), mid, row_cot, gains[1]
     )
-    grad_mid, mid_half, out_half, gain_terms, shares = outs
+    grad_mid, mid_half, part_out, gain_terms, shares, *gate_up_grads = outs
     cols = [weight.shape[1] for weight in (w_q, w_k, w_v, w_o)]
     outs = backward(
-        dp_size, shares, attn_full, cols, grad_mid, mid_half, out_half, gain_terms,
+        dp_size, shares, attn_full, cols, grad_mid, mid_half, mid, part_out, gain_terms,
         [row_in] + list(saved), gains,
     )
     out_row, in_grad, sums = outs[:3]
@@ -1250,7 +1267,7 @@
     for i, gain in enumerate((q_gain, k_gain)):
         share = gain.shape[0] // dp_size
         gain_outs.append(lax.dynamic_slice(sums[2 + i], (lax.axis_index("dp") * share,), (share,)))
-    ffn_grads = [grad.astype(jnp.float32) for grad in outs[7:]]
+    ffn_grads = [grad.astype(jnp.float32) for grad in (*gate_up_grads, outs[7])]
     return (out_row[None], in_grad[None], *outs[3:7], *ffn_grads, *gain_outs)
 
 

time: 433 us -> 425 us (0.982)
  the two profiles are of different devices: /device:TPU:0 before, /device:TPU:20 now
where the time goes in v6:
time: 425 us; the launch traced here: 417 us
  Pallas kernels  402 us (95%)
  local copies, waits for them, and re-layouts  8.37 us (2%)
  other arithmetic  5.11 us (1%)
    pallas_call x1, Pallas kernels, forward(): pl.pallas_call(functools.partial(forward_kernel, dp_size), out_shape=shap...  172 us
    pallas_call x1, Pallas kernels, backward(): pl.pallas_call(functools.partial(backward_kernel, dp_size), out_shape=sha...  121 us
    pallas_call x1, Pallas kernels, mlp(): pl.pallas_call(functools.partial(mlp_kernel, dp_size), out_shape=shapes,...  109 us

profile of v6, /device:TPU:20, one launch (start us, length us, event | category | flops | bytes accessed | tf_op | source)
XLA Modules:
  0.0 417.1 jit_solution(6587345281981459132)
XLA Ops:
  0.6 1.5 copy.27.seg_col
  2.1 172.0 %shard_map.237 = (bf16[2048,3072]{1,0:T(8,128)(2,1)}, bf16[2048,2304]{1,0:T(8,128)(2,1)}, bf16[4,2,128,2048]{3,2,1,0:T(8,128)(2,1)}, bf16[4,2,128,2048]{3,2,1,0:...) custom-call(bf16[128,1024]{1,0:T(8,128)(2,1)} %w_q.1, ...), custom_call_target="tpu_custom_call" | custom-call | tf_op jit(solution)/shard_map/pallas_call | solution.py:569
  174.1 109.5 %shard_map.238 = (f32[128,2048]{1,0:T(8,128)}, bf16[256,2048]{1,0:T(8,128)(2,1)}, bf16[1024,2048]{1,0:T(8,128)(2,1)}, f32[1,2048]{1,0:T(1,128)}, bf16[4,128,768]...) custom-call(bf16[2048,2304]{1,0:T(8,128)(2,1)} %get-tuple-element.44.weights, ...), custom_call_target="tpu_custom_call" | custom-call | tf_op jit(solution)/shard_map/pallas_call | solution.py:830
  283.5 0.0 copy-start.3
  283.6 121.0 %shard_map.239 = (bf16[256,2048]{1,0:T(8,128)(2,1)}, bf16[256,2048]{1,0:T(8,128)(2,1)}, f32[8,128]{1,0:T(8,128)}, f32[128,1024]{1,0:T(8,128)}, f32[128,512]{1,0:...) custom-call(bf16[4,128,768]{2,1,0:T(8,128)(2,1)} %get-tuple-element.48.shares, ...), custom_call_target="tpu_custom_call" | custom-call | tf_op jit(solution)/shard_map/pallas_call | solution.py:1187
  404.6 0.0 copy-start.2
  404.6 0.0 copy-start.1
  404.6 1.3 fusion
  406.0 0.6 dynamic-slice_bitcast_fusion
  406.6 0.0 copy-start
  406.6 2.5 convert_element_type.11
  409.1 0.0 copy-done.3
  409.1 0.0 copy-start.5
  409.1 1.3 convert_element_type.10
  410.4 0.0 copy-start.7
  410.4 0.0 copy-start.6
  410.4 0.0 copy-done.2
  410.4 0.0 copy-start.4
  410.4 1.3 convert_element_type.9
  411.7 0.0 copy-done.1
  411.7 1.0 copy.34
  412.7 0.0 copy-done
  412.7 1.0 copy.35
  413.6 0.0 copy-done.5
  413.6 0.8 copy.36
  414.4 0.0 copy-done.7
  414.4 0.7 copy.37
  415.1 0.0 copy-done.6
  415.1 0.7 copy.38
  415.9 0.0 copy-done.4
  415.9 0.8 copy.39
Async XLA Ops:
  283.5 125.5 %copy-start.3 = (bf16[128,3072]{1,0:T(8,128)(2,1)S(1)}, bf16[128,3072]{1,0:T(8,128)(2,1)}, u32[]{:S(2)}) copy-start(bf16[128,3072]{1,0:T(8,128)(2,1)} %get-tuple-element.72) | copy-start | bytes 2359300
  404.6 5.8 %copy-start.2 = (bf16[128,3072]{1,0:T(8,128)(2,1)S(1)}, bf16[128,3072]{1,0:T(8,128)(2,1)}, u32[]{:S(2)}) copy-start(bf16[128,3072]{1,0:T(8,128)(2,1)} %get-tuple-element.71) | copy-start | bytes 2359300
  404.6 7.1 %copy-start.1 = (bf16[256,2048]{1,0:T(8,128)(2,1)S(1)}, bf16[256,2048]{1,0:T(8,128)(2,1)}, u32[]{:S(2)}) copy-start(bf16[256,2048]{1,0:T(8,128)(2,1)} %get-tuple-element.65) | copy-start | bytes 3145732
  406.6 6.1 %copy-start = (bf16[256,2048]{1,0:T(8,128)(2,1)S(1)}, bf16[256,2048]{1,0:T(8,128)(2,1)}, u32[]{:S(2)}) copy-start(bf16[256,2048]{1,0:T(8,128)(2,1)} %get-tuple-element.66) | copy-start | bytes 3145732
  409.1 4.6 %copy-start.5 = (f32[128,1024]{1,0:T(8,128)S(1)}, f32[128,1024]{1,0:T(8,128)}, u32[]{:S(2)}) copy-start(f32[128,1024]{1,0:T(8,128)} %get-tuple-element.96) | copy-start | bytes 1572868
  410.4 4.1 copy-start.7
  410.4 4.8 %copy-start.6 = (f32[128,512]{1,0:T(8,128)S(1)}, f32[128,512]{1,0:T(8,128)}, u32[]{:S(2)}) copy-start(f32[128,512]{1,0:T(8,128)} %get-tuple-element.98) | copy-start | bytes 786436
  410.4 5.5 %copy-start.4 = (f32[128,1024]{1,0:T(8,128)S(1)}, f32[128,1024]{1,0:T(8,128)}, u32[]{:S(2)}) copy-start(f32[128,1024]{1,0:T(8,128)} %get-tuple-element.99) | copy-start | bytes 1572868
